TPU v7x, 128 devices: a whole 4x4x4 slice. The times are simulated.
128 devices in a mesh: group: 2 (over core), dev: 64 (over y, z, x).
Axes of the slice: x: 4, y: 4, z: 4, core: 2. Of those that a mesh axis runs over, the one named last changes fastest.
Arguments:
- points: float32 [2048, 3, 256], P(('group', 'dev')), may hold values from -6 to 6
- charges: float32 [2048, 32, 256], P(('group', 'dev')), may hold values from -1.5 to 1.5
- basis: float32 [2048, 64, 256], P(('group', 'dev')), may hold values from -0.375 to 0.375
- leaf_transfer: float32 [2048, 64, 64], P(('group', 'dev')), may hold values from -0.1875 to 0.1875
- dev_skeleton: float32 [128, 3, 64], P(('group', 'dev')), may hold values from -6 to 6
- dev_transfer: float32 [128, 64, 64], P(('group', 'dev')), may hold values from -0.25 to 0.25
- group_skeleton: float32 [2, 3, 64], replicated, may hold values from -6 to 6
- neighbours: int32 [2048, 12], P(('group', 'dev')), may hold values from 0 to 2047, as said below
- counts: int32 [2048], P(('group', 'dev')), may hold values from 1 to 12, as said below
- far_list: int32 [128, 16], P(('group', 'dev')), may hold values from 0 to 127, as said below
Outputs:
- kernel_product: float32 [2048, 32, 256], P(('group', 'dev'))
- slope_product: float32 [2048, 32, 256], P(('group', 'dev'))
Inputs may be any that keep to these rules, and one draw needn't show every extreme that they name: `neighbours`: row l starts with l itself; its other entries lie within 14 leaves of l and may repeat. `counts`: some leaf uses all 12 slots and some only one. `far_list`: entries of a row are distinct and never the row's own node.
All inputs are finite; a program needn't handle non-finite values.
Results may differ from a plain program's by a relative error of at most 0.0003.
Values sent between devices are 32-bit elements; how exact they have to be, the bound alone decides.
No kernel may reach another device: no remote copies, remote signals or barrier semaphores. Data moves between devices by JAX's collectives and lax.ppermute only.
A program may use at most 64 MiB of HBM per device.

v0:
```python
import math

import jax
import jax.numpy as jnp
from jax import lax
from jax.sharding import PartitionSpec as P

REACH = 14


SQRT_THREE = math.sqrt(3.0)
LENGTH_SCALE = 0.8
NUGGET = 0.01
HIGH = lax.Precision.HIGHEST


def partner(value, axis, distance):
    return lax.ppermute(value, axis, [(i, i ^ 1 << distance) for i in range(lax.axis_size(axis))])


def extended_2(value, sides, width):
    for axis, dim in sides:
        size, length = (lax.axis_size(axis), value.shape[dim])
        up = [(i, (i + 1) % size) for i in range(size - 1)]
        down = [(j, i) for i, j in up]
        last = lax.slice_in_dim(value, length - width, length, axis=dim)
        first = lax.slice_in_dim(value, 0, width, axis=dim)
        before = lax.ppermute(last, axis, up)
        after = lax.ppermute(first, axis, down)
        value = jnp.concatenate([before, value, after], axis=dim)
    return value


def matern_pair(target, source):
    squared = jnp.float32(0.0)
    for coord in range(3):
        differ = target[..., coord, :, None] - source[..., coord, None, :]
        squared = squared + differ * differ
    scaled = SQRT_THREE / LENGTH_SCALE * jnp.sqrt(squared + NUGGET)
    decay = jnp.exp(-scaled)
    return ((1.0 + scaled) * decay, scaled * scaled * decay / LENGTH_SCALE)


def local(
    points,
    charges,
    basis,
    leaf_transfer,
    dev_skeleton,
    dev_transfer,
    group_skeleton,
    neighbours,
    counts,
    far_list,
):
    leaves = points.shape[0]
    slots = neighbours.shape[1]
    device_rank = lax.axis_index(("group", "dev"))
    group_rank = lax.axis_index("group")
    coef_leaf = jnp.einsum("lvp,lap->lva", charges, basis, precision=HIGH)
    coef_dev = jnp.einsum("lab,lvb->va", leaf_transfer, coef_leaf, precision=HIGH)[None]
    image = jnp.einsum("ab,vb->va", dev_transfer[0], coef_dev[0], precision=HIGH)
    all_coef, all_skeleton = (
        lax.all_gather(coef_dev, ("group", "dev"), axis=0, tiled=True),
        lax.all_gather(dev_skeleton, ("group", "dev"), axis=0, tiled=True),
    )
    own_group = lax.psum(image, "dev")
    other = partner(own_group, "group", 0)
    listed = far_list[0]
    remote = all_coef[listed]
    node_value, node_slope = matern_pair(dev_skeleton, all_skeleton[listed])
    far_value = jnp.einsum("sab,svb->va", node_value, remote, precision=HIGH)
    far_slope = jnp.einsum("sab,svb->va", node_slope, remote, precision=HIGH)
    own_skeleton = lax.dynamic_index_in_dim(group_skeleton, group_rank, 0, keepdims=False)
    other_skeleton = lax.dynamic_index_in_dim(group_skeleton, 1 - group_rank, 0, keepdims=False)
    group_value, group_slope = matern_pair(own_skeleton, other_skeleton)
    top_value = jnp.einsum("ab,vb->va", group_value, other, precision=HIGH)
    top_slope = jnp.einsum("ab,vb->va", group_slope, other, precision=HIGH)
    local_dev = jnp.stack([far_value, far_slope]) + jnp.einsum(
        "ab,kva->kvb", dev_transfer[0], jnp.stack([top_value, top_slope]), precision=HIGH
    )
    local_leaf = jnp.einsum("lab,kva->klvb", leaf_transfer, local_dev, precision=HIGH)
    far_part = jnp.einsum("klva,lap->klvp", local_leaf, basis, precision=HIGH)
    stacked = jnp.concatenate([points, charges], axis=1)
    extended = extended_2(stacked, ((("group", "dev"), 0),), REACH)
    local_ids = neighbours - (device_rank * leaves - REACH)

    def leaf_near(item):
        target, chosen, count = item
        sources = extended[chosen]
        tile_value, tile_slope = matern_pair(target[None], sources[:, :3])
        live = (jnp.arange(slots) < count).astype(jnp.float32)[:, None, None]
        vectors = sources[:, 3:]
        return jnp.stack(
            [
                jnp.einsum("jpq,jvq->vp", tile_value * live, vectors, precision=HIGH),
                jnp.einsum("jpq,jvq->vp", tile_slope * live, vectors, precision=HIGH),
            ]
        )

    block_leaves = min(leaves, 8)
    near_part = jnp.moveaxis(
        lax.map(leaf_near, (points, local_ids, counts), batch_size=block_leaves), 1, 0
    )
    result = near_part + far_part
    return (result[0], result[1])


def solution(mesh):
    placed = (
        P(("group", "dev"), None, None),
        P(("group", "dev"), None, None),
        P(("group", "dev"), None, None),
        P(("group", "dev"), None, None),
        P(("group", "dev"), None, None),
        P(("group", "dev"), None, None),
        P(),
        P(("group", "dev"), None),
        P(("group", "dev")),
        P(("group", "dev"), None),
    )
    return jax.shard_map(
        local,
        mesh=mesh,
        in_specs=placed,
        out_specs=(P(("group", "dev"), None, None), P(("group", "dev"), None, None)),
        check_vma=False,
    )
```

profile of v0, /device:TPU:1, one launch (start us, length us, event | category | flops | bytes accessed | tf_op | source)
XLA Modules:
  0.0 916.9 jit_solution(15999637364941915086)
XLA Ops:
  7.3 1.2 copy-done
  8.5 2.0 fusion.127
  10.5 2.2 convolution_bitcast_fusion.5
  12.7 0.9 fusion.79
  13.7 295.5 %psum.7 = f32[32,64]{1,0:T(8,128)S(1)} all-reduce(f32[32,64]{1,0:T(8,128)S(1)} %fusion.79), channel_id=1, replica_groups=mesh['group'=2,'dev'=64] {'dev'}, use_global_device_ids=true, to_apply=%region_2.3 | all-reduce | flops 2048 | bytes 16384 | tf_op jit(solution)/shard_map/psum | solution.py:67
  309.2 56.1 %collective-permute-start.2 = (f32[32,64]{1,0:T(8,128)S(1)}, f32[32,64]{1,0:T(8,128)S(1)}, u32[]{:S(2)}, u32[]{:S(2)}) collective-permute-start(f32[32,64]{1,0:T(8,128)S(1)} %psum.7), channel_id=1, source_target_pairs={{0,64},{64,0},{1,65},{65,1},{2,66},{66,2},{3,67},{67,3},{4,68},{68... | collective-permute-start | bytes 24584 | tf_op jit(solution)/shard_map/ppermute | solution.py:18
  365.3 0.8 copy.30
  366.2 1.3 fusion.50
  367.4 1.9 collective-permute-start
  369.4 9.1 collective-permute-start.1
  378.5 336.6 %all_gather.7 = f32[128,3,64]{2,1,0:T(4,128)} all-gather(f32[1,3,64]{2,1,0:T(4,128)S(1)} %copy.33), channel_id=1, replica_groups=mesh['group'=2,'dev'=64] {'group','dev'}, dimensions={0}, use_global_device_ids=true | all-gather | bytes 99072 | tf_op jit(solution)/shard_map/all_gather | solution.py:65
  715.1 1.5 gather_fusion.2
  718.0 0.9 convolution_bitcast_fusion.1
  718.9 0.9 convolution_bitcast_fusion.2
  719.8 0.8 copy-done.5
  720.6 1.4 pad_maximum_fusion
  722.1 179.4 %while.10 = (s32[]{:T(128)}, f32[2,8,2,32,256]{4,3,2,1,0:T(8,128)}, s32[2,8,12]{2,1,0:T(8,128)S(1)}, f32[44,35,256]{2,1,0:T(8,128)S(1)}, f32[2,8,3,256]{3,1,0,2:T(8,128)S(1)}, /*index=5*/s32[2,8]{1,0:T(2,128)S(1)}, s32[]{:T(128)}) while((s32[]{:T(128)}, f32[2,8,2,32,256]{4,3,2,1,0:T(8,128)}, s32[2,8,12]{2,1,0:T(8,128)S(1)}, ...), condition=%wide.region_1.2_spmd, body=%wide.region_0.0_spmd.sunk | while | flops 5008132096 | bytes 30535796 | solution.py:103
  722.2 2.7 gather_fusion
  724.9 2.4 fusion.155
  727.5 42.3 %fusion.158 = f32[1,8,32,256]{3,2,1,0:T(8,128)S(1)} fusion(f32[8,12]{1,0:T(8,128)S(1)} %fusion.157, f32[8,12,256]{2,1,0:T(8,128)S(1)} %get-tuple-element.130, f32[8,256]{1,0:T(8,128)S(1)} %get-tuple-element.131, f32[8,12,256]{2,1,0:T(8,128)S(1)} %get-tuple-element.132, f32[8,256]{1,0:T(8,128)S(1)} %get-tuple-element.133, ...), kind=kOutput, calls=%fused_computation.34.clone.1 | convolution fusion | flops 2503999488 | bytes 3727744 | tf_op jit(solution)/shard_map/while/body/eval_jaxpr/vmap(jpq,jvq->vp)/dot_general | solution.py:96
  769.9 41.0 %fusion.156 = f32[1,8,32,256]{3,2,1,0:T(8,128)S(1)} fusion(f32[8,12]{1,0:T(8,128)S(1)} %fusion.154, f32[8,12,256]{2,1,0:T(8,128)S(1)} %get-tuple-element.130, f32[8,256]{1,0:T(8,128)S(1)} %get-tuple-element.131, f32[8,12,256]{2,1,0:T(8,128)S(1)} %get-tuple-element.132, f32[8,256]{1,0:T(8,128)S(1)} %get-tuple-element.133, ...), kind=kOutput, calls=%fused_computation.35.clone.1 | convolution fusion | flops 2503999488 | bytes 3829760 | tf_op jit(solution)/shard_map/while/body/eval_jaxpr/vmap(jpq,jvq->vp)/dot_general | solution.py:97
  811.0 0.9 copy_dynamic-update-slice_fusion.2
  811.9 2.7 gather_fusion
  814.6 2.4 fusion.155
  817.2 42.3 %fusion.158 = f32[1,8,32,256]{3,2,1,0:T(8,128)S(1)} fusion(f32[8,12]{1,0:T(8,128)S(1)} %fusion.157, f32[8,12,256]{2,1,0:T(8,128)S(1)} %get-tuple-element.130, f32[8,256]{1,0:T(8,128)S(1)} %get-tuple-element.131, f32[8,12,256]{2,1,0:T(8,128)S(1)} %get-tuple-element.132, f32[8,256]{1,0:T(8,128)S(1)} %get-tuple-element.133, ...), kind=kOutput, calls=%fused_computation.34.clone.1 | convolution fusion | flops 2503999488 | bytes 3727744 | tf_op jit(solution)/shard_map/while/body/eval_jaxpr/vmap(jpq,jvq->vp)/dot_general | solution.py:96
  859.6 41.0 %fusion.156 = f32[1,8,32,256]{3,2,1,0:T(8,128)S(1)} fusion(f32[8,12]{1,0:T(8,128)S(1)} %fusion.154, f32[8,12,256]{2,1,0:T(8,128)S(1)} %get-tuple-element.130, f32[8,256]{1,0:T(8,128)S(1)} %get-tuple-element.131, f32[8,12,256]{2,1,0:T(8,128)S(1)} %get-tuple-element.132, f32[8,256]{1,0:T(8,128)S(1)} %get-tuple-element.133, ...), kind=kOutput, calls=%fused_computation.35.clone.1 | convolution fusion | flops 2503999488 | bytes 3829760 | tf_op jit(solution)/shard_map/while/body/eval_jaxpr/vmap(jpq,jvq->vp)/dot_general | solution.py:97
  900.6 0.8 copy_dynamic-update-slice_fusion.2
  901.5 2.3 gather_fusion.1
  903.9 1.0 convolution_bitcast_fusion.4
  905.0 1.0 convolution_bitcast_fusion.3
  906.8 2.2 fusion.126
  909.0 1.0 slice_bitcast_fusion.3
  (79 shorter events, 2.8 us)
Async XLA Ops:
  7.2 1.3 copy-start
  7.2 713.4 %copy-start.2 = (f32[16,32,256]{2,1,0:T(8,128)S(1)}, f32[16,32,256]{2,1,0:T(8,128)}, u32[]{:S(2)}) copy-start(f32[16,32,256]{2,1,0:T(8,128)} %param.13) | copy-start | bytes 1572868
  7.2 371.3 %copy-start.19 = (s32[1,16]{1,0:T(1,128)S(1)}, s32[1,16]{1,0:T(1,128)}, u32[]{:S(2)}) copy-start(s32[1,16]{1,0:T(1,128)} %param.21) | copy-start | bytes 196
  7.2 371.3 %copy-start.14 = (f32[1,3,64]{2,0,1:T(1,128)S(1)}, f32[1,3,64]{2,0,1:T(1,128)}, u32[]{:S(2)}) copy-start(f32[1,3,64]{2,0,1:T(1,128)} %param.16) | copy-start | bytes 2308
  7.2 710.1 %copy-start.9 = (s32[16,12]{1,0:T(8,128)S(1)}, s32[16,12]{1,0:T(8,128)}, u32[]{:S(2)}) copy-start(s32[16,12]{1,0:T(8,128)} %param.19) | copy-start | bytes 2308
  7.2 710.7 %copy-start.15 = (f32[2,3,64]{2,0,1:T(2,128)S(1)}, f32[2,3,64]{2,0,1:T(2,128)}, u32[]{:S(2)}) copy-start(f32[2,3,64]{2,0,1:T(2,128)} %param.18) | copy-start | bytes 4612
  7.2 710.7 %copy-start.20 = (s32[16]{0:T(128)S(1)}, s32[16]{0:T(128)}, u32[]{:S(2)}) copy-start(s32[16]{0:T(128)} %param.20) | copy-start | bytes 196
  7.2 894.3 %all-gather.3.cloned.1.call-start = ((), (), s32[]{:S(2)}) async-start(), calls=%async_computation | async-start | bytes 2113536 | tf_op jit(solution)/shard_map/all_gather | solution.py:64
  10.5 711.5 %copy-start.4 = (f32[16,3,256]{2,0,1:T(8,128)S(1)}, f32[16,3,256]{2,0,1:T(8,128)}, u32[]{:S(2)}) copy-start(f32[16,3,256]{2,0,1:T(8,128)} %param.12) | copy-start | bytes 147460
  309.2 408.8 %collective-permute-start.2 = (f32[32,64]{1,0:T(8,128)S(1)}, f32[32,64]{1,0:T(8,128)S(1)}, u32[]{:S(2)}, u32[]{:S(2)}) collective-permute-start(f32[32,64]{1,0:T(8,128)S(1)} %psum.7), channel_id=1, source_target_pairs={{0,64},{64,0},{1,65},{65,1},{2,66},{66,2},{3,67},{67,3},{4,68},{68... | collective-permute-start | bytes 24584 | tf_op jit(solution)/shard_map/ppermute | solution.py:18
  367.4 352.3 %collective-permute-start = (f32[14,35,256]{2,1,0:T(8,128)S(1)}, f32[14,35,256]{2,1,0:T(8,128)S(1)}, u32[]{:S(2)}, u32[]{:S(2)}) collective-permute-start(f32[14,35,256]{2,1,0:T(8,128)S(1)} %get-tuple-element.69), channel_id=1, source_target_pairs={{0,1},{1,2},{2,3},{3,4},{4,5},{5,6},{6,7},{7,8},{8,9},{9,10},{10,1... | collective-permute-start | bytes 1505288 | tf_op jit(solution)/shard_map/ppermute | solution.py:28
  369.4 351.2 %collective-permute-start.1 = (f32[14,35,256]{2,1,0:T(8,128)S(1)}, f32[14,35,256]{2,1,0:T(8,128)}, u32[]{:S(2)}, u32[]{:S(2)}) collective-permute-start(f32[14,35,256]{2,1,0:T(8,128)S(1)} %get-tuple-element.70), channel_id=1, source_target_pairs={{1,0},{2,1},{3,2},{4,3},{5,4},{6,5},{7,6},{8,7},{9,8},{10,9},{11,1... | collective-permute-start | bytes 1505288 | tf_op jit(solution)/shard_map/ppermute | solution.py:29
  378.5 338.8 %copy-start.13 = (s32[1024]{0:T(1024)}, s32[1024]{0:T(1024)S(1)}, u32[]{:S(2)}) copy-start(s32[1024]{0:T(1024)S(1)} %pad_clamp_fusion.1) | copy-start | bytes 12292
  719.8 0.8 copy-start.5
  722.0 181.8 %copy-start.10 = (f32[16,1,64]{2,1,0:T(1,128)S(1)}, f32[16,1,64]{2,1,0:T(1,128)}, u32[]{:S(2)}) copy-start(f32[16,1,64]{2,1,0:T(1,128)} %get-tuple-element.71) | copy-start | bytes 12292
  722.0 181.8 %copy-start.11 = (f32[16,1,64]{2,1,0:T(1,128)S(1)}, f32[16,1,64]{2,1,0:T(1,128)}, u32[]{:S(2)}) copy-start(f32[16,1,64]{2,1,0:T(1,128)} %get-tuple-element.72) | copy-start | bytes 12292
  722.1 181.8 %copy-start.12 = (f32[16,1,64]{2,1,0:T(1,128)S(1)}, f32[16,1,64]{2,1,0:T(1,128)}, u32[]{:S(2)}) copy-start(f32[16,1,64]{2,1,0:T(1,128)} %get-tuple-element.73) | copy-start | bytes 12292
  722.1 181.8 %copy-start.16 = (f32[64]{0:T(128)S(1)}, f32[64]{0:T(128)}, u32[]{:S(2)}) copy-start(f32[64]{0:T(128)} %get-tuple-element.80) | copy-start | bytes 772
  722.1 181.8 %copy-start.17 = (f32[64]{0:T(128)S(1)}, f32[64]{0:T(128)}, u32[]{:S(2)}) copy-start(f32[64]{0:T(128)} %get-tuple-element.81) | copy-start | bytes 772
  722.1 181.8 %copy-start.18 = (f32[64]{0:T(128)S(1)}, f32[64]{0:T(128)}, u32[]{:S(2)}) copy-start(f32[64]{0:T(128)} %get-tuple-element.82) | copy-start | bytes 772
  727.5 42.4 %copy-start.1 = (f32[96,35,256]{2,1,0:T(8,128)S(1)}, f32[96,35,256]{2,1,0:T(8,128)}, u32[]{:S(2)}) copy-start(f32[96,35,256]{2,1,0:T(8,128)} %gather_fusion) | copy-start | bytes 10321924 | tf_op jit(solution)/shard_map/while
  817.2 42.4 %copy-start.1 = (f32[96,35,256]{2,1,0:T(8,128)S(1)}, f32[96,35,256]{2,1,0:T(8,128)}, u32[]{:S(2)}) copy-start(f32[96,35,256]{2,1,0:T(8,128)} %gather_fusion) | copy-start | bytes 10321924 | tf_op jit(solution)/shard_map/while
  901.5 4.5 copy-start.6
  901.5 4.6 copy-start.7
  901.5 4.6 copy-start.8
  901.5 4.7 copy-start.3
Sparse Core Ops, SparseCore 0:
  12.9 68.9 all-gather.2
where the time goes:
time: 918 us; the launch traced here: 917 us
  blocking collectives  632 us (69%)
  matrix products  179 us (19%)
  starting transfers between devices  67.1 us (7%)
  local copies, waits for them, and re-layouts  19.6 us (2%)
  between operations  14.4 us (2%)
    all_gather x1, blocking collectives, local(): lax.all_gather(dev_skeleton, ('group', 'dev'), axis=0, tiled=True)  337 us
    psum x1, blocking collectives, local(): own_group = lax.psum(image, 'dev')  296 us
    dot_general x2, matrix products, leaf_near(): jnp.einsum('jpq,jvq->vp', tile_value * live, vectors, precision=HIGH)  84.7 us
    dot_general x2, matrix products, leaf_near(): jnp.einsum('jpq,jvq->vp', tile_slope * live, vectors, precision=HIGH)  82.1 us
    ppermute x1, starting transfers between devices, partner(): lax.ppermute(value, axis, [(i, i ^ 1 << distance) for i in range(lax.axis...  56.1 us
  transfers between devices with their start and end apart: 4, of which 0 were waited for; matrix products, arithmetic and copies ran while one was open for 21% of the time, Pallas kernels for 0%

commit v1 on v0

v1 whole, which is shorter than its diff:
```python
import math

import jax
import jax.numpy as jnp
from jax import lax
from jax.experimental import pallas as pl
from jax.experimental.pallas import tpu as pltpu
from jax.sharding import PartitionSpec as P

BF = jnp.bfloat16
F32 = jnp.float32
HIGH = lax.Precision.HIGHEST
REACH = 14
NUGGET = 0.01
LENGTH = 0.8
LOG2E = math.log2(math.e)
LN2 = math.log(2.0)
ALPHA = math.sqrt(3.0) / LENGTH * LOG2E
X0 = ALPHA * ALPHA * NUGGET
VALUE_SCALE = LN2
SLOPE_SCALE = LN2 * LN2 / LENGTH
NODE_ROWS = 24
MIB = 2**20
AXES = ("group", "dev")


def dot(a, b):
    return jnp.dot(a, b, preferred_element_type=F32)


def dot32(a, b):
    return jnp.dot(a, b, preferred_element_type=F32, precision=HIGH)


def split2(x):
    hi = x.astype(BF)
    return hi, (x - hi.astype(F32)).astype(BF)


def split3(x):
    one = x.astype(BF).astype(F32)
    rest = x - one
    two = rest.astype(BF).astype(F32)
    return one, two, rest - two


def matern_terms(x):
    t = x * lax.rsqrt(x)
    e = jnp.exp2(-t)
    return (t + LOG2E) * e, x * e


def source_rows(points):
    b = points * (-2.0 * ALPHA)
    b1, b2, b3 = split3(b)
    m1, m2, m3 = split3(jnp.sum(b * b, axis=0, keepdims=True) * 0.25)
    one = jnp.ones((3, b.shape[1]), F32)
    zero = jnp.zeros((2, b.shape[1]), F32)
    return jnp.concatenate([b1, b2, b1, b2, b3, b1, b3, b2, one, m1, m2, m3, zero], axis=0)


def target_rows(points):
    a = points * ALPHA
    a1, a2, a3 = split3(a)
    n1, n2, n3 = split3(jnp.sum(a * a, axis=0, keepdims=True) + X0)
    one = jnp.ones((3, a.shape[1]), F32)
    zero = jnp.zeros((2, a.shape[1]), F32)
    return jnp.concatenate([a1, a1, a2, a2, a1, a3, a2, a3, n1, n2, n3, one, zero], axis=0)


def coef_kernel(charges, basis, leaf_transfer, dev_transfer, skeleton, out):
    leaves = charges.shape[0]
    total = jnp.zeros((32, 64), F32)
    for l in range(leaves):
        leaf = lax.dot_general(
            charges[l], basis[l], (((1,), (1,)), ((), ())), precision=HIGH, preferred_element_type=F32
        )
        total += lax.dot_general(
            leaf, leaf_transfer[l], (((1,), (1,)), ((), ())), precision=HIGH, preferred_element_type=F32
        )
    image = lax.dot_general(
        total, dev_transfer[...], (((1,), (1,)), ((), ())), precision=HIGH, preferred_element_type=F32
    )
    out[0:16, :] = jnp.concatenate([total[:16], total[16:]], axis=1)
    out[16:24, :] = jnp.zeros((8, 128), F32)
    out[16:19, 0:64] = skeleton[...]
    out[24:40, :] = jnp.concatenate([image[:16], image[16:]], axis=1)


def near_kernel(place, neighbours, counts, own, before, after, acc, wa, c2, ua, order, *slots):
    leaves, width = neighbours.shape
    pairs = leaves * width
    half = before.shape[0]
    total = leaves + 2 * half
    first = place[0] * leaves - half
    depth = len(slots) // 2
    xs, tiles = slots[:depth], slots[depth:]

    def note(i, carry):
        leaf, slot = i // width, i % width
        chosen = jnp.clip(neighbours[leaf, slot] - first, 0, total - 1)
        order[i] = jnp.where(slot < counts[leaf], chosen, total)
        return carry

    lax.fori_loop(0, pairs, note, 0)

    def prepare(ref, offset, count):
        def step(l, carry):
            rows = ref[l]
            wa[offset + l] = jnp.transpose(source_rows(rows[0:3])).astype(BF)
            hi, lo = split2(rows[8:40])
            c2[offset + l, 0:32, :] = hi
            c2[offset + l, 32:64, :] = lo
            return carry

        lax.fori_loop(0, count, step, 0)

    prepare(before, 0, half)
    prepare(own, half, leaves)
    prepare(after, half + leaves, half)
    wa[total] = wa[half]
    c2[total] = jnp.zeros(c2.shape[1:], BF)

    def aim(l, carry):
        ua[l] = target_rows(own[l, 0:3, :]).astype(BF)
        return carry

    lax.fori_loop(0, leaves, aim, 0)
    acc[...] = jnp.zeros_like(acc)
    tiles[depth - 1][...] = jnp.zeros(tiles[0].shape, BF)
    xs[0][...] = dot(wa[order[0]], ua[0])

    def gather_up(i, tile):
        c = c2[order[i]]
        target = i // width
        one, two = dot(c, tile[0]), dot(c[:32], tile[1])
        three, four = dot(c, tile[2]), dot(c[:32], tile[3])
        acc[target, 0:32, :] += one[:32] + two
        acc[target, 32:64, :] += one[32:]
        acc[target, 64:96, :] += three[:32] + four
        acc[target, 96:128, :] += three[32:]

    def step(i, b):
        after_, before_ = jnp.minimum(i + 1, pairs - 1), jnp.maximum(i - 1, 0)
        xs[(b + 1) % depth][...] = dot(wa[order[after_]], ua[after_ // width])
        value, slope = matern_terms(xs[b][...])
        tiles[b][0], tiles[b][1] = split2(value)
        tiles[b][2], tiles[b][3] = split2(slope)
        gather_up(before_, tiles[(b - 1) % depth])

    def body(j, carry):
        for u in range(depth):
            step(j * depth + u, u)
        return carry

    lax.fori_loop(0, pairs // depth, body, 0)
    gather_up(pairs - 1, tiles[depth - 1])


def far_kernel(place, far_list, mine, theirs, own_skeleton, groups, dev_transfer, leaf_transfer, basis, near,
               value_out, slope_out, coefs, kernels):
    leaves = basis.shape[0]
    rank = place[0]
    group, node = rank // 64, rank % 64
    x0, z0, y0 = node % 4, (node // 4) % 4, node // 16

    def pair_kernel(column, row):
        x = jnp.full((64, 64), X0, F32)
        for c in range(3):
            d = (column[:, c : c + 1] - row[c : c + 1, :]) * ALPHA
            x = x + d * d
        value, slope = matern_terms(x)
        return jnp.concatenate([value * VALUE_SCALE, slope * SLOPE_SCALE], axis=1)

    own = own_skeleton[...]
    for j in range(far_list.shape[1]):
        s = far_list[0, j]
        d = s % 64
        jx, jz, jy = (x0 - d % 4 + 4) % 4, (z0 - (d // 4) % 4 + 4) % 4, (y0 - d // 16 + 4) % 4
        row = pl.multiple_of(((jy * 4 + jz) * 4 + jx) * NODE_ROWS, 8)
        block = jnp.where(s // 64 == group, mine[pl.ds(row, NODE_ROWS), :], theirs[pl.ds(row, NODE_ROWS), :])
        coefs[:, 64 * j : 64 * j + 64] = jnp.concatenate([block[:16, :64], block[:16, 64:]], axis=0)
        kernels[64 * j : 64 * j + 64, :] = pair_kernel(jnp.transpose(block[16:24, :])[:64], own)
    far = dot32(coefs[...], kernels[...])
    other = theirs[theirs.shape[0] - 16 :, :]
    other = jnp.concatenate([other[:, :64], other[:, 64:]], axis=0)
    near_group, far_group = groups[:, pl.ds(group, 1), :][:, 0], groups[:, pl.ds(1 - group, 1), :][:, 0]
    column = jnp.transpose(jnp.concatenate([far_group, jnp.zeros((5, 64), F32)], axis=0))
    top = dot32(other, pair_kernel(column, near_group))
    far = jnp.concatenate([far[:, :64], far[:, 64:]], axis=0)
    top = jnp.concatenate([top[:, :64], top[:, 64:]], axis=0)
    local_dev = far + dot32(top, dev_transfer[...])
    for l in range(leaves):
        part = dot32(dot32(local_dev, leaf_transfer[l]), basis[l])
        value_out[l] = (near[l, 0:32, :] + near[l, 32:64, :]) * VALUE_SCALE + part[:32]
        slope_out[l] = (near[l, 64:96, :] + near[l, 96:128, :]) * SLOPE_SCALE + part[32:]


VMEM = pl.BlockSpec(memory_space=pltpu.VMEM)
SMEM = pl.BlockSpec(memory_space=pltpu.SMEM)


def dev_shift(div, step):
    return [(i, i - (i // div) % 4 * div + ((i // div) % 4 + step) % 4 * div) for i in range(64)]


def gather_nodes(block):
    for div in (1, 4, 16):
        came = [block] + [lax.ppermute(block, "dev", dev_shift(div, k)) for k in (1, 2, 3)]
        images = (came[0][-16:] + came[1][-16:]) + (came[2][-16:] + came[3][-16:])
        block = jnp.concatenate([c[:-16] for c in came] + [images], axis=0)
    return block


def local(points, charges, basis, leaf_transfer, dev_skeleton, dev_transfer, group_skeleton, neighbours, counts, far_list):
    leaves = points.shape[0]
    rank = lax.axis_index(AXES)
    place = jnp.full((1,), rank, jnp.int32)
    stacked = jnp.concatenate([points, jnp.zeros((leaves, 5, 256), F32), charges], axis=1)
    size = lax.axis_size(AXES)
    up = [(i, i + 1) for i in range(size - 1)]
    down = [(j, i) for i, j in up]
    before = lax.ppermute(stacked[leaves - REACH :], AXES, up)
    after = lax.ppermute(stacked[:REACH], AXES, down)
    block = pl.pallas_call(
        coef_kernel,
        out_shape=jax.ShapeDtypeStruct((40, 128), F32),
        in_specs=[VMEM] * 5,
        out_specs=VMEM,
        compiler_params=pltpu.CompilerParams(vmem_limit_bytes=32 * MIB),
    )(charges, basis, leaf_transfer, dev_transfer[0], dev_skeleton[0])
    mine = gather_nodes(block)
    theirs = lax.ppermute(mine, "group", [(0, 1), (1, 0)])
    total = leaves + 2 * REACH
    depth = 4
    near = pl.pallas_call(
        near_kernel,
        out_shape=jax.ShapeDtypeStruct((leaves, 128, 256), F32),
        in_specs=[SMEM] * 3 + [VMEM] * 3,
        out_specs=VMEM,
        scratch_shapes=[
            pltpu.VMEM((total + 1, 256, 32), BF),
            pltpu.VMEM((total + 1, 64, 256), BF),
            pltpu.VMEM((leaves, 32, 256), BF),
            pltpu.SMEM((leaves * neighbours.shape[1],), jnp.int32),
        ]
        + [pltpu.VMEM((256, 256), F32)] * depth
        + [pltpu.VMEM((4, 256, 256), BF)] * depth,
        compiler_params=pltpu.CompilerParams(vmem_limit_bytes=40 * MIB),
    )(place, neighbours, counts, stacked, before, after)
    out = jax.ShapeDtypeStruct((leaves, 32, 256), F32)
    return pl.pallas_call(
        far_kernel,
        out_shape=(out, out),
        in_specs=[SMEM] * 2 + [VMEM] * 8,
        out_specs=(VMEM, VMEM),
        scratch_shapes=[pltpu.VMEM((32, 1024), F32), pltpu.VMEM((1024, 128), F32)],
        compiler_params=pltpu.CompilerParams(vmem_limit_bytes=32 * MIB),
    )(place, far_list, mine, theirs, dev_skeleton[0], jnp.transpose(group_skeleton, (1, 0, 2)), dev_transfer[0],
      leaf_transfer, basis, near)


def solution(mesh):
    leaf = P(AXES, None, None)
    placed = (leaf, leaf, leaf, leaf, leaf, leaf, P(), P(AXES, None), P(AXES), P(AXES, None))
    return jax.shard_map(local, mesh=mesh, in_specs=placed, out_specs=(leaf, leaf), check_vma=False)
```

time: 918 us -> 115 us (0.13)
  the two profiles are of different devices: /device:TPU:1 before, /device:TPU:8 now
where the time goes in v1:
time: 115 us; the launch traced here: 114 us
  Pallas kernels  51.9 us (45%)
  waiting for transfers between devices  33.4 us (29%)
  starting transfers between devices  21.6 us (19%)
  local copies, waits for them, and re-layouts  6.11 us (5%)
    pallas_call x1, Pallas kernels, local(): pl.pallas_call(near_kernel, out_shape=jax.ShapeDtypeStruct((leaves, 128,...  43.6 us
    ppermute x9, starting transfers between devices, gather_nodes(): lax.ppermute(block, 'dev', dev_shift(div, k))  15 us
    ppermute x9, waiting for transfers between devices, gather_nodes(): lax.ppermute(block, 'dev', dev_shift(div, k))  13.8 us
    ppermute x1, waiting for transfers between devices, local(): after = lax.ppermute(stacked[:REACH], AXES, down)  11.3 us
    ppermute x1, waiting for transfers between devices, local(): before = lax.ppermute(stacked[leaves - REACH:], AXES, up)  8.34 us
    pallas_call x1, Pallas kernels, local(): pl.pallas_call(far_kernel, out_shape=(out, out), in_specs=[SMEM] * 2 + [V...  6.19 us
    unnamed x36, local copies, waits for them, and re-layouts  4.91 us
    ppermute x1, starting transfers between devices, local(): after = lax.ppermute(stacked[:REACH], AXES, down)  4.65 us
  transfers between devices with their start and end apart: 12, of which 7 were waited for; matrix products, arithmetic and copies ran while one was open for 1% of the time, Pallas kernels for 38%

profile of v1, /device:TPU:8, one launch (start us, length us, event | category | flops | bytes accessed | tf_op | source)
XLA Modules:
  0.0 114.1 jit_solution(16195031824743893824)
XLA Ops:
  0.6 0.7 copy.15
  1.3 1.2 %copy-done = f32[16,64,256]{2,1,0:T(8,128)S(1)} copy-done((f32[16,64,256]{2,1,0:T(8,128)S(1)}, f32[16,64,256]{2,1,0:T(8,128)}, u32[]{:S(2)}) %copy-start) | copy-done | bytes 1048600
  2.5 1.0 copy-done.2
  3.6 1.0 copy-done.3
  4.6 0.8 copy-done.5
  5.4 2.2 %shard_map.113 = f32[40,128]{1,0:T(8,128)S(1)} custom-call(f32[16,32,256]{2,1,0:T(8,128)S(1)} %copy-done.2, f32[16,64,256]{2,1,0:T(8,128)S(1)} %copy-done, f32[16,64,64]{2,1,0:T(8,128)S(1)} %copy-done.3, f32[64,64]{1,0:T(8,128)S(1)} %bitcast.6, f32[3,64]{1,0:T(4,128)S(1)} %bitcast.8), custom_call_target="tpu_custom_call" | custom-call | tf_op jit(solution)/shard_map/pallas_call | solution.py:225
  7.6 2.8 %collective-permute-start.2 = (f32[40,128]{1,0:T(8,128)S(1)}, f32[40,128]{1,0:T(8,128)S(1)}, u32[]{:S(2)}, u32[]{:S(2)}) collective-permute-start(f32[40,128]{1,0:T(8,128)S(1)} %shard_map.113), channel_id=1, source_target_pairs={{0,3},{1,0},{2,1},{3,2},{4,7},{5,4},{6,5},{7,6},{8,11},{9,8},{10,9... | collective-permute-start | bytes 61448 | tf_op jit(solution)/shard_map/ppermute | solution.py:209
  10.4 0.8 collective-permute-start.1
  11.2 0.9 collective-permute-start
  12.1 4.1 %collective-permute-done = f32[40,128]{1,0:T(8,128)S(1)} collective-permute-done((f32[40,128]{1,0:T(8,128)S(1)}, f32[40,128]{1,0:T(8,128)S(1)}, u32[]{:S(2)}, u32[]{:S(2)}) %collective-permute-start) | collective-permute-done | bytes 20512 | tf_op jit(solution)/shard_map/ppermute | solution.py:209
  16.3 2.0 %collective-permute-start.3 = (f32[112,128]{1,0:T(8,128)S(1)}, f32[112,128]{1,0:T(8,128)S(1)}, u32[]{:S(2)}, u32[]{:S(2)}) collective-permute-start(f32[112,128]{1,0:T(8,128)S(1)} %get-tuple-element.4), channel_id=1, source_target_pairs={{0,4},{1,5},{2,6},{3,7},{4,8},{5,9},{6,10},{7,11},{8,12},{9,13},{1... | collective-permute-start | bytes 172040 | tf_op jit(solution)/shard_map/ppermute | solution.py:209
  18.3 0.1 pad.1.clone
  18.4 2.2 %collective-permute-start.5 = (f32[112,128]{1,0:T(8,128)S(1)}, f32[112,128]{1,0:T(8,128)S(1)}, u32[]{:S(2)}, u32[]{:S(2)}) collective-permute-start(f32[112,128]{1,0:T(8,128)S(1)} %get-tuple-element.4), channel_id=1, source_target_pairs={{0,12},{1,13},{2,14},{3,15},{4,0},{5,1},{6,2},{7,3},{8,4},{9,5},{1... | collective-permute-start | bytes 172040 | tf_op jit(solution)/shard_map/ppermute | solution.py:209
  20.5 1.8 %collective-permute-start.4 = (f32[112,128]{1,0:T(8,128)S(1)}, f32[112,128]{1,0:T(8,128)S(1)}, u32[]{:S(2)}, u32[]{:S(2)}) collective-permute-start(f32[112,128]{1,0:T(8,128)S(1)} %get-tuple-element.4), channel_id=1, source_target_pairs={{0,8},{1,9},{2,10},{3,11},{4,12},{5,13},{6,14},{7,15},{8,0},{9,1},... | collective-permute-start | bytes 172040 | tf_op jit(solution)/shard_map/ppermute | solution.py:209
  22.4 0.2 collective-permute-done.3
  22.6 3.7 %collective-permute-done.4 = f32[112,128]{1,0:T(8,128)S(1)} collective-permute-done((f32[112,128]{1,0:T(8,128)S(1)}, f32[112,128]{1,0:T(8,128)S(1)}, u32[]{:S(2)}, u32[]{:S(2)}) %collective-permute-start.4) | collective-permute-done | bytes 57376 | tf_op jit(solution)/shard_map/ppermute | solution.py:209
  26.3 0.0 copy-start.7
  26.3 0.0 copy-start.9
  26.3 1.6 %collective-permute-start.6 = (f32[400,128]{1,0:T(8,128)S(1)}, f32[400,128]{1,0:T(8,128)S(1)}, u32[]{:S(2)}, u32[]{:S(2)}) collective-permute-start(f32[400,128]{1,0:T(8,128)S(1)} %get-tuple-element.2), channel_id=1, source_target_pairs={{0,16},{1,17},{2,18},{3,19},{4,20},{5,21},{6,22},{7,23},{8,24},{9,... | collective-permute-start | bytes 614408 | tf_op jit(solution)/shard_map/ppermute | solution.py:209
  28.0 0.1 pad_maximum_fusion.own
  28.1 0.5 collective-permute-start.8
  28.6 2.3 %collective-permute-start.7 = (f32[400,128]{1,0:T(8,128)S(1)}, f32[400,128]{1,0:T(8,128)S(1)}, u32[]{:S(2)}, u32[]{:S(2)}) collective-permute-start(f32[400,128]{1,0:T(8,128)S(1)} %get-tuple-element.2), channel_id=1, source_target_pairs={{0,32},{1,33},{2,34},{3,35},{4,36},{5,37},{6,38},{7,39},{8,40},{9,... | collective-permute-start | bytes 614408 | tf_op jit(solution)/shard_map/ppermute | solution.py:209
  30.9 2.5 %collective-permute-done.6 = f32[400,128]{1,0:T(8,128)S(1)} collective-permute-done((f32[400,128]{1,0:T(8,128)S(1)}, f32[400,128]{1,0:T(8,128)S(1)}, u32[]{:S(2)}, u32[]{:S(2)}) %collective-permute-start.6) | collective-permute-done | bytes 204832 | tf_op jit(solution)/shard_map/ppermute | solution.py:209
  33.4 3.4 %collective-permute-done.7 = f32[400,128]{1,0:T(8,128)S(1)} collective-permute-done((f32[400,128]{1,0:T(8,128)S(1)}, f32[400,128]{1,0:T(8,128)S(1)}, u32[]{:S(2)}, u32[]{:S(2)}) %collective-permute-start.7) | collective-permute-done | bytes 204832 | tf_op jit(solution)/shard_map/ppermute | solution.py:209
  36.9 0.1 collective-permute-start.9
  37.0 1.1 fusion.5
  38.1 4.7 %collective-permute-start.11 = (f32[14,40,256]{2,1,0:T(8,128)}, f32[14,40,256]{2,1,0:T(8,128)}, u32[]{:S(2)}, u32[]{:S(2)}) collective-permute-start(f32[14,40,256]{2,1,0:T(8,128)} %get-tuple-element.6), channel_id=1, source_target_pairs={{1,0},{2,1},{3,2},{4,3},{5,4},{6,5},{7,6},{8,7},{9,8},{10,9},{11,1... | collective-permute-start | bytes 1720328 | tf_op jit(solution)/shard_map/ppermute | solution.py:224
  42.8 1.9 %collective-permute-start.10 = (f32[14,40,256]{2,1,0:T(8,128)}, f32[14,40,256]{2,1,0:T(8,128)}, u32[]{:S(2)}, u32[]{:S(2)}) collective-permute-start(f32[14,40,256]{2,1,0:T(8,128)} %get-tuple-element.7), channel_id=1, source_target_pairs={{0,1},{1,2},{2,3},{3,4},{4,5},{5,6},{6,7},{7,8},{8,9},{9,10},{10,1... | collective-permute-start | bytes 1720328 | tf_op jit(solution)/shard_map/ppermute | solution.py:223
  44.7 11.3 %collective-permute-done.11.after = f32[14,40,256]{2,1,0:T(8,128)} collective-permute-done((f32[14,40,256]{2,1,0:T(8,128)}, f32[14,40,256]{2,1,0:T(8,128)}, u32[]{:S(2)}, u32[]{:S(2)}) %collective-permute-start.11) | collective-permute-done | bytes 573472 | tf_op jit(solution)/shard_map/ppermute | solution.py:224
  56.0 8.3 %collective-permute-done.10.before = f32[14,40,256]{2,1,0:T(8,128)} collective-permute-done((f32[14,40,256]{2,1,0:T(8,128)}, f32[14,40,256]{2,1,0:T(8,128)}, u32[]{:S(2)}, u32[]{:S(2)}) %collective-permute-start.10) | collective-permute-done | bytes 573472 | tf_op jit(solution)/shard_map/ppermute | solution.py:223
  64.3 43.6 %shard_map.114.near = f32[16,128,256]{2,1,0:T(8,128)S(1)} custom-call(s32[1]{0:T(128)} %bitcast.place, s32[16,12]{1,0:T(8,128)S(1)} %copy-done.7, s32[16]{0:T(128)S(1)} %copy-done.9, f32[16,40,256]{2,1,0:T(8,128)S(1)} %pad_maximum_fusion.own, f32[14,40,256]{2,1,0:T(8,128)} %collective-permute-done.10.before, f32[14,40,256]{2,1,0:T(8,128)} %collective-permute-done.11.after), custom_call_target="tpu_custom_call" | custom-call | tf_op jit(solution)/shard_map/pallas_call | solution.py:236
  107.9 6.2 %shard_map.115 = (f32[16,32,256]{2,1,0:T(8,128)}, f32[16,32,256]{2,1,0:T(8,128)}) custom-call(s32[1]{0:T(128)} %bitcast.place, s32[1,16]{1,0:T(1,128)S(1)} %copy-done.10, f32[1552,128]{1,0:T(8,128)S(1)} %constant_dynamic-update-slice_fusion.13.mine, f32[1552,128]{1,0:T(8,128)} %collective-permute-done.9.theirs, f32[3,64]{1,0:T(4,128)S(1)} %bitcast.9, ...), custom_call_target="tpu_custom_call" | custom-call | tf_op jit(solution)/shard_map/pallas_call | solution.py:252
  (38 shorter events, 0.2 us)
Async XLA Ops:
  1.3 1.2 %copy-start = (f32[16,64,256]{2,1,0:T(8,128)S(1)}, f32[16,64,256]{2,1,0:T(8,128)}, u32[]{:S(2)}) copy-start(f32[16,64,256]{2,1,0:T(8,128)} %basis.3) | copy-start | bytes 3145732
  2.5 1.0 copy-start.2
  3.6 1.0 copy-start.3
  4.6 0.8 copy-start.5
  5.4 12.9 %copy-start.11 = (f32[16,3,256]{2,0,1:T(8,128)S(1)}, f32[16,3,256]{2,0,1:T(8,128)}, u32[]{:S(2)}) copy-start(f32[16,3,256]{2,0,1:T(8,128)} %param.10) | copy-start | bytes 147460
  7.6 8.7 %collective-permute-start.2 = (f32[40,128]{1,0:T(8,128)S(1)}, f32[40,128]{1,0:T(8,128)S(1)}, u32[]{:S(2)}, u32[]{:S(2)}) collective-permute-start(f32[40,128]{1,0:T(8,128)S(1)} %shard_map.113), channel_id=1, source_target_pairs={{0,3},{1,0},{2,1},{3,2},{4,7},{5,4},{6,5},{7,6},{8,11},{9,8},{10,9... | collective-permute-start | bytes 61448 | tf_op jit(solution)/shard_map/ppermute | solution.py:209
  10.4 5.8 %collective-permute-start.1 = (f32[40,128]{1,0:T(8,128)S(1)}, f32[40,128]{1,0:T(8,128)S(1)}, u32[]{:S(2)}, u32[]{:S(2)}) collective-permute-start(f32[40,128]{1,0:T(8,128)S(1)} %shard_map.113), channel_id=1, source_target_pairs={{0,2},{1,3},{2,0},{3,1},{4,6},{5,7},{6,4},{7,5},{8,10},{9,11},{10,... | collective-permute-start | bytes 61448 | tf_op jit(solution)/shard_map/ppermute | solution.py:209
  11.2 5.0 %collective-permute-start = (f32[40,128]{1,0:T(8,128)S(1)}, f32[40,128]{1,0:T(8,128)S(1)}, u32[]{:S(2)}, u32[]{:S(2)}) collective-permute-start(f32[40,128]{1,0:T(8,128)S(1)} %shard_map.113), channel_id=1, source_target_pairs={{0,1},{1,2},{2,3},{3,0},{4,5},{5,6},{6,7},{7,4},{8,9},{9,10},{10,1... | collective-permute-start | bytes 61448 | tf_op jit(solution)/shard_map/ppermute | solution.py:209
  16.3 6.3 %collective-permute-start.3 = (f32[112,128]{1,0:T(8,128)S(1)}, f32[112,128]{1,0:T(8,128)S(1)}, u32[]{:S(2)}, u32[]{:S(2)}) collective-permute-start(f32[112,128]{1,0:T(8,128)S(1)} %get-tuple-element.4), channel_id=1, source_target_pairs={{0,4},{1,5},{2,6},{3,7},{4,8},{5,9},{6,10},{7,11},{8,12},{9,13},{1... | collective-permute-start | bytes 172040 | tf_op jit(solution)/shard_map/ppermute | solution.py:209
  18.4 7.9 %collective-permute-start.5 = (f32[112,128]{1,0:T(8,128)S(1)}, f32[112,128]{1,0:T(8,128)S(1)}, u32[]{:S(2)}, u32[]{:S(2)}) collective-permute-start(f32[112,128]{1,0:T(8,128)S(1)} %get-tuple-element.4), channel_id=1, source_target_pairs={{0,12},{1,13},{2,14},{3,15},{4,0},{5,1},{6,2},{7,3},{8,4},{9,5},{1... | collective-permute-start | bytes 172040 | tf_op jit(solution)/shard_map/ppermute | solution.py:209
  20.5 5.7 %collective-permute-start.4 = (f32[112,128]{1,0:T(8,128)S(1)}, f32[112,128]{1,0:T(8,128)S(1)}, u32[]{:S(2)}, u32[]{:S(2)}) collective-permute-start(f32[112,128]{1,0:T(8,128)S(1)} %get-tuple-element.4), channel_id=1, source_target_pairs={{0,8},{1,9},{2,10},{3,11},{4,12},{5,13},{6,14},{7,15},{8,0},{9,1},... | collective-permute-start | bytes 172040 | tf_op jit(solution)/shard_map/ppermute | solution.py:209
  26.3 38.0 %copy-start.7 = (s32[16,12]{1,0:T(8,128)S(1)}, s32[16,12]{1,0:T(8,128)}, u32[]{:S(2)}) copy-start(s32[16,12]{1,0:T(8,128)} %neighbours.1) | copy-start | bytes 2308
  26.3 38.0 %copy-start.9 = (s32[16]{0:T(128)S(1)}, s32[16]{0:T(128)}, u32[]{:S(2)}) copy-start(s32[16]{0:T(128)} %counts.1) | copy-start | bytes 196
  26.3 7.1 %collective-permute-start.6 = (f32[400,128]{1,0:T(8,128)S(1)}, f32[400,128]{1,0:T(8,128)S(1)}, u32[]{:S(2)}, u32[]{:S(2)}) collective-permute-start(f32[400,128]{1,0:T(8,128)S(1)} %get-tuple-element.2), channel_id=1, source_target_pairs={{0,16},{1,17},{2,18},{3,19},{4,20},{5,21},{6,22},{7,23},{8,24},{9,... | collective-permute-start | bytes 614408 | tf_op jit(solution)/shard_map/ppermute | solution.py:209
  28.1 8.8 %collective-permute-start.8 = (f32[400,128]{1,0:T(8,128)S(1)}, f32[400,128]{1,0:T(8,128)S(1)}, u32[]{:S(2)}, u32[]{:S(2)}) collective-permute-start(f32[400,128]{1,0:T(8,128)S(1)} %get-tuple-element.2), channel_id=1, source_target_pairs={{0,48},{1,49},{2,50},{3,51},{4,52},{5,53},{6,54},{7,55},{8,56},{9,... | collective-permute-start | bytes 614408 | tf_op jit(solution)/shard_map/ppermute | solution.py:209
  28.6 8.2 %collective-permute-start.7 = (f32[400,128]{1,0:T(8,128)S(1)}, f32[400,128]{1,0:T(8,128)S(1)}, u32[]{:S(2)}, u32[]{:S(2)}) collective-permute-start(f32[400,128]{1,0:T(8,128)S(1)} %get-tuple-element.2), channel_id=1, source_target_pairs={{0,32},{1,33},{2,34},{3,35},{4,36},{5,37},{6,38},{7,39},{8,40},{9,... | collective-permute-start | bytes 614408 | tf_op jit(solution)/shard_map/ppermute | solution.py:209
  36.9 71.0 %collective-permute-start.9 = (f32[1552,128]{1,0:T(8,128)S(1)}, f32[1552,128]{1,0:T(8,128)}, u32[]{:S(2)}, u32[]{:S(2)}) collective-permute-start(f32[1552,128]{1,0:T(8,128)S(1)} %constant_dynamic-update-slice_fusion.13.mine), channel_id=1, source_target_pairs={{0,64},{64,0},{1,65},{65,1},{2,66},{66,2},{3,67},{67,3},{4,68},{68... | collective-permute-start | bytes 2383880 | tf_op jit(solution)/shard_map/ppermute | solution.py:233
  38.1 69.8 %copy-start.1 = (f32[16,64,256]{2,1,0:T(8,128)S(1)}, f32[16,64,256]{2,1,0:T(8,128)}, u32[]{:S(2)}) copy-start(f32[16,64,256]{2,1,0:T(8,128)} %basis.3) | copy-start | bytes 3145732
  38.1 69.8 %copy-start.4 = (f32[16,64,64]{2,1,0:T(8,128)S(1)}, f32[16,64,64]{2,1,0:T(8,128)}, u32[]{:S(2)}) copy-start(f32[16,64,64]{2,1,0:T(8,128)} %leaf_transfer.3) | copy-start | bytes 786436
  38.1 69.8 %copy-start.6 = (f32[1,64,64]{2,1,0:T(8,128)S(1)}, f32[1,64,64]{2,1,0:T(8,128)}, u32[]{:S(2)}) copy-start(f32[1,64,64]{2,1,0:T(8,128)} %param.15) | copy-start | bytes 49156
  38.1 69.8 %copy-start.8 = (f32[2,3,64]{2,0,1:T(2,128)S(1)}, f32[2,3,64]{2,0,1:T(2,128)}, u32[]{:S(2)}) copy-start(f32[2,3,64]{2,0,1:T(2,128)} %param.16) | copy-start | bytes 4612
  38.1 69.8 %copy-start.10 = (s32[1,16]{1,0:T(1,128)S(1)}, s32[1,16]{1,0:T(1,128)}, u32[]{:S(2)}) copy-start(s32[1,16]{1,0:T(1,128)} %far_list.1) | copy-start | bytes 196
  38.1 17.8 %collective-permute-start.11 = (f32[14,40,256]{2,1,0:T(8,128)}, f32[14,40,256]{2,1,0:T(8,128)}, u32[]{:S(2)}, u32[]{:S(2)}) collective-permute-start(f32[14,40,256]{2,1,0:T(8,128)} %get-tuple-element.6), channel_id=1, source_target_pairs={{1,0},{2,1},{3,2},{4,3},{5,4},{6,5},{7,6},{8,7},{9,8},{10,9},{11,1... | collective-permute-start | bytes 1720328 | tf_op jit(solution)/shard_map/ppermute | solution.py:224
  42.8 21.5 %collective-permute-start.10 = (f32[14,40,256]{2,1,0:T(8,128)}, f32[14,40,256]{2,1,0:T(8,128)}, u32[]{:S(2)}, u32[]{:S(2)}) collective-permute-start(f32[14,40,256]{2,1,0:T(8,128)} %get-tuple-element.7), channel_id=1, source_target_pairs={{0,1},{1,2},{2,3},{3,4},{4,5},{5,6},{6,7},{7,8},{8,9},{9,10},{10,1... | collective-permute-start | bytes 1720328 | tf_op jit(solution)/shard_map/ppermute | solution.py:223

commit v2 on v1

v2 whole, which is shorter than its diff:
```python
import math

import jax
import jax.numpy as jnp
from jax import lax
from jax.experimental import pallas as pl
from jax.experimental.pallas import tpu as pltpu
from jax.sharding import PartitionSpec as P

BF = jnp.bfloat16
F32 = jnp.float32
HIGH = lax.Precision.HIGHEST
REACH = 14
NUGGET = 0.01
LENGTH = 0.8
LOG2E = math.log2(math.e)
LN2 = math.log(2.0)
ALPHA = math.sqrt(3.0) / LENGTH * LOG2E
X0 = ALPHA * ALPHA * NUGGET
VALUE_SCALE = LN2
SLOPE_SCALE = LN2 * LN2 / LENGTH
NODE_ROWS = 24
DEPTH = 4
CUTS = (4, 12, 24)
MIB = 2**20
AXES = ("group", "dev")


def dot(a, b):
    return jnp.dot(a, b, preferred_element_type=F32)


def dot32(a, b):
    return jnp.dot(a, b, preferred_element_type=F32, precision=HIGH)


def split2(x):
    hi = x.astype(BF)
    return hi, (x - hi.astype(F32)).astype(BF)


def split3(x):
    one = x.astype(BF).astype(F32)
    rest = x - one
    two = rest.astype(BF).astype(F32)
    return one, two, rest - two


def matern_terms(x):
    t = x * lax.rsqrt(x)
    e = jnp.exp2(-t)
    return (t + LOG2E) * e, x * e


def write_rows(rows, points, source):
    leaves = points[0].shape[0]
    spread = rows.shape[0] // 2

    def put(row, value):
        for h in range(2):
            rows[pl.ds(h * spread + row, leaves, stride=32), :] = value[:, 128 * h : 128 * h + 128]

    scaled = [p * (-2.0 * ALPHA if source else ALPHA) for p in points]
    square = scaled[0] * scaled[0] + scaled[1] * scaled[1] + scaled[2] * scaled[2]
    square = square * 0.25 if source else square + X0
    picks = (0, 1, 0, 1, 2, 0, 2, 1) if source else (0, 0, 1, 1, 0, 2, 1, 2)
    for c, value in enumerate(scaled):
        parts = split3(value)
        for r, pick in enumerate(picks):
            put(8 * c + r, parts[pick])
    one = jnp.ones_like(square)
    norms = split3(square)
    for r in range(3):
        put(24 + r, one if source else norms[r])
        put(27 + r, norms[r] if source else one)
        if r:
            put(29 + r, jnp.zeros_like(square))


def leaf_rows(rows, l):
    spread = rows.shape[0] // 2
    return [rows[pl.ds(h * spread + 32 * l, 32), :] for h in range(2)]


def write_source(wa, at, rows, l):
    for h, part in enumerate(leaf_rows(rows, l)):
        wa[at, 128 * h : 128 * h + 128, :] = jnp.transpose(part).astype(BF)


def node_block(charges, basis, leaf_transfer, dev_transfer, skeleton, out):
    total = jnp.zeros((32, 64), F32)
    for l in range(charges.shape[0]):
        leaf = lax.dot_general(
            charges[l], basis[l], (((1,), (1,)), ((), ())), precision=HIGH, preferred_element_type=F32
        )
        total += lax.dot_general(
            leaf, leaf_transfer[l], (((1,), (1,)), ((), ())), precision=HIGH, preferred_element_type=F32
        )
    image = lax.dot_general(
        total, dev_transfer[...], (((1,), (1,)), ((), ())), precision=HIGH, preferred_element_type=F32
    )
    out[0:16, :] = jnp.concatenate([total[:16], total[16:]], axis=1)
    out[16:24, :] = jnp.zeros((8, 128), F32)
    for c in range(3):
        out[16 + c : 17 + c, 0:64] = skeleton[c]
    out[24:40, :] = jnp.concatenate([image[:16], image[16:]], axis=1)


def prepare_kernel(reach, place, points_in, charges_in, neighbours_in, counts_in, basis_in, leaf_transfer_in, dev_transfer_in,
                   skeleton_in, up, down, packed, order, limits, block,
                   rows, points, charges, neighbours, counts, basis, leaf_transfer, dev_transfer, skeleton, sems):
    leaves, width = neighbours.shape
    sources = (points_in, charges_in, neighbours_in, counts_in, basis_in, leaf_transfer_in, dev_transfer_in, skeleton_in)
    targets = (points, charges, neighbours, counts, basis, leaf_transfer, dev_transfer, skeleton)
    loads = [pltpu.make_async_copy(a, b, sems.at[i]) for i, (a, b) in enumerate(zip(sources, targets))]
    for load in loads:
        load.start()
    loads[0].wait()
    coords = [points[c] for c in range(3)]
    for source in (True, False):
        write_rows(rows, coords, source)
        at = 0 if source else 32
        for l in range(leaves):
            packed[l, at : at + 32, :] = jnp.concatenate(leaf_rows(rows, l), axis=1).astype(BF)
    for ref, first in ((up, leaves - reach), (down, 0)):
        for c in range(3):
            at = 32 * reach + 16 * c
            ref[at : at + reach, :] = coords[c][first : first + reach]
            ref[at + reach : at + 16, :] = jnp.zeros((16 - reach, 256), F32)
    loads[1].wait()
    for l in range(leaves):
        packed[l, 64:96, :], packed[l, 96:128, :] = split2(charges[l])
        for ref, first in ((up, leaves - reach), (down, 0)):
            if 0 <= l - first < reach:
                ref[32 * (l - first) : 32 * (l - first) + 32, :] = charges[l]
    loads[2].wait()
    loads[3].wait()

    base = place[0] * leaves - reach

    def note(slot, at):
        for leaf in range(leaves):
            chosen = jnp.clip(neighbours[leaf, slot] - base, 0, leaves + 2 * reach - 1)
            order[at] = leaf * 64 + chosen
            at = at + (slot < counts[leaf]).astype(jnp.int32)
        return at

    ends = lax.fori_loop(0, width, note, 0)
    for k in range(DEPTH):
        order[ends + k] = leaves + 2 * reach
    limits[0] = (ends + DEPTH - 1) // DEPTH
    for load in loads[4:]:
        load.wait()
    node_block(charges, basis, leaf_transfer, dev_transfer, skeleton, block)


def merge_kernel(one, two, three, four, earlier, out):
    del earlier
    came = (one, two, three, four)
    count = one.shape[0] - 16
    for i, ref in enumerate(came):
        out[count * i : count * i + count, :] = ref[:count, :]
    out[4 * count :, :] = (one[count:, :] + two[count:, :]) + (three[count:, :] + four[count:, :])


def near_pairs(lo, hi, order, wa, c2, ua, acc, slots):
    xs, tiles = slots[:DEPTH], slots[DEPTH:]
    acc[...] = jnp.zeros_like(acc)
    tiles[DEPTH - 1][...] = jnp.zeros(tiles[0].shape, BF)

    def distances(i):
        pair = order[i]
        return dot(wa[pair % 64], ua[pair // 64])

    def gather_up(i, tile):
        pair = order[i]
        c, target = c2[pair % 64], pair // 64
        one, two = dot(c, tile[0]), dot(c[:32], tile[1])
        three, four = dot(c, tile[2]), dot(c[:32], tile[3])
        acc[target, 0:32, :] += one[:32] + two
        acc[target, 32:64, :] += one[32:]
        acc[target, 64:96, :] += three[:32] + four
        acc[target, 96:128, :] += three[32:]

    def step(i, b):
        xs[(b + 1) % DEPTH][...] = distances(jnp.minimum(i + 1, DEPTH * hi - 1))
        value, slope = matern_terms(xs[b][...])
        tiles[b][0], tiles[b][1] = split2(value)
        tiles[b][2], tiles[b][3] = split2(slope)
        gather_up(jnp.maximum(i - 1, DEPTH * lo), tiles[(b - 1) % DEPTH])

    def body(j, carry):
        for u in range(DEPTH):
            step(j * DEPTH + u, u)
        return carry

    @pl.when(jnp.asarray(hi > lo))
    def _():
        xs[0][...] = distances(DEPTH * lo)
        lax.fori_loop(lo, hi, body, 0)
        gather_up(DEPTH * hi - 1, tiles[DEPTH - 1])


def unpack(packed, offset, wa, c2):
    for l in range(packed.shape[0]):
        wa[offset + l] = jnp.transpose(packed[l, 0:32, :].astype(F32)).astype(BF)
        c2[offset + l] = packed[l, 64:128, :]


class Targets:
    def __init__(self, packed):
        self.packed = packed

    def __getitem__(self, i):
        return self.packed[i, 32:64, :]


class Selves:
    def __getitem__(self, i):
        return i * 65


def own_kernel(end, packed, earlier, acc, wa, c2, *slots):
    del earlier
    unpack(packed, 0, wa, c2)
    near_pairs(0, end, Selves(), wa, c2, Targets(packed), acc, slots)


def first_kernel(begin, end, order, limits, packed, before, after, earlier, acc, wa, c2, rows, *slots):
    del earlier
    leaves, half = packed.shape[0], before.shape[0] // 35
    total = leaves + 2 * half
    unpack(packed, half, wa, c2)
    for ref, offset in ((before, 0), (after, half + leaves)):
        write_rows(rows, [ref[32 * half + 16 * c : 32 * half + 16 * c + half, :] for c in range(3)], True)
        for l in range(half):
            write_source(wa, offset + l, rows, l)
            c2[offset + l, 0:32, :], c2[offset + l, 32:64, :] = split2(ref[32 * l : 32 * l + 32, :])
    wa[total] = wa[half]
    c2[total] = jnp.zeros(c2.shape[1:], BF)
    near_pairs(jnp.minimum(begin, limits[0]), jnp.minimum(end, limits[0]), order, wa, c2, Targets(packed), acc, slots)


def next_kernel(begin, end, order, limits, wa, c2, packed, earlier, acc, *slots):
    del earlier
    near_pairs(jnp.minimum(begin, limits[0]), jnp.minimum(end, limits[0]), order, wa, c2, Targets(packed), acc, slots)


def far_kernel(place, far_list, mine, theirs, own_skeleton, groups, dev_transfer, leaf_transfer, basis, near0, near1, near2, near3,
               value_out, slope_out, coefs, kernels):
    leaves = basis.shape[0]
    rank = place[0]
    group, node = rank // 64, rank % 64
    x0, z0, y0 = node % 4, (node // 4) % 4, node // 16

    def pair_kernel(column, row):
        x = jnp.full((64, 64), X0, F32)
        for c in range(3):
            d = (column[:, c : c + 1] - row[c : c + 1, :]) * ALPHA
            x = x + d * d
        value, slope = matern_terms(x)
        return jnp.concatenate([value * VALUE_SCALE, slope * SLOPE_SCALE], axis=1)

    own = jnp.concatenate([own_skeleton[c] for c in range(3)], axis=0)
    for j in range(far_list.shape[1]):
        s = far_list[0, j]
        d = s % 64
        jx, jz, jy = (x0 - d % 4 + 4) % 4, (z0 - (d // 4) % 4 + 4) % 4, (y0 - d // 16 + 4) % 4
        row = pl.multiple_of(((jx * 4 + jz) * 4 + jy) * NODE_ROWS, 8)
        block = jnp.where(s // 64 == group, mine[pl.ds(row, NODE_ROWS), :], theirs[pl.ds(row, NODE_ROWS), :])
        coefs[:, 64 * j : 64 * j + 64] = jnp.concatenate([block[:16, :64], block[:16, 64:]], axis=0)
        kernels[64 * j : 64 * j + 64, :] = pair_kernel(jnp.transpose(block[16:24, :])[:64], own)
    far = dot32(coefs[...], kernels[...])
    other = theirs[theirs.shape[0] - 16 :, :]
    other = jnp.concatenate([other[:, :64], other[:, 64:]], axis=0)
    near_group, far_group = groups[:, pl.ds(group, 1), :][:, 0], groups[:, pl.ds(1 - group, 1), :][:, 0]
    column = jnp.transpose(jnp.concatenate([far_group, jnp.zeros((5, 64), F32)], axis=0))
    top = dot32(other, pair_kernel(column, near_group))
    far = jnp.concatenate([far[:, :64], far[:, 64:]], axis=0)
    top = jnp.concatenate([top[:, :64], top[:, 64:]], axis=0)
    local_dev = far + dot32(top, dev_transfer[...])
    for l in range(leaves):
        part = dot32(dot32(local_dev, leaf_transfer[l]), basis[l])
        near = (near0[l] + near1[l]) + (near2[l] + near3[l])
        value_out[l] = (near[0:32] + near[32:64]) * VALUE_SCALE + part[:32]
        slope_out[l] = (near[64:96] + near[96:128]) * SLOPE_SCALE + part[32:]


VMEM = pl.BlockSpec(memory_space=pltpu.VMEM)
SMEM = pl.BlockSpec(memory_space=pltpu.SMEM)


def dev_shift(div, step):
    return [(i, i - (i // div) % 4 * div + ((i // div) % 4 + step) % 4 * div) for i in range(64)]


def local(points, charges, basis, leaf_transfer, dev_skeleton, dev_transfer, group_skeleton, neighbours, counts, far_list):
    leaves, width = neighbours.shape
    place = jnp.full((1,), lax.axis_index(AXES), jnp.int32)
    size = lax.axis_size(AXES)
    forward = [(i, i + 1) for i in range(size - 1)]
    anywhere = pl.BlockSpec(memory_space=pl.ANY)
    light = pl.CostEstimate(flops=1000, bytes_accessed=1000, transcendentals=0)

    def call(kernel, outs, ins, scratch, args, limit):
        return pl.pallas_call(
            kernel,
            out_shape=tuple(jax.ShapeDtypeStruct(shape, kind) for shape, kind in outs),
            in_specs=ins,
            out_specs=tuple(SMEM if kind == jnp.int32 else VMEM for _, kind in outs),
            scratch_shapes=scratch,
            compiler_params=pltpu.CompilerParams(vmem_limit_bytes=limit * MIB),
            cost_estimate=light,
        )(*args)

    def gathered(block, div, earlier):
        rows = 4 * block.shape[0] - 48
        came = [block] + [lax.ppermute(block, "dev", dev_shift(div, k)) for k in (1, 2, 3)]
        return call(merge_kernel, [((rows, 128), F32)], [VMEM] * 4 + [anywhere], [], (*came, earlier), 8)[0]

    points = jnp.transpose(points, (1, 0, 2))
    skeleton = jnp.transpose(dev_skeleton, (1, 0, 2))
    total = leaves + 2 * REACH
    strip = ((REACH * 32 + 48, 256), F32)
    rows = pltpu.VMEM((leaves * 64, 128), F32)
    held = (points, charges, neighbours, counts, basis, leaf_transfer, dev_transfer[0], skeleton)
    up, down, packed, order, limits, mine = call(
        lambda *refs: prepare_kernel(REACH, *refs),
        [strip, strip, ((leaves, 128, 256), BF),
         ((leaves * width + 2 * DEPTH,), jnp.int32), ((1,), jnp.int32), ((40, 128), F32)],
        [SMEM] + [pl.BlockSpec(memory_space=pltpu.HBM)] * 8,
        [rows] + [(pltpu.SMEM if h.dtype == jnp.int32 else pltpu.VMEM)(h.shape, h.dtype) for h in held]
        + [pltpu.SemaphoreType.DMA((8,))],
        (place, *held), 60,
    )
    before = lax.ppermute(up, AXES, forward)
    after = lax.ppermute(down, AXES, [(j, i) for i, j in forward])
    partial = ((leaves, 128, 256), F32)
    slots = [pltpu.VMEM((256, 256), F32)] * DEPTH + [pltpu.VMEM((4, 256, 256), BF)] * DEPTH
    (near0,) = call(
        lambda *refs: own_kernel(CUTS[0], *refs),
        [partial], [VMEM, anywhere], [pltpu.VMEM((leaves, 256, 32), BF), pltpu.VMEM((leaves, 64, 256), BF)] + slots,
        (packed, mine), 24,
    )
    mine = gathered(mine, 16, near0)
    near1, wa, c2 = call(
        lambda *refs: first_kernel(CUTS[0], CUTS[1], *refs),
        [partial, ((total + 1, 256, 32), BF), ((total + 1, 64, 256), BF)],
        [SMEM] * 2 + [VMEM] * 3 + [anywhere], [rows] + slots,
        (order, limits, packed, before, after, mine), 24,
    )
    mine = gathered(mine, 4, near1)
    (near2,) = call(
        lambda *refs: next_kernel(CUTS[1], CUTS[2], *refs),
        [partial], [SMEM] * 2 + [VMEM] * 3 + [anywhere], slots, (order, limits, wa, c2, packed, mine), 24,
    )
    mine = gathered(mine, 1, near2)
    theirs = lax.ppermute(mine, "group", [(0, 1), (1, 0)])
    (near3,) = call(
        lambda *refs: next_kernel(CUTS[2], leaves * width, *refs),
        [partial], [SMEM] * 2 + [VMEM] * 3 + [anywhere], slots, (order, limits, wa, c2, packed, mine), 24,
    )
    out = ((leaves, 32, 256), F32)
    return call(
        far_kernel, [out, out], [SMEM] * 2 + [VMEM] * 11,
        [pltpu.VMEM((32, 1024), F32), pltpu.VMEM((1024, 128), F32)],
        (place, far_list, mine, theirs, skeleton, jnp.transpose(group_skeleton, (1, 0, 2)), dev_transfer[0],
         leaf_transfer, basis, near0, near1, near2, near3), 24,
    )


def solution(mesh):
    leaf = P(AXES, None, None)
    placed = (leaf, leaf, leaf, leaf, leaf, leaf, P(), P(AXES, None), P(AXES), P(AXES, None))
    return jax.shard_map(local, mesh=mesh, in_specs=placed, out_specs=(leaf, leaf), check_vma=False)
```

time: 115 us -> 79.2 us (0.69)
  the two profiles are of different devices: /device:TPU:8 before, /device:TPU:58 now
where the time goes in v2:
time: 79.2 us; the launch traced here: 78.3 us
  Pallas kernels  51.3 us (65%)
  starting transfers between devices  24.1 us (30%)
  local copies, waits for them, and re-layouts  1.99 us (3%)
  between operations  0.89 us (1%)
    pallas_call x9, Pallas kernels, call(): pl.pallas_call(kernel, out_shape=tuple((jax.ShapeDtypeStruct(shape, kind)...  51.3 us
    ppermute x9, starting transfers between devices, gathered(): lax.ppermute(block, 'dev', dev_shift(div, k))  18.1 us
    ppermute x1, starting transfers between devices, local(): before = lax.ppermute(up, AXES, forward)  3.4 us
    ppermute x1, starting transfers between devices, local(): after = lax.ppermute(down, AXES, [(j, i) for i, j in forward])  2.45 us
    unnamed x18, local copies, waits for them, and re-layouts  1.99 us
  transfers between devices with their start and end apart: 12, of which 0 were waited for; matrix products, arithmetic and copies ran while one was open for 0% of the time, Pallas kernels for 51%

profile of v2, /device:TPU:58, one launch (start us, length us, event | category | flops | bytes accessed | tf_op | source)
XLA Modules:
  0.0 78.3 jit_solution(11849465207767646382)
XLA Ops:
  0.6 5.7 %shard_map.113 = (f32[496,256]{1,0:T(8,128)}, f32[496,256]{1,0:T(8,128)}, bf16[16,128,256]{2,1,0:T(8,128)(2,1)}, s32[200]{0:T(256)}, s32[1]{0:T(128)}, /*index=5*/f32[40,128]{1,0:T(8,128)}) custom-call(s32[1]{0:T(128)} %bitcast.refs_0_.place, f32[3,16,256]{2,1,0:T(8,128)} %bitcast.10, f32[16,32,256]{2,1,0:T(8,128)} %refs_2_.1, s32[16,12]{1,0:T(8,128)} %refs_3_.1, ...), custom_call_target="tpu_custom_call" | custom-call | flops 1000 | bytes 1000 | tf_op jit(solution)/shard_map/pallas_call | solution.py:306
  6.3 3.4 %collective-permute-start.6 = (f32[496,256]{1,0:T(8,128)}, f32[496,256]{1,0:T(8,128)S(1)}, u32[]{:S(2)}, u32[]{:S(2)}) collective-permute-start(f32[496,256]{1,0:T(8,128)} %get-tuple-element.15), channel_id=1, source_target_pairs={{0,1},{1,2},{2,3},{3,4},{4,5},{5,6},{6,7},{7,8},{8,9},{9,10},{10,1... | collective-permute-start | bytes 1523720 | tf_op jit(solution)/shard_map/ppermute | solution.py:336
  9.7 2.4 %collective-permute-start.7 = (f32[496,256]{1,0:T(8,128)}, f32[496,256]{1,0:T(8,128)S(1)}, u32[]{:S(2)}, u32[]{:S(2)}) collective-permute-start(f32[496,256]{1,0:T(8,128)} %get-tuple-element.16), channel_id=1, source_target_pairs={{1,0},{2,1},{3,2},{4,3},{5,4},{6,5},{7,6},{8,7},{9,8},{10,9},{11,1... | collective-permute-start | bytes 1523720 | tf_op jit(solution)/shard_map/ppermute | solution.py:337
  12.2 0.8 %collective-permute-start.2 = (f32[40,128]{1,0:T(8,128)}, f32[40,128]{1,0:T(8,128)S(1)}, u32[]{:S(2)}, u32[]{:S(2)}) collective-permute-start(f32[40,128]{1,0:T(8,128)} %get-tuple-element.11.refs_1_.one), channel_id=1, source_target_pairs={{0,48},{1,49},{2,50},{3,51},{4,52},{5,53},{6,54},{7,55},{8,56},{9,... | collective-permute-start | bytes 61448 | tf_op jit(solution)/shard_map/ppermute | solution.py:318
  13.0 0.9 %collective-permute-start.1 = (f32[40,128]{1,0:T(8,128)}, f32[40,128]{1,0:T(8,128)S(1)}, u32[]{:S(2)}, u32[]{:S(2)}) collective-permute-start(f32[40,128]{1,0:T(8,128)} %get-tuple-element.11.refs_1_.one), channel_id=1, source_target_pairs={{0,32},{1,33},{2,34},{3,35},{4,36},{5,37},{6,38},{7,39},{8,40},{9,... | collective-permute-start | bytes 61448 | tf_op jit(solution)/shard_map/ppermute | solution.py:318
  13.9 2.2 %collective-permute-start = (f32[40,128]{1,0:T(8,128)}, f32[40,128]{1,0:T(8,128)S(1)}, u32[]{:S(2)}, u32[]{:S(2)}) collective-permute-start(f32[40,128]{1,0:T(8,128)} %get-tuple-element.11.refs_1_.one), channel_id=1, source_target_pairs={{0,16},{1,17},{2,18},{3,19},{4,20},{5,21},{6,22},{7,23},{8,24},{9,... | collective-permute-start | bytes 61448 | tf_op jit(solution)/shard_map/ppermute | solution.py:318
  16.1 1.2 %copy-done = bf16[16,128,256]{2,1,0:T(8,128)(2,1)S(1)} copy-done((bf16[16,128,256]{2,1,0:T(8,128)(2,1)S(1)}, bf16[16,128,256]{2,1,0:T(8,128)(2,1)}, u32[]{:S(2)}) %copy-start) | copy-done | bytes 1048600
  17.3 0.7 copy-done.4
  18.1 3.4 %shard_map.114.earlier.near0 = f32[16,128,256]{2,1,0:T(8,128)S(1)} custom-call(bf16[16,128,256]{2,1,0:T(8,128)(2,1)S(1)} %copy-done, f32[40,128]{1,0:T(8,128)S(1)} %copy-done.4), custom_call_target="tpu_custom_call" | custom-call | flops 1000 | bytes 1000 | tf_op jit(solution)/shard_map/pallas_call | solution.py:306
  21.4 0.0 collective-permute-done.2.four
  21.5 0.0 collective-permute-done.two
  21.5 0.2 collective-permute-start.5
  21.7 3.3 %collective-permute-start.4 = (f32[112,128]{1,0:T(8,128)S(1)}, f32[112,128]{1,0:T(8,128)S(1)}, u32[]{:S(2)}, u32[]{:S(2)}) collective-permute-start(f32[112,128]{1,0:T(8,128)S(1)} %shard_map.115.refs_5_.one), channel_id=1, source_target_pairs={{0,8},{1,9},{2,10},{3,11},{4,12},{5,13},{6,14},{7,15},{8,0},{9,1},... | collective-permute-start | bytes 172040 | tf_op jit(solution)/shard_map/ppermute | solution.py:318
  24.9 2.2 %collective-permute-start.3 = (f32[112,128]{1,0:T(8,128)S(1)}, f32[112,128]{1,0:T(8,128)S(1)}, u32[]{:S(2)}, u32[]{:S(2)}) collective-permute-start(f32[112,128]{1,0:T(8,128)S(1)} %shard_map.115.refs_5_.one), channel_id=1, source_target_pairs={{0,4},{1,5},{2,6},{3,7},{4,8},{5,9},{6,10},{7,11},{8,12},{9,13},{1... | collective-permute-start | bytes 172040 | tf_op jit(solution)/shard_map/ppermute | solution.py:318
  27.2 0.0 collective-permute-done.6.refs_3_
  27.2 8.6 %shard_map.116 = (f32[16,128,256]{2,1,0:T(8,128)S(1)}, bf16[45,256,32]{2,1,0:T(8,128)(2,1)S(1)}, bf16[45,64,256]{2,1,0:T(8,128)(2,1)S(1)}) custom-call(s32[200]{0:T(256)S(1)} %copy-done.5, s32[1]{0:T(128)} %get-tuple-element.14.refs_1_, bf16[16,128,256]{2,1,0:T(8,128)(2,1)S(1)} %copy-done, f32[496,256]{1,0:T(8,128)S(1)} %collective-permute-done.6.refs_3_, ...), custom_call_target="tpu_custom_call" | custom-call | flops 1000 | bytes 1000 | tf_op jit(solution)/shard_map/pallas_call | solution.py:306
  35.8 0.0 collective-permute-done.5.four
  35.9 2.9 %collective-permute-start.10 = (f32[400,128]{1,0:T(8,128)S(1)}, f32[400,128]{1,0:T(8,128)S(1)}, u32[]{:S(2)}, u32[]{:S(2)}) collective-permute-start(f32[400,128]{1,0:T(8,128)S(1)} %shard_map.117.refs_5_.one), channel_id=1, source_target_pairs={{0,3},{1,0},{2,1},{3,2},{4,7},{5,4},{6,5},{7,6},{8,11},{9,8},{10,9... | collective-permute-start | bytes 614408 | tf_op jit(solution)/shard_map/ppermute | solution.py:318
  38.8 3.1 %collective-permute-start.9 = (f32[400,128]{1,0:T(8,128)S(1)}, f32[400,128]{1,0:T(8,128)S(1)}, u32[]{:S(2)}, u32[]{:S(2)}) collective-permute-start(f32[400,128]{1,0:T(8,128)S(1)} %shard_map.117.refs_5_.one), channel_id=1, source_target_pairs={{0,2},{1,3},{2,0},{3,1},{4,6},{5,7},{6,4},{7,5},{8,10},{9,11},{10,... | collective-permute-start | bytes 614408 | tf_op jit(solution)/shard_map/ppermute | solution.py:318
  41.8 2.5 %collective-permute-start.8 = (f32[400,128]{1,0:T(8,128)S(1)}, f32[400,128]{1,0:T(8,128)S(1)}, u32[]{:S(2)}, u32[]{:S(2)}) collective-permute-start(f32[400,128]{1,0:T(8,128)S(1)} %shard_map.117.refs_5_.one), channel_id=1, source_target_pairs={{0,1},{1,2},{2,3},{3,0},{4,5},{5,6},{6,7},{7,4},{8,9},{9,10},{10,1... | collective-permute-start | bytes 614408 | tf_op jit(solution)/shard_map/ppermute | solution.py:318
  44.4 9.9 %shard_map.118.earlier.near2 = f32[16,128,256]{2,1,0:T(8,128)S(1)} custom-call(s32[200]{0:T(256)S(1)} %copy-done.5, s32[1]{0:T(128)} %get-tuple-element.14.refs_1_, bf16[45,256,32]{2,1,0:T(8,128)(2,1)S(1)} %get-tuple-element.18.refs_2_, bf16[45,64,256]{2,1,0:T(8,128)(2,1)S(1)} %get-tuple-element.19.refs_3_, bf16[16,128,256]{2,1,0:T(8,128)(2,1)S(1)} %copy-done, ...), custom_call_target="tpu_custom_call" | custom-call | flops 1000 | bytes 1000 | tf_op jit(solution)/shard_map/pallas_call | solution.py:306
  54.3 0.0 collective-permute-done.10.four
  54.3 0.1 shard_map.119.refs_5_.mine
  54.4 0.0 copy-start.1
  54.4 0.0 copy-start.2
  54.4 0.0 copy-start.3
  54.4 0.0 copy-start.6
  54.5 0.0 copy-start.7
  54.5 0.0 copy-start.8
  54.5 0.1 collective-permute-start.11
  54.6 18.0 %shard_map.120.near3 = f32[16,128,256]{2,1,0:T(8,128)S(1)} custom-call(s32[200]{0:T(256)S(1)} %copy-done.5, s32[1]{0:T(128)} %get-tuple-element.14.refs_1_, bf16[45,256,32]{2,1,0:T(8,128)(2,1)S(1)} %get-tuple-element.18.refs_2_, bf16[45,64,256]{2,1,0:T(8,128)(2,1)S(1)} %get-tuple-element.19.refs_3_, bf16[16,128,256]{2,1,0:T(8,128)(2,1)S(1)} %copy-done, ...), custom_call_target="tpu_custom_call" | custom-call | flops 1000 | bytes 1000 | tf_op jit(solution)/shard_map/pallas_call | solution.py:306
  72.7 5.6 %shard_map.121 = (f32[16,32,256]{2,1,0:T(8,128)}, f32[16,32,256]{2,1,0:T(8,128)}) custom-call(s32[1]{0:T(128)} %bitcast.refs_0_.place, s32[1,16]{1,0:T(1,128)S(1)} %copy-done.8, f32[1552,128]{1,0:T(8,128)S(1)} %shard_map.119.refs_5_.mine, f32[1552,128]{1,0:T(8,128)S(1)} %collective-permute-done.11.theirs, f32[3,1,64]{2,1,0:T(1,128)S(1)} %bitcast.8, ...), custom_call_target="tpu_custom_call" | custom-call | flops 1000 | bytes 1000 | tf_op jit(solution)/shard_map/pallas_call | solution.py:306
  (19 shorter events, 0.1 us)
Async XLA Ops:
  6.3 20.9 %collective-permute-start.6 = (f32[496,256]{1,0:T(8,128)}, f32[496,256]{1,0:T(8,128)S(1)}, u32[]{:S(2)}, u32[]{:S(2)}) collective-permute-start(f32[496,256]{1,0:T(8,128)} %get-tuple-element.15), channel_id=1, source_target_pairs={{0,1},{1,2},{2,3},{3,4},{4,5},{5,6},{6,7},{7,8},{8,9},{9,10},{10,1... | collective-permute-start | bytes 1523720 | tf_op jit(solution)/shard_map/ppermute | solution.py:336
  9.7 17.5 %collective-permute-start.7 = (f32[496,256]{1,0:T(8,128)}, f32[496,256]{1,0:T(8,128)S(1)}, u32[]{:S(2)}, u32[]{:S(2)}) collective-permute-start(f32[496,256]{1,0:T(8,128)} %get-tuple-element.16), channel_id=1, source_target_pairs={{1,0},{2,1},{3,2},{4,3},{5,4},{6,5},{7,6},{8,7},{9,8},{10,9},{11,1... | collective-permute-start | bytes 1523720 | tf_op jit(solution)/shard_map/ppermute | solution.py:337
  12.2 9.3 %collective-permute-start.2 = (f32[40,128]{1,0:T(8,128)}, f32[40,128]{1,0:T(8,128)S(1)}, u32[]{:S(2)}, u32[]{:S(2)}) collective-permute-start(f32[40,128]{1,0:T(8,128)} %get-tuple-element.11.refs_1_.one), channel_id=1, source_target_pairs={{0,48},{1,49},{2,50},{3,51},{4,52},{5,53},{6,54},{7,55},{8,56},{9,... | collective-permute-start | bytes 61448 | tf_op jit(solution)/shard_map/ppermute | solution.py:318
  13.0 8.5 %collective-permute-start.1 = (f32[40,128]{1,0:T(8,128)}, f32[40,128]{1,0:T(8,128)S(1)}, u32[]{:S(2)}, u32[]{:S(2)}) collective-permute-start(f32[40,128]{1,0:T(8,128)} %get-tuple-element.11.refs_1_.one), channel_id=1, source_target_pairs={{0,32},{1,33},{2,34},{3,35},{4,36},{5,37},{6,38},{7,39},{8,40},{9,... | collective-permute-start | bytes 61448 | tf_op jit(solution)/shard_map/ppermute | solution.py:318
  13.9 7.6 %collective-permute-start = (f32[40,128]{1,0:T(8,128)}, f32[40,128]{1,0:T(8,128)S(1)}, u32[]{:S(2)}, u32[]{:S(2)}) collective-permute-start(f32[40,128]{1,0:T(8,128)} %get-tuple-element.11.refs_1_.one), channel_id=1, source_target_pairs={{0,16},{1,17},{2,18},{3,19},{4,20},{5,21},{6,22},{7,23},{8,24},{9,... | collective-permute-start | bytes 61448 | tf_op jit(solution)/shard_map/ppermute | solution.py:318
  16.1 1.2 %copy-start = (bf16[16,128,256]{2,1,0:T(8,128)(2,1)S(1)}, bf16[16,128,256]{2,1,0:T(8,128)(2,1)}, u32[]{:S(2)}) copy-start(bf16[16,128,256]{2,1,0:T(8,128)(2,1)} %get-tuple-element.12.refs_0_.refs_2_.refs_4_) | copy-start | bytes 3145732
  17.3 0.7 copy-start.4
  18.1 9.1 %copy-start.5 = (s32[200]{0:T(256)S(1)}, s32[200]{0:T(256)}, u32[]{:S(2)}) copy-start(s32[200]{0:T(256)} %get-tuple-element.13.refs_0_) | copy-start | bytes 2404
  21.5 14.3 %collective-permute-start.5 = (f32[112,128]{1,0:T(8,128)S(1)}, f32[112,128]{1,0:T(8,128)S(1)}, u32[]{:S(2)}, u32[]{:S(2)}) collective-permute-start(f32[112,128]{1,0:T(8,128)S(1)} %shard_map.115.refs_5_.one), channel_id=1, source_target_pairs={{0,12},{1,13},{2,14},{3,15},{4,0},{5,1},{6,2},{7,3},{8,4},{9,5},{1... | collective-permute-start | bytes 172040 | tf_op jit(solution)/shard_map/ppermute | solution.py:318
  21.7 14.1 %collective-permute-start.4 = (f32[112,128]{1,0:T(8,128)S(1)}, f32[112,128]{1,0:T(8,128)S(1)}, u32[]{:S(2)}, u32[]{:S(2)}) collective-permute-start(f32[112,128]{1,0:T(8,128)S(1)} %shard_map.115.refs_5_.one), channel_id=1, source_target_pairs={{0,8},{1,9},{2,10},{3,11},{4,12},{5,13},{6,14},{7,15},{8,0},{9,1},... | collective-permute-start | bytes 172040 | tf_op jit(solution)/shard_map/ppermute | solution.py:318
  24.9 10.9 %collective-permute-start.3 = (f32[112,128]{1,0:T(8,128)S(1)}, f32[112,128]{1,0:T(8,128)S(1)}, u32[]{:S(2)}, u32[]{:S(2)}) collective-permute-start(f32[112,128]{1,0:T(8,128)S(1)} %shard_map.115.refs_5_.one), channel_id=1, source_target_pairs={{0,4},{1,5},{2,6},{3,7},{4,8},{5,9},{6,10},{7,11},{8,12},{9,13},{1... | collective-permute-start | bytes 172040 | tf_op jit(solution)/shard_map/ppermute | solution.py:318
  35.9 18.5 %collective-permute-start.10 = (f32[400,128]{1,0:T(8,128)S(1)}, f32[400,128]{1,0:T(8,128)S(1)}, u32[]{:S(2)}, u32[]{:S(2)}) collective-permute-start(f32[400,128]{1,0:T(8,128)S(1)} %shard_map.117.refs_5_.one), channel_id=1, source_target_pairs={{0,3},{1,0},{2,1},{3,2},{4,7},{5,4},{6,5},{7,6},{8,11},{9,8},{10,9... | collective-permute-start | bytes 614408 | tf_op jit(solution)/shard_map/ppermute | solution.py:318
  38.8 15.5 %collective-permute-start.9 = (f32[400,128]{1,0:T(8,128)S(1)}, f32[400,128]{1,0:T(8,128)S(1)}, u32[]{:S(2)}, u32[]{:S(2)}) collective-permute-start(f32[400,128]{1,0:T(8,128)S(1)} %shard_map.117.refs_5_.one), channel_id=1, source_target_pairs={{0,2},{1,3},{2,0},{3,1},{4,6},{5,7},{6,4},{7,5},{8,10},{9,11},{10,... | collective-permute-start | bytes 614408 | tf_op jit(solution)/shard_map/ppermute | solution.py:318
  41.8 12.5 %collective-permute-start.8 = (f32[400,128]{1,0:T(8,128)S(1)}, f32[400,128]{1,0:T(8,128)S(1)}, u32[]{:S(2)}, u32[]{:S(2)}) collective-permute-start(f32[400,128]{1,0:T(8,128)S(1)} %shard_map.117.refs_5_.one), channel_id=1, source_target_pairs={{0,1},{1,2},{2,3},{3,0},{4,5},{5,6},{6,7},{7,4},{8,9},{9,10},{10,1... | collective-permute-start | bytes 614408 | tf_op jit(solution)/shard_map/ppermute | solution.py:318
  54.4 18.2 %copy-start.1 = (f32[16,64,256]{2,1,0:T(8,128)S(1)}, f32[16,64,256]{2,1,0:T(8,128)}, u32[]{:S(2)}) copy-start(f32[16,64,256]{2,1,0:T(8,128)} %basis.1) | copy-start | bytes 3145732
  54.4 18.2 %copy-start.2 = (f32[16,64,64]{2,1,0:T(8,128)S(1)}, f32[16,64,64]{2,1,0:T(8,128)}, u32[]{:S(2)}) copy-start(f32[16,64,64]{2,1,0:T(8,128)} %leaf_transfer.1) | copy-start | bytes 786436
  54.4 18.2 %copy-start.3 = (f32[1,64,64]{2,1,0:T(8,128)S(1)}, f32[1,64,64]{2,1,0:T(8,128)}, u32[]{:S(2)}) copy-start(f32[1,64,64]{2,1,0:T(8,128)} %param.15) | copy-start | bytes 49156
  54.4 18.2 %copy-start.6 = (f32[1,3,64]{2,0,1:T(1,128)S(1)}, f32[1,3,64]{2,0,1:T(1,128)}, u32[]{:S(2)}) copy-start(f32[1,3,64]{2,0,1:T(1,128)} %param.14) | copy-start | bytes 2308
  54.5 18.2 %copy-start.7 = (f32[2,3,64]{2,0,1:T(2,128)S(1)}, f32[2,3,64]{2,0,1:T(2,128)}, u32[]{:S(2)}) copy-start(f32[2,3,64]{2,0,1:T(2,128)} %param.16) | copy-start | bytes 4612
  54.5 18.2 %copy-start.8 = (s32[1,16]{1,0:T(1,128)S(1)}, s32[1,16]{1,0:T(1,128)}, u32[]{:S(2)}) copy-start(s32[1,16]{1,0:T(1,128)} %far_list.1) | copy-start | bytes 196
  54.5 18.1 %collective-permute-start.11 = (f32[1552,128]{1,0:T(8,128)S(1)}, f32[1552,128]{1,0:T(8,128)S(1)}, u32[]{:S(2)}, u32[]{:S(2)}) collective-permute-start(f32[1552,128]{1,0:T(8,128)S(1)} %shard_map.119.refs_5_.mine), channel_id=1, source_target_pairs={{0,64},{64,0},{1,65},{65,1},{2,66},{66,2},{3,67},{67,3},{4,68},{68... | collective-permute-start | bytes 2383880 | tf_op jit(solution)/shard_map/ppermute | solution.py:358

commit v3 on v2

--- a/solution.py
+++ b/solution.py
@@ -20,8 +20,11 @@
 VALUE_SCALE = LN2
 SLOPE_SCALE = LN2 * LN2 / LENGTH
 NODE_ROWS = 24
-DEPTH = 4
-CUTS = (4, 12, 24)
+LIFT = 6
+CHARGE_LIFT = 14
+F8 = jnp.float8_e5m2
+DEPTH = 8
+CUTS = (2, 6, 12)
 MIB = 2**20
 AXES = ("group", "dev")
 
@@ -46,9 +49,9 @@
     return one, two, rest - two
 
 
-def matern_terms(x):
+def matern_terms(x, lift=0):
     t = x * lax.rsqrt(x)
-    e = jnp.exp2(-t)
+    e = jnp.exp2(lift - t)
     return (t + LOG2E) * e, x * e
 
 
@@ -87,15 +90,21 @@
         wa[at, 128 * h : 128 * h + 128, :] = jnp.transpose(part).astype(BF)
 
 
-def node_block(charges, basis, leaf_transfer, dev_transfer, skeleton, out):
-    total = jnp.zeros((32, 64), F32)
-    for l in range(charges.shape[0]):
-        leaf = lax.dot_general(
-            charges[l], basis[l], (((1,), (1,)), ((), ())), precision=HIGH, preferred_element_type=F32
-        )
-        total += lax.dot_general(
-            leaf, leaf_transfer[l], (((1,), (1,)), ((), ())), precision=HIGH, preferred_element_type=F32
-        )
+def dot_t(a, b):
+    return lax.dot_general(a, b, (((1,), (1,)), ((), ())), preferred_element_type=F32)
+
+
+def node_block(packed, basis, leaf_transfer, dev_transfer, skeleton, product, out):
+    high, low = jnp.zeros((64, 64), F32), jnp.zeros((32, 64), F32)
+    for l in range(basis.shape[0]):
+        left, left_low = split2(leaf_transfer[l])
+        right, right_low = split2(basis[l])
+        both = dot(jnp.concatenate([left, left_low], axis=0), right)
+        one, two = split2(both[:64] + both[64:] + dot(left, right_low))
+        product[l, 0:64, :], product[l, 64:128, :] = one, two
+        high += dot_t(packed[l, 64:128, :], one)
+        low += dot_t(packed[l, 64:96, :], two)
+    total = high[:32] + high[32:] + low
     image = lax.dot_general(
         total, dev_transfer[...], (((1,), (1,)), ((), ())), precision=HIGH, preferred_element_type=F32
     )
@@ -107,7 +116,7 @@
 
 
 def prepare_kernel(reach, place, points_in, charges_in, neighbours_in, counts_in, basis_in, leaf_transfer_in, dev_transfer_in,
-                   skeleton_in, up, down, packed, order, limits, block,
+                   skeleton_in, up, down, packed, order, limits, block, product,
                    rows, points, charges, neighbours, counts, basis, leaf_transfer, dev_transfer, skeleton, sems):
     leaves, width = neighbours.shape
     sources = (points_in, charges_in, neighbours_in, counts_in, basis_in, leaf_transfer_in, dev_transfer_in, skeleton_in)
@@ -151,32 +160,32 @@
     limits[0] = (ends + DEPTH - 1) // DEPTH
     for load in loads[4:]:
         load.wait()
-    node_block(charges, basis, leaf_transfer, dev_transfer, skeleton, block)
+    node_block(packed, basis, leaf_transfer, dev_transfer, skeleton, product, block)
 
 
 def merge_kernel(one, two, three, four, earlier, out):
     del earlier
-    came = (one, two, three, four)
     count = one.shape[0] - 16
-    for i, ref in enumerate(came):
+    for i, ref in enumerate((one, two, three, four)):
         out[count * i : count * i + count, :] = ref[:count, :]
     out[4 * count :, :] = (one[count:, :] + two[count:, :]) + (three[count:, :] + four[count:, :])
 
 
-def near_pairs(lo, hi, order, wa, c2, ua, acc, slots):
-    xs, tiles = slots[:DEPTH], slots[DEPTH:]
+def near_pairs(lo, hi, order, wa, c2, c8, ua, acc, slots):
+    xs, highs, lows = slots[:DEPTH], slots[DEPTH : 2 * DEPTH], slots[2 * DEPTH :]
     acc[...] = jnp.zeros_like(acc)
-    tiles[DEPTH - 1][...] = jnp.zeros(tiles[0].shape, BF)
+    highs[DEPTH - 1][...] = jnp.zeros(highs[0].shape, BF)
+    lows[DEPTH - 1][...] = jnp.zeros(lows[0].shape, F8)
 
     def distances(i):
         pair = order[i]
         return dot(wa[pair % 64], ua[pair // 64])
 
-    def gather_up(i, tile):
+    def gather_up(i, b):
         pair = order[i]
-        c, target = c2[pair % 64], pair // 64
-        one, two = dot(c, tile[0]), dot(c[:32], tile[1])
-        three, four = dot(c, tile[2]), dot(c[:32], tile[3])
+        c, small, target = c2[pair % 64], c8[pair % 64], pair // 64
+        one, two = dot(c, highs[b][0]), dot(small, lows[b][0]) * 2.0**-CHARGE_LIFT
+        three, four = dot(c, highs[b][1]), dot(small, lows[b][1]) * 2.0**-CHARGE_LIFT
         acc[target, 0:32, :] += one[:32] + two
         acc[target, 32:64, :] += one[32:]
         acc[target, 64:96, :] += three[:32] + four
@@ -184,10 +193,11 @@
 
     def step(i, b):
         xs[(b + 1) % DEPTH][...] = distances(jnp.minimum(i + 1, DEPTH * hi - 1))
-        value, slope = matern_terms(xs[b][...])
-        tiles[b][0], tiles[b][1] = split2(value)
-        tiles[b][2], tiles[b][3] = split2(slope)
-        gather_up(jnp.maximum(i - 1, DEPTH * lo), tiles[(b - 1) % DEPTH])
+        for k, term in enumerate(matern_terms(xs[b][...], LIFT)):
+            high = term.astype(BF)
+            highs[b][k] = high
+            lows[b][k] = (term - high.astype(F32)).astype(F8)
+        gather_up(jnp.maximum(i - 1, DEPTH * lo), (b - 1) % DEPTH)
 
     def body(j, carry):
         for u in range(DEPTH):
@@ -198,13 +208,18 @@
     def _():
         xs[0][...] = distances(DEPTH * lo)
         lax.fori_loop(lo, hi, body, 0)
-        gather_up(DEPTH * hi - 1, tiles[DEPTH - 1])
-
-
-def unpack(packed, offset, wa, c2):
+        gather_up(DEPTH * hi - 1, DEPTH - 1)
+
+
+def small_charges(high):
+    return (high.astype(F32) * 2.0**CHARGE_LIFT).astype(F8)
+
+
+def unpack(packed, wa, c2, c8, offset):
     for l in range(packed.shape[0]):
         wa[offset + l] = jnp.transpose(packed[l, 0:32, :].astype(F32)).astype(BF)
         c2[offset + l] = packed[l, 64:128, :]
+        c8[offset + l] = small_charges(packed[l, 64:96, :])
 
 
 class Targets:
@@ -220,38 +235,40 @@
         return i * 65
 
 
-def own_kernel(end, packed, earlier, acc, wa, c2, *slots):
+def own_kernel(end, packed, earlier, acc, wa, c2, c8, *slots):
     del earlier
-    unpack(packed, 0, wa, c2)
-    near_pairs(0, end, Selves(), wa, c2, Targets(packed), acc, slots)
-
-
-def first_kernel(begin, end, order, limits, packed, before, after, earlier, acc, wa, c2, rows, *slots):
+    unpack(packed, wa, c2, c8, 0)
+    near_pairs(0, end, Selves(), wa, c2, c8, Targets(packed), acc, slots)
+
+
+def first_kernel(begin, end, order, limits, packed, before, after, earlier, acc, wa, c2, c8, rows, *slots):
     del earlier
     leaves, half = packed.shape[0], before.shape[0] // 35
     total = leaves + 2 * half
-    unpack(packed, half, wa, c2)
+    unpack(packed, wa, c2, c8, half)
     for ref, offset in ((before, 0), (after, half + leaves)):
         write_rows(rows, [ref[32 * half + 16 * c : 32 * half + 16 * c + half, :] for c in range(3)], True)
         for l in range(half):
             write_source(wa, offset + l, rows, l)
-            c2[offset + l, 0:32, :], c2[offset + l, 32:64, :] = split2(ref[32 * l : 32 * l + 32, :])
+            high, low = split2(ref[32 * l : 32 * l + 32, :])
+            c2[offset + l, 0:32, :], c2[offset + l, 32:64, :] = high, low
+            c8[offset + l] = small_charges(high)
     wa[total] = wa[half]
     c2[total] = jnp.zeros(c2.shape[1:], BF)
-    near_pairs(jnp.minimum(begin, limits[0]), jnp.minimum(end, limits[0]), order, wa, c2, Targets(packed), acc, slots)
-
-
-def next_kernel(begin, end, order, limits, wa, c2, packed, earlier, acc, *slots):
+    c8[total] = jnp.zeros(c8.shape[1:], F8)
+    near_pairs(jnp.minimum(begin, limits[0]), jnp.minimum(end, limits[0]), order, wa, c2, c8, Targets(packed), acc, slots)
+
+
+def next_kernel(begin, end, order, limits, wa, c2, c8, packed, earlier, acc, *slots):
     del earlier
-    near_pairs(jnp.minimum(begin, limits[0]), jnp.minimum(end, limits[0]), order, wa, c2, Targets(packed), acc, slots)
-
-
-def far_kernel(place, far_list, mine, theirs, own_skeleton, groups, dev_transfer, leaf_transfer, basis, near0, near1, near2, near3,
-               value_out, slope_out, coefs, kernels):
-    leaves = basis.shape[0]
+    near_pairs(jnp.minimum(begin, limits[0]), jnp.minimum(end, limits[0]), order, wa, c2, c8, Targets(packed), acc, slots)
+
+
+def far_kernel(place, far_list, mine, theirs, own_skeleton, groups, dev_transfer, product, *refs):
+    nears, (value_out, slope_out, coefs, kernels) = refs[:-4], refs[-4:]
+    leaves = product.shape[0]
     rank = place[0]
     group, node = rank // 64, rank % 64
-    x0, z0, y0 = node % 4, (node // 4) % 4, node // 16
 
     def pair_kernel(column, row):
         x = jnp.full((64, 64), X0, F32)
@@ -264,13 +281,15 @@
     own = jnp.concatenate([own_skeleton[c] for c in range(3)], axis=0)
     for j in range(far_list.shape[1]):
         s = far_list[0, j]
-        d = s % 64
-        jx, jz, jy = (x0 - d % 4 + 4) % 4, (z0 - (d // 4) % 4 + 4) % 4, (y0 - d // 16 + 4) % 4
-        row = pl.multiple_of(((jx * 4 + jz) * 4 + jy) * NODE_ROWS, 8)
+        x, z, y = node - s, node // 4 - s % 64 // 4, node // 16 - s % 64 // 16
+        row = pl.multiple_of(((x & 3) * 16 + (z & 3) * 4 + (y & 3)) * NODE_ROWS, 8)
         block = jnp.where(s // 64 == group, mine[pl.ds(row, NODE_ROWS), :], theirs[pl.ds(row, NODE_ROWS), :])
         coefs[:, 64 * j : 64 * j + 64] = jnp.concatenate([block[:16, :64], block[:16, 64:]], axis=0)
         kernels[64 * j : 64 * j + 64, :] = pair_kernel(jnp.transpose(block[16:24, :])[:64], own)
-    far = dot32(coefs[...], kernels[...])
+    coef, coef_low = split2(coefs[...])
+    kernel, kernel_low = split2(kernels[...])
+    both = dot(jnp.concatenate([coef, coef_low], axis=0), kernel)
+    far = both[:32] + both[32:] + dot(coef, kernel_low)
     other = theirs[theirs.shape[0] - 16 :, :]
     other = jnp.concatenate([other[:, :64], other[:, 64:]], axis=0)
     near_group, far_group = groups[:, pl.ds(group, 1), :][:, 0], groups[:, pl.ds(1 - group, 1), :][:, 0]
@@ -278,12 +297,14 @@
     top = dot32(other, pair_kernel(column, near_group))
     far = jnp.concatenate([far[:, :64], far[:, 64:]], axis=0)
     top = jnp.concatenate([top[:, :64], top[:, 64:]], axis=0)
-    local_dev = far + dot32(top, dev_transfer[...])
+    local_dev, local_low = split2(far + dot32(top, dev_transfer[...]))
+    local_both = jnp.concatenate([local_dev, local_low], axis=0)
     for l in range(leaves):
-        part = dot32(dot32(local_dev, leaf_transfer[l]), basis[l])
-        near = (near0[l] + near1[l]) + (near2[l] + near3[l])
-        value_out[l] = (near[0:32] + near[32:64]) * VALUE_SCALE + part[:32]
-        slope_out[l] = (near[64:96] + near[96:128]) * SLOPE_SCALE + part[32:]
+        both = dot(local_both, product[l, 0:64, :])
+        part = both[:64] + both[64:] + dot(local_dev, product[l, 64:128, :])
+        near = (nears[0][l] + nears[1][l]) + (nears[2][l] + nears[3][l])
+        value_out[l] = (near[0:32] + near[32:64]) * (VALUE_SCALE * 2.0**-LIFT) + part[:32]
+        slope_out[l] = (near[64:96] + near[96:128]) * (SLOPE_SCALE * 2.0**-LIFT) + part[32:]
 
 
 VMEM = pl.BlockSpec(memory_space=pltpu.VMEM)
@@ -315,7 +336,8 @@
 
     def gathered(block, div, earlier):
         rows = 4 * block.shape[0] - 48
-        came = [block] + [lax.ppermute(block, "dev", dev_shift(div, k)) for k in (1, 2, 3)]
+        came = [block] + [lax.ppermute(block, "dev", dev_shift(div, k)) for k in (1, 3, 2)]
+        came = [came[0], came[1], came[3], came[2]]
         return call(merge_kernel, [((rows, 128), F32)], [VMEM] * 4 + [anywhere], [], (*came, earlier), 8)[0]
 
     points = jnp.transpose(points, (1, 0, 2))
@@ -324,10 +346,10 @@
     strip = ((REACH * 32 + 48, 256), F32)
     rows = pltpu.VMEM((leaves * 64, 128), F32)
     held = (points, charges, neighbours, counts, basis, leaf_transfer, dev_transfer[0], skeleton)
-    up, down, packed, order, limits, mine = call(
+    up, down, packed, order, limits, mine, product = call(
         lambda *refs: prepare_kernel(REACH, *refs),
         [strip, strip, ((leaves, 128, 256), BF),
-         ((leaves * width + 2 * DEPTH,), jnp.int32), ((1,), jnp.int32), ((40, 128), F32)],
+         ((leaves * width + 2 * DEPTH,), jnp.int32), ((1,), jnp.int32), ((40, 128), F32), ((leaves, 128, 256), BF)],
         [SMEM] + [pl.BlockSpec(memory_space=pltpu.HBM)] * 8,
         [rows] + [(pltpu.SMEM if h.dtype == jnp.int32 else pltpu.VMEM)(h.shape, h.dtype) for h in held]
         + [pltpu.SemaphoreType.DMA((8,))],
@@ -336,36 +358,38 @@
     before = lax.ppermute(up, AXES, forward)
     after = lax.ppermute(down, AXES, [(j, i) for i, j in forward])
     partial = ((leaves, 128, 256), F32)
-    slots = [pltpu.VMEM((256, 256), F32)] * DEPTH + [pltpu.VMEM((4, 256, 256), BF)] * DEPTH
+    slots = [pltpu.VMEM((256, 256), F32)] * DEPTH + [pltpu.VMEM((2, 256, 256), BF)] * DEPTH
+    slots += [pltpu.VMEM((2, 256, 256), F8)] * DEPTH
+    sources = [((leaves, 256, 32), BF), ((leaves, 64, 256), BF), ((leaves, 32, 256), F8)]
     (near0,) = call(
         lambda *refs: own_kernel(CUTS[0], *refs),
-        [partial], [VMEM, anywhere], [pltpu.VMEM((leaves, 256, 32), BF), pltpu.VMEM((leaves, 64, 256), BF)] + slots,
-        (packed, mine), 24,
+        [partial], [VMEM, anywhere], [pltpu.VMEM(*source) for source in sources] + slots, (packed, mine), 24,
     )
     mine = gathered(mine, 16, near0)
-    near1, wa, c2 = call(
+    near1, *held = call(
         lambda *refs: first_kernel(CUTS[0], CUTS[1], *refs),
-        [partial, ((total + 1, 256, 32), BF), ((total + 1, 64, 256), BF)],
+        [partial] + [((total + 1, *shape[1:]), kind) for shape, kind in sources],
         [SMEM] * 2 + [VMEM] * 3 + [anywhere], [rows] + slots,
         (order, limits, packed, before, after, mine), 24,
     )
     mine = gathered(mine, 4, near1)
     (near2,) = call(
         lambda *refs: next_kernel(CUTS[1], CUTS[2], *refs),
-        [partial], [SMEM] * 2 + [VMEM] * 3 + [anywhere], slots, (order, limits, wa, c2, packed, mine), 24,
+        [partial], [SMEM] * 2 + [VMEM] * 4 + [anywhere], slots, (order, limits, *held, packed, mine), 24,
     )
     mine = gathered(mine, 1, near2)
     theirs = lax.ppermute(mine, "group", [(0, 1), (1, 0)])
     (near3,) = call(
-        lambda *refs: next_kernel(CUTS[2], leaves * width, *refs),
-        [partial], [SMEM] * 2 + [VMEM] * 3 + [anywhere], slots, (order, limits, wa, c2, packed, mine), 24,
-    )
+        lambda *refs: next_kernel(CUTS[2], leaves * width // DEPTH, *refs),
+        [partial], [SMEM] * 2 + [VMEM] * 4 + [anywhere], slots, (order, limits, *held, packed, mine), 24,
+    )
+    nears = (near0, near1, near2, near3)
     out = ((leaves, 32, 256), F32)
     return call(
-        far_kernel, [out, out], [SMEM] * 2 + [VMEM] * 11,
+        far_kernel, [out, out], [SMEM] * 2 + [VMEM] * (6 + len(nears)),
         [pltpu.VMEM((32, 1024), F32), pltpu.VMEM((1024, 128), F32)],
         (place, far_list, mine, theirs, skeleton, jnp.transpose(group_skeleton, (1, 0, 2)), dev_transfer[0],
-         leaf_transfer, basis, near0, near1, near2, near3), 24,
+         product, *nears), 24,
     )
 
 

time: 79.2 us -> 75.4 us (0.952)
  the two profiles are of different devices: /device:TPU:58 before, /device:TPU:90 now
where the time goes in v3:
time: 75.4 us; the launch traced here: 74.4 us
  Pallas kernels  46.4 us (62%)
  starting transfers between devices  25 us (33%)
  local copies, waits for them, and re-layouts  1.98 us (3%)
  between operations  0.9 us (1%)
    pallas_call x9, Pallas kernels, call(): pl.pallas_call(kernel, out_shape=tuple((jax.ShapeDtypeStruct(shape, kind)...  46.4 us
    ppermute x9, starting transfers between devices, gathered(): lax.ppermute(block, 'dev', dev_shift(div, k))  18.9 us
    ppermute x1, starting transfers between devices, local(): before = lax.ppermute(up, AXES, forward)  3.39 us
    ppermute x1, starting transfers between devices, local(): after = lax.ppermute(down, AXES, [(j, i) for i, j in forward])  2.45 us
    unnamed x16, local copies, waits for them, and re-layouts  1.98 us
  transfers between devices with their start and end apart: 12, of which 0 were waited for; matrix products, arithmetic and copies ran while one was open for 0% of the time, Pallas kernels for 49%

profile of v3, /device:TPU:90, one launch (start us, length us, event | category | flops | bytes accessed | tf_op | source)
XLA Modules:
  0.0 74.4 jit_solution(11298371459466462219)
XLA Ops:
  0.6 5.4 %shard_map.113 = (f32[496,256]{1,0:T(8,128)}, f32[496,256]{1,0:T(8,128)}, bf16[16,128,256]{2,1,0:T(8,128)(2,1)}, s32[208]{0:T(256)}, s32[1]{0:T(128)}, /*index=5*/f32[40,128]{1,0:T(8,128)}, bf16[16,128,256]{2,1,0:T(8,128)(2,1)}) custom-call(s32[1]{0:T(128)} %bitcast.refs_0_.place, f32[3,16,256]{2,1,0:T(8,128)} %bitcast.10, f32[16,32,256]{2,1,0:T(8,128)} %refs_2_.1, ...), custom_call_target="tpu_custom_call" | custom-call | flops 1000 | bytes 1000 | tf_op jit(solution)/shard_map/pallas_call | solution.py:327
  6.1 3.4 %collective-permute-start.6 = (f32[496,256]{1,0:T(8,128)}, f32[496,256]{1,0:T(8,128)S(1)}, u32[]{:S(2)}, u32[]{:S(2)}) collective-permute-start(f32[496,256]{1,0:T(8,128)} %get-tuple-element.17), channel_id=1, source_target_pairs={{0,1},{1,2},{2,3},{3,4},{4,5},{5,6},{6,7},{7,8},{8,9},{9,10},{10,1... | collective-permute-start | bytes 1523720 | tf_op jit(solution)/shard_map/ppermute | solution.py:358
  9.5 2.4 %collective-permute-start.7 = (f32[496,256]{1,0:T(8,128)}, f32[496,256]{1,0:T(8,128)S(1)}, u32[]{:S(2)}, u32[]{:S(2)}) collective-permute-start(f32[496,256]{1,0:T(8,128)} %get-tuple-element.18), channel_id=1, source_target_pairs={{1,0},{2,1},{3,2},{4,3},{5,4},{6,5},{7,6},{8,7},{9,8},{10,9},{11,1... | collective-permute-start | bytes 1523720 | tf_op jit(solution)/shard_map/ppermute | solution.py:359
  11.9 0.8 %collective-permute-start.2 = (f32[40,128]{1,0:T(8,128)}, f32[40,128]{1,0:T(8,128)S(1)}, u32[]{:S(2)}, u32[]{:S(2)}) collective-permute-start(f32[40,128]{1,0:T(8,128)} %get-tuple-element.13.refs_1_.one), channel_id=1, source_target_pairs={{0,48},{1,49},{2,50},{3,51},{4,52},{5,53},{6,54},{7,55},{8,56},{9,... | collective-permute-start | bytes 61448 | tf_op jit(solution)/shard_map/ppermute | solution.py:339
  12.7 0.9 %collective-permute-start.1 = (f32[40,128]{1,0:T(8,128)}, f32[40,128]{1,0:T(8,128)S(1)}, u32[]{:S(2)}, u32[]{:S(2)}) collective-permute-start(f32[40,128]{1,0:T(8,128)} %get-tuple-element.13.refs_1_.one), channel_id=1, source_target_pairs={{0,32},{1,33},{2,34},{3,35},{4,36},{5,37},{6,38},{7,39},{8,40},{9,... | collective-permute-start | bytes 61448 | tf_op jit(solution)/shard_map/ppermute | solution.py:339
  13.7 2.2 %collective-permute-start = (f32[40,128]{1,0:T(8,128)}, f32[40,128]{1,0:T(8,128)S(1)}, u32[]{:S(2)}, u32[]{:S(2)}) collective-permute-start(f32[40,128]{1,0:T(8,128)} %get-tuple-element.13.refs_1_.one), channel_id=1, source_target_pairs={{0,16},{1,17},{2,18},{3,19},{4,20},{5,21},{6,22},{7,23},{8,24},{9,... | collective-permute-start | bytes 61448 | tf_op jit(solution)/shard_map/ppermute | solution.py:339
  15.9 1.2 %copy-done = bf16[16,128,256]{2,1,0:T(8,128)(2,1)S(1)} copy-done((bf16[16,128,256]{2,1,0:T(8,128)(2,1)S(1)}, bf16[16,128,256]{2,1,0:T(8,128)(2,1)}, u32[]{:S(2)}) %copy-start) | copy-done | bytes 1048600
  17.1 0.7 copy-done.3
  17.8 3.2 %shard_map.114.earlier.refs_0_ = f32[16,128,256]{2,1,0:T(8,128)S(1)} custom-call(bf16[16,128,256]{2,1,0:T(8,128)(2,1)S(1)} %copy-done, f32[40,128]{1,0:T(8,128)S(1)} %copy-done.3), custom_call_target="tpu_custom_call" | custom-call | flops 1000 | bytes 1000 | tf_op jit(solution)/shard_map/pallas_call | solution.py:327
  21.0 0.0 collective-permute-done.2.four
  21.0 0.0 collective-permute-done.1.three
  21.0 0.0 collective-permute-done.two
  21.1 0.2 collective-permute-start.5
  21.2 3.6 %collective-permute-start.4 = (f32[112,128]{1,0:T(8,128)S(1)}, f32[112,128]{1,0:T(8,128)S(1)}, u32[]{:S(2)}, u32[]{:S(2)}) collective-permute-start(f32[112,128]{1,0:T(8,128)S(1)} %shard_map.115.refs_5_.one), channel_id=1, source_target_pairs={{0,8},{1,9},{2,10},{3,11},{4,12},{5,13},{6,14},{7,15},{8,0},{9,1},... | collective-permute-start | bytes 172040 | tf_op jit(solution)/shard_map/ppermute | solution.py:339
  24.8 8.3 %shard_map.116 = (f32[16,128,256]{2,1,0:T(8,128)S(1)}, bf16[45,256,32]{2,1,0:T(8,128)(2,1)S(1)}, bf16[45,64,256]{2,1,0:T(8,128)(2,1)S(1)}, f8e5m2[45,32,256]{2,1,0:T(32,128)(4,1)S(1)}) custom-call(s32[208]{0:T(256)S(1)} %copy-done.4, s32[1]{0:T(128)} %get-tuple-element.16.refs_1_, bf16[16,128,256]{2,1,0:T(8,128)(2,1)S(1)} %copy-done, ...), custom_call_target="tpu_custom_call" | custom-call | flops 1000 | bytes 1000 | tf_op jit(solution)/shard_map/pallas_call | solution.py:327
  33.1 0.0 collective-permute-done.5.four
  33.2 0.0 collective-permute-done.3.two
  33.2 3.4 %collective-permute-start.10 = (f32[400,128]{1,0:T(8,128)S(1)}, f32[400,128]{1,0:T(8,128)S(1)}, u32[]{:S(2)}, u32[]{:S(2)}) collective-permute-start(f32[400,128]{1,0:T(8,128)S(1)} %shard_map.117.refs_6_.one), channel_id=1, source_target_pairs={{0,3},{1,0},{2,1},{3,2},{4,7},{5,4},{6,5},{7,6},{8,11},{9,8},{10,9... | collective-permute-start | bytes 614408 | tf_op jit(solution)/shard_map/ppermute | solution.py:339
  36.6 5.3 %collective-permute-start.9 = (f32[400,128]{1,0:T(8,128)S(1)}, f32[400,128]{1,0:T(8,128)S(1)}, u32[]{:S(2)}, u32[]{:S(2)}) collective-permute-start(f32[400,128]{1,0:T(8,128)S(1)} %shard_map.117.refs_6_.one), channel_id=1, source_target_pairs={{0,2},{1,3},{2,0},{3,1},{4,6},{5,7},{6,4},{7,5},{8,10},{9,11},{10,... | collective-permute-start | bytes 614408 | tf_op jit(solution)/shard_map/ppermute | solution.py:339
  41.9 2.5 %collective-permute-start.8 = (f32[400,128]{1,0:T(8,128)S(1)}, f32[400,128]{1,0:T(8,128)S(1)}, u32[]{:S(2)}, u32[]{:S(2)}) collective-permute-start(f32[400,128]{1,0:T(8,128)S(1)} %shard_map.117.refs_6_.one), channel_id=1, source_target_pairs={{0,1},{1,2},{2,3},{3,0},{4,5},{5,6},{6,7},{7,4},{8,9},{9,10},{10,1... | collective-permute-start | bytes 614408 | tf_op jit(solution)/shard_map/ppermute | solution.py:339
  44.4 9.3 %shard_map.118.earlier.refs_2_ = f32[16,128,256]{2,1,0:T(8,128)S(1)} custom-call(s32[208]{0:T(256)S(1)} %copy-done.4, s32[1]{0:T(128)} %get-tuple-element.16.refs_1_, bf16[45,256,32]{2,1,0:T(8,128)(2,1)S(1)} %get-tuple-element.20.refs_2_, bf16[45,64,256]{2,1,0:T(8,128)(2,1)S(1)} %get-tuple-element.21.refs_3_, ...), custom_call_target="tpu_custom_call" | custom-call | flops 1000 | bytes 1000 | tf_op jit(solution)/shard_map/pallas_call | solution.py:327
  53.7 0.0 collective-permute-done.9.three
  53.7 0.0 collective-permute-done.8.two
  53.7 0.1 shard_map.119.refs_6_.mine
  53.8 0.0 copy-start.2
  53.8 0.0 copy-start.5
  53.8 0.0 copy-start.6
  53.9 0.0 copy-start.7
  53.9 0.3 collective-permute-start.11
  54.1 16.0 %shard_map.120.refs_3_ = f32[16,128,256]{2,1,0:T(8,128)S(1)} custom-call(s32[208]{0:T(256)S(1)} %copy-done.4, s32[1]{0:T(128)} %get-tuple-element.16.refs_1_, bf16[45,256,32]{2,1,0:T(8,128)(2,1)S(1)} %get-tuple-element.20.refs_2_, bf16[45,64,256]{2,1,0:T(8,128)(2,1)S(1)} %get-tuple-element.21.refs_3_, f8e5m2[45,32,256]{2,1,0:T(32,128)(4,1)S(1)} %get-tuple-element.22.refs_4_, ...), custom_call_target="tpu_custom_call" | custom-call | flops 1000 | bytes 1000 | tf_op jit(solution)/shard_map/pallas_call | solution.py:327
  70.1 0.0 collective-permute-done.11.theirs
  70.2 4.2 %shard_map.121 = (f32[16,32,256]{2,1,0:T(8,128)}, f32[16,32,256]{2,1,0:T(8,128)}) custom-call(s32[1]{0:T(128)} %bitcast.refs_0_.place, s32[1,16]{1,0:T(1,128)S(1)} %copy-done.7, f32[1552,128]{1,0:T(8,128)S(1)} %shard_map.119.refs_6_.mine, f32[1552,128]{1,0:T(8,128)S(1)} %collective-permute-done.11.theirs, f32[3,1,64]{2,1,0:T(1,128)S(1)} %bitcast.8, ...), custom_call_target="tpu_custom_call" | custom-call | flops 1000 | bytes 1000 | tf_op jit(solution)/shard_map/pallas_call | solution.py:327
  (17 shorter events, 0.1 us)
Async XLA Ops:
  6.1 18.8 %collective-permute-start.6 = (f32[496,256]{1,0:T(8,128)}, f32[496,256]{1,0:T(8,128)S(1)}, u32[]{:S(2)}, u32[]{:S(2)}) collective-permute-start(f32[496,256]{1,0:T(8,128)} %get-tuple-element.17), channel_id=1, source_target_pairs={{0,1},{1,2},{2,3},{3,4},{4,5},{5,6},{6,7},{7,8},{8,9},{9,10},{10,1... | collective-permute-start | bytes 1523720 | tf_op jit(solution)/shard_map/ppermute | solution.py:358
  9.5 15.4 %collective-permute-start.7 = (f32[496,256]{1,0:T(8,128)}, f32[496,256]{1,0:T(8,128)S(1)}, u32[]{:S(2)}, u32[]{:S(2)}) collective-permute-start(f32[496,256]{1,0:T(8,128)} %get-tuple-element.18), channel_id=1, source_target_pairs={{1,0},{2,1},{3,2},{4,3},{5,4},{6,5},{7,6},{8,7},{9,8},{10,9},{11,1... | collective-permute-start | bytes 1523720 | tf_op jit(solution)/shard_map/ppermute | solution.py:359
  11.9 9.1 %collective-permute-start.2 = (f32[40,128]{1,0:T(8,128)}, f32[40,128]{1,0:T(8,128)S(1)}, u32[]{:S(2)}, u32[]{:S(2)}) collective-permute-start(f32[40,128]{1,0:T(8,128)} %get-tuple-element.13.refs_1_.one), channel_id=1, source_target_pairs={{0,48},{1,49},{2,50},{3,51},{4,52},{5,53},{6,54},{7,55},{8,56},{9,... | collective-permute-start | bytes 61448 | tf_op jit(solution)/shard_map/ppermute | solution.py:339
  12.7 8.3 %collective-permute-start.1 = (f32[40,128]{1,0:T(8,128)}, f32[40,128]{1,0:T(8,128)S(1)}, u32[]{:S(2)}, u32[]{:S(2)}) collective-permute-start(f32[40,128]{1,0:T(8,128)} %get-tuple-element.13.refs_1_.one), channel_id=1, source_target_pairs={{0,32},{1,33},{2,34},{3,35},{4,36},{5,37},{6,38},{7,39},{8,40},{9,... | collective-permute-start | bytes 61448 | tf_op jit(solution)/shard_map/ppermute | solution.py:339
  13.7 7.4 %collective-permute-start = (f32[40,128]{1,0:T(8,128)}, f32[40,128]{1,0:T(8,128)S(1)}, u32[]{:S(2)}, u32[]{:S(2)}) collective-permute-start(f32[40,128]{1,0:T(8,128)} %get-tuple-element.13.refs_1_.one), channel_id=1, source_target_pairs={{0,16},{1,17},{2,18},{3,19},{4,20},{5,21},{6,22},{7,23},{8,24},{9,... | collective-permute-start | bytes 61448 | tf_op jit(solution)/shard_map/ppermute | solution.py:339
  15.9 1.2 %copy-start = (bf16[16,128,256]{2,1,0:T(8,128)(2,1)S(1)}, bf16[16,128,256]{2,1,0:T(8,128)(2,1)}, u32[]{:S(2)}) copy-start(bf16[16,128,256]{2,1,0:T(8,128)(2,1)} %get-tuple-element.14.refs_0_.refs_2_.refs_5_) | copy-start | bytes 3145732
  17.1 0.7 copy-start.3
  17.8 7.0 %copy-start.4 = (s32[208]{0:T(256)S(1)}, s32[208]{0:T(256)}, u32[]{:S(2)}) copy-start(s32[208]{0:T(256)} %get-tuple-element.15.refs_0_) | copy-start | bytes 2500
  21.1 12.1 %collective-permute-start.5 = (f32[112,128]{1,0:T(8,128)S(1)}, f32[112,128]{1,0:T(8,128)S(1)}, u32[]{:S(2)}, u32[]{:S(2)}) collective-permute-start(f32[112,128]{1,0:T(8,128)S(1)} %shard_map.115.refs_5_.one), channel_id=1, source_target_pairs={{0,12},{1,13},{2,14},{3,15},{4,0},{5,1},{6,2},{7,3},{8,4},{9,5},{1... | collective-permute-start | bytes 172040 | tf_op jit(solution)/shard_map/ppermute | solution.py:339
  21.2 11.9 %collective-permute-start.4 = (f32[112,128]{1,0:T(8,128)S(1)}, f32[112,128]{1,0:T(8,128)S(1)}, u32[]{:S(2)}, u32[]{:S(2)}) collective-permute-start(f32[112,128]{1,0:T(8,128)S(1)} %shard_map.115.refs_5_.one), channel_id=1, source_target_pairs={{0,8},{1,9},{2,10},{3,11},{4,12},{5,13},{6,14},{7,15},{8,0},{9,1},... | collective-permute-start | bytes 172040 | tf_op jit(solution)/shard_map/ppermute | solution.py:339
  24.8 8.3 %collective-permute-start.3 = (f32[112,128]{1,0:T(8,128)S(1)}, f32[112,128]{1,0:T(8,128)S(1)}, u32[]{:S(2)}, u32[]{:S(2)}) collective-permute-start(f32[112,128]{1,0:T(8,128)S(1)} %shard_map.115.refs_5_.one), channel_id=1, source_target_pairs={{0,4},{1,5},{2,6},{3,7},{4,8},{5,9},{6,10},{7,11},{8,12},{9,13},{1... | collective-permute-start | bytes 172040 | tf_op jit(solution)/shard_map/ppermute | solution.py:339
  33.2 20.5 %collective-permute-start.10 = (f32[400,128]{1,0:T(8,128)S(1)}, f32[400,128]{1,0:T(8,128)S(1)}, u32[]{:S(2)}, u32[]{:S(2)}) collective-permute-start(f32[400,128]{1,0:T(8,128)S(1)} %shard_map.117.refs_6_.one), channel_id=1, source_target_pairs={{0,3},{1,0},{2,1},{3,2},{4,7},{5,4},{6,5},{7,6},{8,11},{9,8},{10,9... | collective-permute-start | bytes 614408 | tf_op jit(solution)/shard_map/ppermute | solution.py:339
  36.6 17.1 %collective-permute-start.9 = (f32[400,128]{1,0:T(8,128)S(1)}, f32[400,128]{1,0:T(8,128)S(1)}, u32[]{:S(2)}, u32[]{:S(2)}) collective-permute-start(f32[400,128]{1,0:T(8,128)S(1)} %shard_map.117.refs_6_.one), channel_id=1, source_target_pairs={{0,2},{1,3},{2,0},{3,1},{4,6},{5,7},{6,4},{7,5},{8,10},{9,11},{10,... | collective-permute-start | bytes 614408 | tf_op jit(solution)/shard_map/ppermute | solution.py:339
  41.9 11.8 %collective-permute-start.8 = (f32[400,128]{1,0:T(8,128)S(1)}, f32[400,128]{1,0:T(8,128)S(1)}, u32[]{:S(2)}, u32[]{:S(2)}) collective-permute-start(f32[400,128]{1,0:T(8,128)S(1)} %shard_map.117.refs_6_.one), channel_id=1, source_target_pairs={{0,1},{1,2},{2,3},{3,0},{4,5},{5,6},{6,7},{7,4},{8,9},{9,10},{10,1... | collective-permute-start | bytes 614408 | tf_op jit(solution)/shard_map/ppermute | solution.py:339
  53.8 16.3 %copy-start.1 = (bf16[16,128,256]{2,1,0:T(8,128)(2,1)S(1)}, bf16[16,128,256]{2,1,0:T(8,128)(2,1)}, u32[]{:S(2)}) copy-start(bf16[16,128,256]{2,1,0:T(8,128)(2,1)} %get-tuple-element.23.product) | copy-start | bytes 3145732
  53.8 16.3 %copy-start.2 = (f32[1,64,64]{2,1,0:T(8,128)S(1)}, f32[1,64,64]{2,1,0:T(8,128)}, u32[]{:S(2)}) copy-start(f32[1,64,64]{2,1,0:T(8,128)} %param.15) | copy-start | bytes 49156
  53.8 16.3 %copy-start.5 = (f32[1,3,64]{2,0,1:T(1,128)S(1)}, f32[1,3,64]{2,0,1:T(1,128)}, u32[]{:S(2)}) copy-start(f32[1,3,64]{2,0,1:T(1,128)} %param.14) | copy-start | bytes 2308
  53.8 16.3 %copy-start.6 = (f32[2,3,64]{2,0,1:T(2,128)S(1)}, f32[2,3,64]{2,0,1:T(2,128)}, u32[]{:S(2)}) copy-start(f32[2,3,64]{2,0,1:T(2,128)} %param.16) | copy-start | bytes 4612
  53.9 16.3 %copy-start.7 = (s32[1,16]{1,0:T(1,128)S(1)}, s32[1,16]{1,0:T(1,128)}, u32[]{:S(2)}) copy-start(s32[1,16]{1,0:T(1,128)} %far_list.1) | copy-start | bytes 196
  53.9 16.3 %collective-permute-start.11 = (f32[1552,128]{1,0:T(8,128)S(1)}, f32[1552,128]{1,0:T(8,128)S(1)}, u32[]{:S(2)}, u32[]{:S(2)}) collective-permute-start(f32[1552,128]{1,0:T(8,128)S(1)} %shard_map.119.refs_6_.mine), channel_id=1, source_target_pairs={{0,64},{64,0},{1,65},{65,1},{2,66},{66,2},{3,67},{67,3},{4,68},{68... | collective-permute-start | bytes 2383880 | tf_op jit(solution)/shard_map/ppermute | solution.py:381

commit v4 on v3

--- a/solution.py
+++ b/solution.py
@@ -29,6 +29,10 @@
 AXES = ("group", "dev")
 
 
+def my_rank():
+    return lax.axis_index("group") * 64 + lax.axis_index("dev")
+
+
 def dot(a, b):
     return jnp.dot(a, b, preferred_element_type=F32)
 
@@ -94,7 +98,7 @@
     return lax.dot_general(a, b, (((1,), (1,)), ((), ())), preferred_element_type=F32)
 
 
-def node_block(packed, basis, leaf_transfer, dev_transfer, skeleton, product, out):
+def node_block(packed, basis, leaf_transfer, dev_transfer, skeleton, product, out, meanwhile):
     high, low = jnp.zeros((64, 64), F32), jnp.zeros((32, 64), F32)
     for l in range(basis.shape[0]):
         left, left_low = split2(leaf_transfer[l])
@@ -104,6 +108,7 @@
         product[l, 0:64, :], product[l, 64:128, :] = one, two
         high += dot_t(packed[l, 64:128, :], one)
         low += dot_t(packed[l, 64:96, :], two)
+    meanwhile()
     total = high[:32] + high[32:] + low
     image = lax.dot_general(
         total, dev_transfer[...], (((1,), (1,)), ((), ())), precision=HIGH, preferred_element_type=F32
@@ -115,67 +120,90 @@
     out[24:40, :] = jnp.concatenate([image[:16], image[16:]], axis=1)
 
 
-def prepare_kernel(reach, place, points_in, charges_in, neighbours_in, counts_in, basis_in, leaf_transfer_in, dev_transfer_in,
-                   skeleton_in, up, down, packed, order, limits, block, product,
-                   rows, points, charges, neighbours, counts, basis, leaf_transfer, dev_transfer, skeleton, sems):
+def prepare_kernel(reach, points_in, charges_in, neighbours_in, counts_in, basis_in, leaf_transfer_in, dev_transfer_in,
+                   skeleton_in, up, down, packed_out, product_out, order_out, block,
+                   rows, edges, packed, product, points, charges, neighbours, counts, basis, leaf_transfer, dev_transfer,
+                   skeleton, order, load_sems, store_sems):
     leaves, width = neighbours.shape
     sources = (points_in, charges_in, neighbours_in, counts_in, basis_in, leaf_transfer_in, dev_transfer_in, skeleton_in)
     targets = (points, charges, neighbours, counts, basis, leaf_transfer, dev_transfer, skeleton)
-    loads = [pltpu.make_async_copy(a, b, sems.at[i]) for i, (a, b) in enumerate(zip(sources, targets))]
+    loads = [pltpu.make_async_copy(a, b, load_sems.at[i]) for i, (a, b) in enumerate(zip(sources, targets))]
     for load in loads:
         load.start()
+    stores = []
+
+    def store(source, target):
+        stores.append(pltpu.make_async_copy(source, target, store_sems.at[len(stores)]))
+        stores[-1].start()
+
+    moved = 32 * reach
     loads[0].wait()
     coords = [points[c] for c in range(3)]
+    for i, first in enumerate((leaves - reach, 0)):
+        for c in range(3):
+            edges[i, 16 * c : 16 * c + reach, :] = coords[c][first : first + reach]
+            edges[i, 16 * c + reach : 16 * c + 16, :] = jnp.zeros((16 - reach, 256), F32)
+        store(edges.at[i], (up, down)[i].at[pl.ds(moved, 48)])
     for source in (True, False):
         write_rows(rows, coords, source)
         at = 0 if source else 32
         for l in range(leaves):
             packed[l, at : at + 32, :] = jnp.concatenate(leaf_rows(rows, l), axis=1).astype(BF)
-    for ref, first in ((up, leaves - reach), (down, 0)):
-        for c in range(3):
-            at = 32 * reach + 16 * c
-            ref[at : at + reach, :] = coords[c][first : first + reach]
-            ref[at + reach : at + 16, :] = jnp.zeros((16 - reach, 256), F32)
     loads[1].wait()
+    store(charges.at[pl.ds(32 * (leaves - reach), moved)], up.at[pl.ds(0, moved)])
+    store(charges.at[pl.ds(0, moved)], down.at[pl.ds(0, moved)])
     for l in range(leaves):
-        packed[l, 64:96, :], packed[l, 96:128, :] = split2(charges[l])
-        for ref, first in ((up, leaves - reach), (down, 0)):
-            if 0 <= l - first < reach:
-                ref[32 * (l - first) : 32 * (l - first) + 32, :] = charges[l]
-    loads[2].wait()
-    loads[3].wait()
-
-    base = place[0] * leaves - reach
-
-    def note(slot, at):
-        for leaf in range(leaves):
-            chosen = jnp.clip(neighbours[leaf, slot] - base, 0, leaves + 2 * reach - 1)
-            order[at] = leaf * 64 + chosen
-            at = at + (slot < counts[leaf]).astype(jnp.int32)
-        return at
-
-    ends = lax.fori_loop(0, width, note, 0)
-    for k in range(DEPTH):
-        order[ends + k] = leaves + 2 * reach
-    limits[0] = (ends + DEPTH - 1) // DEPTH
+        packed[l, 64:96, :], packed[l, 96:128, :] = split2(charges[32 * l : 32 * l + 32, :])
+    store(packed, packed_out)
     for load in loads[4:]:
         load.wait()
-    node_block(packed, basis, leaf_transfer, dev_transfer, skeleton, product, block)
-
-
-def merge_kernel(one, two, three, four, earlier, out):
+
+    def listing():
+        store(product, product_out)
+        loads[2].wait()
+        loads[3].wait()
+        base = my_rank() * leaves - reach
+
+        def note(slot, at):
+            for leaf in range(leaves):
+                chosen = jnp.clip(neighbours[leaf, slot] - base, 0, leaves + 2 * reach - 1)
+                order[at] = leaf * 64 + chosen
+                at = at + (slot < counts[leaf]).astype(jnp.int32)
+            return at
+
+        ends = lax.fori_loop(0, width, note, 0)
+        for k in range(DEPTH):
+            order[ends + k] = leaves + 2 * reach
+        order[order.shape[0] - 1] = (ends + DEPTH - 1) // DEPTH
+        store(order, order_out)
+
+    node_block(packed, basis, leaf_transfer, dev_transfer, skeleton, product, block, listing)
+    for one in stores:
+        one.wait()
+
+
+def merge_kernel(shifts, own, one, two, three, earlier, out):
     del earlier
     count = one.shape[0] - 16
-    for i, ref in enumerate((one, two, three, four)):
+    for i, ref in zip((0, *shifts), (own, one, two, three)):
         out[count * i : count * i + count, :] = ref[:count, :]
-    out[4 * count :, :] = (one[count:, :] + two[count:, :]) + (three[count:, :] + four[count:, :])
-
-
-def near_pairs(lo, hi, order, wa, c2, c8, ua, acc, slots):
+    out[4 * count :, :] = (own[count:, :] + one[count:, :]) + (two[count:, :] + three[count:, :])
+
+
+def near_pairs(lo, hi, order, wa, c2, c8, ua, start, acc, slots, load=None):
     xs, highs, lows = slots[:DEPTH], slots[DEPTH : 2 * DEPTH], slots[2 * DEPTH :]
-    acc[...] = jnp.zeros_like(acc)
+
+    def begin(l, carry):
+        acc[l] = jnp.zeros(acc.shape[1:], F32) if start is None else start[l]
+        return carry
+
+    lax.fori_loop(0, acc.shape[0], begin, 0)
     highs[DEPTH - 1][...] = jnp.zeros(highs[0].shape, BF)
     lows[DEPTH - 1][...] = jnp.zeros(lows[0].shape, F8)
+    if load is not None:
+        load.wait()
+        last = order[order.shape[0] - 1]
+        lo, hi = jnp.minimum(lo, last), jnp.minimum(hi, last)
 
     def distances(i):
         pair = order[i]
@@ -238,11 +266,13 @@
 def own_kernel(end, packed, earlier, acc, wa, c2, c8, *slots):
     del earlier
     unpack(packed, wa, c2, c8, 0)
-    near_pairs(0, end, Selves(), wa, c2, c8, Targets(packed), acc, slots)
-
-
-def first_kernel(begin, end, order, limits, packed, before, after, earlier, acc, wa, c2, c8, rows, *slots):
+    near_pairs(0, end, Selves(), wa, c2, c8, Targets(packed), None, acc, slots)
+
+
+def first_kernel(begin, end, order_in, packed, before, after, start, earlier, acc, wa, c2, c8, rows, order, sem, *slots):
     del earlier
+    load = pltpu.make_async_copy(order_in, order, sem)
+    load.start()
     leaves, half = packed.shape[0], before.shape[0] // 35
     total = leaves + 2 * half
     unpack(packed, wa, c2, c8, half)
@@ -256,19 +286,22 @@
     wa[total] = wa[half]
     c2[total] = jnp.zeros(c2.shape[1:], BF)
     c8[total] = jnp.zeros(c8.shape[1:], F8)
-    near_pairs(jnp.minimum(begin, limits[0]), jnp.minimum(end, limits[0]), order, wa, c2, c8, Targets(packed), acc, slots)
-
-
-def next_kernel(begin, end, order, limits, wa, c2, c8, packed, earlier, acc, *slots):
+    near_pairs(begin, end, order, wa, c2, c8, Targets(packed), start, acc, slots, load)
+
+
+def next_kernel(begin, end, order_in, wa, c2, c8, packed, start, earlier, acc, order, sem, *slots):
     del earlier
-    near_pairs(jnp.minimum(begin, limits[0]), jnp.minimum(end, limits[0]), order, wa, c2, c8, Targets(packed), acc, slots)
-
-
-def far_kernel(place, far_list, mine, theirs, own_skeleton, groups, dev_transfer, product, *refs):
-    nears, (value_out, slope_out, coefs, kernels) = refs[:-4], refs[-4:]
+    load = pltpu.make_async_copy(order_in, order, sem)
+    load.start()
+    near_pairs(begin, end, order, wa, c2, c8, Targets(packed), start, acc, slots, load)
+
+
+def far_kernel(far_list_in, mine, theirs, own_skeleton, groups, dev_transfer, product, near, value_out, slope_out,
+               coefs, kernels, values, slopes, far_list, load_sem, sems):
+    load = pltpu.make_async_copy(far_list_in, far_list, load_sem)
+    load.start()
     leaves = product.shape[0]
-    rank = place[0]
-    group, node = rank // 64, rank % 64
+    group, node = lax.axis_index("group"), lax.axis_index("dev")
 
     def pair_kernel(column, row):
         x = jnp.full((64, 64), X0, F32)
@@ -278,6 +311,14 @@
         value, slope = matern_terms(x)
         return jnp.concatenate([value * VALUE_SCALE, slope * SLOPE_SCALE], axis=1)
 
+    other = theirs[theirs.shape[0] - 16 :, :]
+    other = jnp.concatenate([other[:, :64], other[:, 64:]], axis=0)
+    near_group, far_group = groups[:, pl.ds(group, 1), :][:, 0], groups[:, pl.ds(1 - group, 1), :][:, 0]
+    column = jnp.transpose(jnp.concatenate([far_group, jnp.zeros((5, 64), F32)], axis=0))
+    top = dot32(other, pair_kernel(column, near_group))
+    top = jnp.concatenate([top[:, :64], top[:, 64:]], axis=0)
+    top = dot32(top, dev_transfer[...])
+    load.wait()
     own = jnp.concatenate([own_skeleton[c] for c in range(3)], axis=0)
     for j in range(far_list.shape[1]):
         s = far_list[0, j]
@@ -290,21 +331,26 @@
     kernel, kernel_low = split2(kernels[...])
     both = dot(jnp.concatenate([coef, coef_low], axis=0), kernel)
     far = both[:32] + both[32:] + dot(coef, kernel_low)
-    other = theirs[theirs.shape[0] - 16 :, :]
-    other = jnp.concatenate([other[:, :64], other[:, 64:]], axis=0)
-    near_group, far_group = groups[:, pl.ds(group, 1), :][:, 0], groups[:, pl.ds(1 - group, 1), :][:, 0]
-    column = jnp.transpose(jnp.concatenate([far_group, jnp.zeros((5, 64), F32)], axis=0))
-    top = dot32(other, pair_kernel(column, near_group))
     far = jnp.concatenate([far[:, :64], far[:, 64:]], axis=0)
-    top = jnp.concatenate([top[:, :64], top[:, 64:]], axis=0)
-    local_dev, local_low = split2(far + dot32(top, dev_transfer[...]))
+    local_dev, local_low = split2(far + top)
     local_both = jnp.concatenate([local_dev, local_low], axis=0)
+    stores = []
     for l in range(leaves):
         both = dot(local_both, product[l, 0:64, :])
         part = both[:64] + both[64:] + dot(local_dev, product[l, 64:128, :])
-        near = (nears[0][l] + nears[1][l]) + (nears[2][l] + nears[3][l])
-        value_out[l] = (near[0:32] + near[32:64]) * (VALUE_SCALE * 2.0**-LIFT) + part[:32]
-        slope_out[l] = (near[64:96] + near[96:128]) * (SLOPE_SCALE * 2.0**-LIFT) + part[32:]
+        both = near[l]
+        values[l] = (both[0:32] + both[32:64]) * (VALUE_SCALE * 2.0**-LIFT) + part[:32]
+        slopes[l] = (both[64:96] + both[96:128]) * (SLOPE_SCALE * 2.0**-LIFT) + part[32:]
+        if l % 4 == 3:
+            some = slice(l - 3, l + 1)
+            stores += [
+                pltpu.make_async_copy(values.at[some], value_out.at[some], sems.at[0, l // 4]),
+                pltpu.make_async_copy(slopes.at[some], slope_out.at[some], sems.at[1, l // 4]),
+            ]
+            stores[-2].start()
+            stores[-1].start()
+    for store in stores:
+        store.wait()
 
 
 VMEM = pl.BlockSpec(memory_space=pltpu.VMEM)
@@ -317,43 +363,44 @@
 
 def local(points, charges, basis, leaf_transfer, dev_skeleton, dev_transfer, group_skeleton, neighbours, counts, far_list):
     leaves, width = neighbours.shape
-    place = jnp.full((1,), lax.axis_index(AXES), jnp.int32)
     size = lax.axis_size(AXES)
     forward = [(i, i + 1) for i in range(size - 1)]
     anywhere = pl.BlockSpec(memory_space=pl.ANY)
     light = pl.CostEstimate(flops=1000, bytes_accessed=1000, transcendentals=0)
 
-    def call(kernel, outs, ins, scratch, args, limit):
+    def call(kernel, outs, ins, scratch, args, limit, specs=None):
         return pl.pallas_call(
             kernel,
             out_shape=tuple(jax.ShapeDtypeStruct(shape, kind) for shape, kind in outs),
             in_specs=ins,
-            out_specs=tuple(SMEM if kind == jnp.int32 else VMEM for _, kind in outs),
+            out_specs=tuple(specs or [SMEM if kind == jnp.int32 else VMEM for _, kind in outs]),
             scratch_shapes=scratch,
             compiler_params=pltpu.CompilerParams(vmem_limit_bytes=limit * MIB),
             cost_estimate=light,
         )(*args)
 
-    def gathered(block, div, earlier):
+    def gathered(block, div, earlier, shifts):
         rows = 4 * block.shape[0] - 48
-        came = [block] + [lax.ppermute(block, "dev", dev_shift(div, k)) for k in (1, 3, 2)]
-        came = [came[0], came[1], came[3], came[2]]
-        return call(merge_kernel, [((rows, 128), F32)], [VMEM] * 4 + [anywhere], [], (*came, earlier), 8)[0]
+        came = [block] + [lax.ppermute(block, "dev", dev_shift(div, k)) for k in shifts]
+        merge = lambda *refs: merge_kernel(shifts, *refs)
+        return call(merge, [((rows, 128), F32)], [VMEM] * 4 + [anywhere], [], (*came, earlier), 8)[0]
 
     points = jnp.transpose(points, (1, 0, 2))
     skeleton = jnp.transpose(dev_skeleton, (1, 0, 2))
     total = leaves + 2 * REACH
     strip = ((REACH * 32 + 48, 256), F32)
     rows = pltpu.VMEM((leaves * 64, 128), F32)
-    held = (points, charges, neighbours, counts, basis, leaf_transfer, dev_transfer[0], skeleton)
-    up, down, packed, order, limits, mine, product = call(
+    held = (points, charges.reshape(leaves * 32, 256), neighbours, counts, basis, leaf_transfer, dev_transfer[0], skeleton)
+    wide = ((leaves, 128, 256), BF)
+    pairs = ((256,), jnp.int32)
+    up, down, packed, product, order, mine = call(
         lambda *refs: prepare_kernel(REACH, *refs),
-        [strip, strip, ((leaves, 128, 256), BF),
-         ((leaves * width + 2 * DEPTH,), jnp.int32), ((1,), jnp.int32), ((40, 128), F32), ((leaves, 128, 256), BF)],
-        [SMEM] + [pl.BlockSpec(memory_space=pltpu.HBM)] * 8,
-        [rows] + [(pltpu.SMEM if h.dtype == jnp.int32 else pltpu.VMEM)(h.shape, h.dtype) for h in held]
-        + [pltpu.SemaphoreType.DMA((8,))],
-        (place, *held), 60,
+        [strip, strip, wide, wide, pairs, ((40, 128), F32)],
+        [pl.BlockSpec(memory_space=pltpu.HBM)] * 8,
+        [rows, pltpu.VMEM((2, 48, 256), F32), pltpu.VMEM(*wide), pltpu.VMEM(*wide)]
+        + [(pltpu.SMEM if h.dtype == jnp.int32 else pltpu.VMEM)(h.shape, h.dtype) for h in held]
+        + [pltpu.SMEM(*pairs), pltpu.SemaphoreType.DMA((8,)), pltpu.SemaphoreType.DMA((7,))],
+        held, 60, [anywhere] * 5 + [VMEM],
     )
     before = lax.ppermute(up, AXES, forward)
     after = lax.ppermute(down, AXES, [(j, i) for i, j in forward])
@@ -361,35 +408,36 @@
     slots = [pltpu.VMEM((256, 256), F32)] * DEPTH + [pltpu.VMEM((2, 256, 256), BF)] * DEPTH
     slots += [pltpu.VMEM((2, 256, 256), F8)] * DEPTH
     sources = [((leaves, 256, 32), BF), ((leaves, 64, 256), BF), ((leaves, 32, 256), F8)]
+    listing = [pltpu.SMEM(*pairs), pltpu.SemaphoreType.DMA(())]
     (near0,) = call(
         lambda *refs: own_kernel(CUTS[0], *refs),
         [partial], [VMEM, anywhere], [pltpu.VMEM(*source) for source in sources] + slots, (packed, mine), 24,
     )
-    mine = gathered(mine, 16, near0)
+    mine = gathered(mine, 16, near0, (3, 2, 1))
     near1, *held = call(
         lambda *refs: first_kernel(CUTS[0], CUTS[1], *refs),
         [partial] + [((total + 1, *shape[1:]), kind) for shape, kind in sources],
-        [SMEM] * 2 + [VMEM] * 3 + [anywhere], [rows] + slots,
-        (order, limits, packed, before, after, mine), 24,
-    )
-    mine = gathered(mine, 4, near1)
+        [anywhere] + [VMEM] * 4 + [anywhere], [rows] + listing + slots,
+        (order, packed, before, after, near0, mine), 24,
+    )
+    mine = gathered(mine, 4, near1, (3, 2, 1))
     (near2,) = call(
         lambda *refs: next_kernel(CUTS[1], CUTS[2], *refs),
-        [partial], [SMEM] * 2 + [VMEM] * 4 + [anywhere], slots, (order, limits, *held, packed, mine), 24,
-    )
-    mine = gathered(mine, 1, near2)
+        [partial], [anywhere] + [VMEM] * 5 + [anywhere], listing + slots, (order, *held, packed, near1, mine), 24,
+    )
+    mine = gathered(mine, 1, near2, (2, 1, 3))
     theirs = lax.ppermute(mine, "group", [(0, 1), (1, 0)])
     (near3,) = call(
         lambda *refs: next_kernel(CUTS[2], leaves * width // DEPTH, *refs),
-        [partial], [SMEM] * 2 + [VMEM] * 4 + [anywhere], slots, (order, limits, *held, packed, mine), 24,
-    )
-    nears = (near0, near1, near2, near3)
+        [partial], [anywhere] + [VMEM] * 5 + [anywhere], listing + slots, (order, *held, packed, near2, mine), 24,
+    )
     out = ((leaves, 32, 256), F32)
     return call(
-        far_kernel, [out, out], [SMEM] * 2 + [VMEM] * (6 + len(nears)),
-        [pltpu.VMEM((32, 1024), F32), pltpu.VMEM((1024, 128), F32)],
-        (place, far_list, mine, theirs, skeleton, jnp.transpose(group_skeleton, (1, 0, 2)), dev_transfer[0],
-         product, *nears), 24,
+        far_kernel, [out, out], [anywhere] + [VMEM] * 7,
+        [pltpu.VMEM((32, 1024), F32), pltpu.VMEM((1024, 128), F32), pltpu.VMEM(*out), pltpu.VMEM(*out),
+         pltpu.SMEM(far_list.shape, jnp.int32), pltpu.SemaphoreType.DMA(()), pltpu.SemaphoreType.DMA((2, leaves // 4))],
+        (far_list, mine, theirs, skeleton, jnp.transpose(group_skeleton, (1, 0, 2)), dev_transfer[0],
+         product, near3), 24, [anywhere] * 2,
     )
 
 

time: 75.4 us -> 73.3 us (0.972)
  the two profiles are of different devices: /device:TPU:90 before, /device:TPU:91 now
where the time goes in v4:
time: 73.3 us; the launch traced here: 73.6 us
  Pallas kernels  45.4 us (62%)
  starting transfers between devices  25 us (34%)
  local copies, waits for them, and re-layouts  1.98 us (3%)
  between operations  0.88 us (1%)
    pallas_call x9, Pallas kernels, call(): pl.pallas_call(kernel, out_shape=tuple((jax.ShapeDtypeStruct(shape, kind)...  45.4 us
    ppermute x9, starting transfers between devices, gathered(): lax.ppermute(block, 'dev', dev_shift(div, k))  12.4 us
    ppermute x1, starting transfers between devices, local(): theirs = lax.ppermute(mine, 'group', [(0, 1), (1, 0)])  7.26 us
    ppermute x1, starting transfers between devices, local(): before = lax.ppermute(up, AXES, forward)  3.12 us
    ppermute x1, starting transfers between devices, local(): after = lax.ppermute(down, AXES, [(j, i) for i, j in forward])  2.16 us
    unnamed x16, local copies, waits for them, and re-layouts  1.98 us
  transfers between devices with their start and end apart: 12, of which 1 were waited for; matrix products, arithmetic and copies ran while one was open for 0% of the time, Pallas kernels for 49%

profile of v4, /device:TPU:91, one launch (start us, length us, event | category | flops | bytes accessed | tf_op | source)
XLA Modules:
  0.0 73.6 jit_solution(3578592548822317541)
XLA Ops:
  0.6 5.4 %shard_map.113 = (f32[496,256]{1,0:T(8,128)}, f32[496,256]{1,0:T(8,128)}, bf16[16,128,256]{2,1,0:T(8,128)(2,1)}, bf16[16,128,256]{2,1,0:T(8,128)(2,1)}, s32[256]{0:T(256)}, /*index=5*/f32[40,128]{1,0:T(8,128)}) custom-call(f32[3,16,256]{2,1,0:T(8,128)} %bitcast.11, f32[512,256]{1,0:T(8,128)} %bitcast.10, s32[16,12]{1,0:T(8,128)} %refs_2_.1, s32[16]{0:T(128)} %refs_3_.1, ...), custom_call_target="tpu_custom_call" | custom-call | flops 1000 | bytes 1000 | tf_op jit(solution)/shard_map/pallas_call | solution.py:372
  6.0 3.1 %collective-permute-start.6 = (f32[496,256]{1,0:T(8,128)}, f32[496,256]{1,0:T(8,128)S(1)}, u32[]{:S(2)}, u32[]{:S(2)}) collective-permute-start(f32[496,256]{1,0:T(8,128)} %get-tuple-element.15), channel_id=1, source_target_pairs={{0,1},{1,2},{2,3},{3,4},{4,5},{5,6},{6,7},{7,8},{8,9},{9,10},{10,1... | collective-permute-start | bytes 1523720 | tf_op jit(solution)/shard_map/ppermute | solution.py:405
  9.1 2.2 %collective-permute-start.7 = (f32[496,256]{1,0:T(8,128)}, f32[496,256]{1,0:T(8,128)S(1)}, u32[]{:S(2)}, u32[]{:S(2)}) collective-permute-start(f32[496,256]{1,0:T(8,128)} %get-tuple-element.16), channel_id=1, source_target_pairs={{1,0},{2,1},{3,2},{4,3},{5,4},{6,5},{7,6},{8,7},{9,8},{10,9},{11,1... | collective-permute-start | bytes 1523720 | tf_op jit(solution)/shard_map/ppermute | solution.py:406
  11.3 0.5 collective-permute-start
  11.8 0.7 collective-permute-start.1
  12.5 1.9 %collective-permute-start.2 = (f32[40,128]{1,0:T(8,128)}, f32[40,128]{1,0:T(8,128)S(1)}, u32[]{:S(2)}, u32[]{:S(2)}) collective-permute-start(f32[40,128]{1,0:T(8,128)} %get-tuple-element.12.refs_1_.refs_0_), channel_id=1, source_target_pairs={{0,16},{1,17},{2,18},{3,19},{4,20},{5,21},{6,22},{7,23},{8,24},{9,... | collective-permute-start | bytes 61448 | tf_op jit(solution)/shard_map/ppermute | solution.py:384
  14.4 1.2 %copy-done = bf16[16,128,256]{2,1,0:T(8,128)(2,1)S(1)} copy-done((bf16[16,128,256]{2,1,0:T(8,128)(2,1)S(1)}, bf16[16,128,256]{2,1,0:T(8,128)(2,1)}, u32[]{:S(2)}) %copy-start) | copy-done | bytes 1048600
  15.6 0.7 copy-done.3
  16.3 3.4 %shard_map.114.refs_4_ = f32[16,128,256]{2,1,0:T(8,128)S(1)} custom-call(bf16[16,128,256]{2,1,0:T(8,128)(2,1)S(1)} %copy-done, f32[40,128]{1,0:T(8,128)S(1)} %copy-done.3), custom_call_target="tpu_custom_call" | custom-call | flops 1000 | bytes 1000 | tf_op jit(solution)/shard_map/pallas_call | solution.py:372
  19.8 0.0 collective-permute-done.refs_1_
  19.8 0.0 collective-permute-done.2.refs_3_
  19.8 0.1 collective-permute-start.3
  19.9 3.1 %collective-permute-start.4 = (f32[112,128]{1,0:T(8,128)S(1)}, f32[112,128]{1,0:T(8,128)S(1)}, u32[]{:S(2)}, u32[]{:S(2)}) collective-permute-start(f32[112,128]{1,0:T(8,128)S(1)} %shard_map.115.refs_5_.refs_0_), channel_id=1, source_target_pairs={{0,8},{1,9},{2,10},{3,11},{4,12},{5,13},{6,14},{7,15},{8,0},{9,1},... | collective-permute-start | bytes 172040 | tf_op jit(solution)/shard_map/ppermute | solution.py:384
  23.0 0.0 collective-permute-start.5
  23.0 0.0 collective-permute-done.6.refs_2_
  23.0 0.3 collective-permute-done.7.refs_3_
  23.4 7.3 %shard_map.116 = (f32[16,128,256]{2,1,0:T(8,128)S(1)}, bf16[45,256,32]{2,1,0:T(8,128)(2,1)S(1)}, bf16[45,64,256]{2,1,0:T(8,128)(2,1)S(1)}, f8e5m2[45,32,256]{2,1,0:T(32,128)(4,1)S(1)}) custom-call(s32[256]{0:T(256)S(1)} %copy-done.4, bf16[16,128,256]{2,1,0:T(8,128)(2,1)S(1)} %copy-done, f32[496,256]{1,0:T(8,128)S(1)} %collective-permute-done.6.refs_2_, ...), custom_call_target="tpu_custom_call" | custom-call | flops 1000 | bytes 1000 | tf_op jit(solution)/shard_map/pallas_call | solution.py:372
  30.7 0.0 collective-permute-done.5.refs_3_
  30.8 3.9 %collective-permute-start.10 = (f32[400,128]{1,0:T(8,128)S(1)}, f32[400,128]{1,0:T(8,128)S(1)}, u32[]{:S(2)}, u32[]{:S(2)}) collective-permute-start(f32[400,128]{1,0:T(8,128)S(1)} %shard_map.117.refs_6_.refs_0_), channel_id=1, source_target_pairs={{0,3},{1,0},{2,1},{3,2},{4,7},{5,4},{6,5},{7,6},{8,11},{9,8},{10,9... | collective-permute-start | bytes 614408 | tf_op jit(solution)/shard_map/ppermute | solution.py:384
  34.7 0.2 collective-permute-start.8
  34.9 2.0 %collective-permute-start.9 = (f32[400,128]{1,0:T(8,128)S(1)}, f32[400,128]{1,0:T(8,128)S(1)}, u32[]{:S(2)}, u32[]{:S(2)}) collective-permute-start(f32[400,128]{1,0:T(8,128)S(1)} %shard_map.117.refs_6_.refs_0_), channel_id=1, source_target_pairs={{0,1},{1,2},{2,3},{3,0},{4,5},{5,6},{6,7},{7,4},{8,9},{9,10},{10,1... | collective-permute-start | bytes 614408 | tf_op jit(solution)/shard_map/ppermute | solution.py:384
  36.9 8.8 %shard_map.118.refs_4_.refs_5_ = f32[16,128,256]{2,1,0:T(8,128)S(1)} custom-call(s32[256]{0:T(256)S(1)} %copy-done.4, bf16[45,256,32]{2,1,0:T(8,128)(2,1)S(1)} %get-tuple-element.18.refs_1_, bf16[45,64,256]{2,1,0:T(8,128)(2,1)S(1)} %get-tuple-element.19.refs_2_, f8e5m2[45,32,256]{2,1,0:T(32,128)(4,1)S(1)} %get-tuple-element.20.refs_3_, ...), custom_call_target="tpu_custom_call" | custom-call | flops 1000 | bytes 1000 | tf_op jit(solution)/shard_map/pallas_call | solution.py:372
  45.7 0.0 collective-permute-done.8.refs_1_
  45.7 0.0 collective-permute-done.9.refs_2_
  45.7 0.1 shard_map.119.refs_6_.mine
  45.8 0.0 copy-start.2
  45.8 0.0 copy-start.5
  45.8 0.0 copy-start.6
  45.8 0.0 copy-start.7
  45.8 7.3 %collective-permute-start.11 = (f32[1552,128]{1,0:T(8,128)S(1)}, f32[1552,128]{1,0:T(8,128)S(1)}, u32[]{:S(2)}, u32[]{:S(2)}) collective-permute-start(f32[1552,128]{1,0:T(8,128)S(1)} %shard_map.119.refs_6_.mine), channel_id=1, source_target_pairs={{0,64},{64,0},{1,65},{65,1},{2,66},{66,2},{3,67},{67,3},{4,68},{68... | collective-permute-start | bytes 2383880 | tf_op jit(solution)/shard_map/ppermute | solution.py:429
  53.1 16.6 %shard_map.120.near = f32[16,128,256]{2,1,0:T(8,128)S(1)} custom-call(s32[256]{0:T(256)S(1)} %copy-done.4, bf16[45,256,32]{2,1,0:T(8,128)(2,1)S(1)} %get-tuple-element.18.refs_1_, bf16[45,64,256]{2,1,0:T(8,128)(2,1)S(1)} %get-tuple-element.19.refs_2_, f8e5m2[45,32,256]{2,1,0:T(32,128)(4,1)S(1)} %get-tuple-element.20.refs_3_, ...), custom_call_target="tpu_custom_call" | custom-call | flops 1000 | bytes 1000 | tf_op jit(solution)/shard_map/pallas_call | solution.py:372
  69.7 3.9 %shard_map.121 = (f32[16,32,256]{2,1,0:T(8,128)}, f32[16,32,256]{2,1,0:T(8,128)}) custom-call(s32[1,16]{1,0:T(1,128)S(1)} %copy-done.7, f32[1552,128]{1,0:T(8,128)S(1)} %shard_map.119.refs_6_.mine, f32[1552,128]{1,0:T(8,128)S(1)} %collective-permute-done.11.theirs, f32[3,1,64]{2,1,0:T(1,128)S(1)} %bitcast.8, f32[3,2,64]{2,1,0:T(2,128)S(1)} %bitcast.9, ...), custom_call_target="tpu_custom_call" | custom-call | flops 1000 | bytes 1000 | tf_op jit(solution)/shard_map/pallas_call | solution.py:372
  (17 shorter events, 0.1 us)
Async XLA Ops:
  6.0 17.0 %collective-permute-start.6 = (f32[496,256]{1,0:T(8,128)}, f32[496,256]{1,0:T(8,128)S(1)}, u32[]{:S(2)}, u32[]{:S(2)}) collective-permute-start(f32[496,256]{1,0:T(8,128)} %get-tuple-element.15), channel_id=1, source_target_pairs={{0,1},{1,2},{2,3},{3,4},{4,5},{5,6},{6,7},{7,8},{8,9},{9,10},{10,1... | collective-permute-start | bytes 1523720 | tf_op jit(solution)/shard_map/ppermute | solution.py:405
  9.1 14.2 %collective-permute-start.7 = (f32[496,256]{1,0:T(8,128)}, f32[496,256]{1,0:T(8,128)S(1)}, u32[]{:S(2)}, u32[]{:S(2)}) collective-permute-start(f32[496,256]{1,0:T(8,128)} %get-tuple-element.16), channel_id=1, source_target_pairs={{1,0},{2,1},{3,2},{4,3},{5,4},{6,5},{7,6},{8,7},{9,8},{10,9},{11,1... | collective-permute-start | bytes 1523720 | tf_op jit(solution)/shard_map/ppermute | solution.py:406
  11.3 8.5 %collective-permute-start = (f32[40,128]{1,0:T(8,128)}, f32[40,128]{1,0:T(8,128)S(1)}, u32[]{:S(2)}, u32[]{:S(2)}) collective-permute-start(f32[40,128]{1,0:T(8,128)} %get-tuple-element.12.refs_1_.refs_0_), channel_id=1, source_target_pairs={{0,48},{1,49},{2,50},{3,51},{4,52},{5,53},{6,54},{7,55},{8,56},{9,... | collective-permute-start | bytes 61448 | tf_op jit(solution)/shard_map/ppermute | solution.py:384
  11.8 8.0 %collective-permute-start.1 = (f32[40,128]{1,0:T(8,128)}, f32[40,128]{1,0:T(8,128)S(1)}, u32[]{:S(2)}, u32[]{:S(2)}) collective-permute-start(f32[40,128]{1,0:T(8,128)} %get-tuple-element.12.refs_1_.refs_0_), channel_id=1, source_target_pairs={{0,32},{1,33},{2,34},{3,35},{4,36},{5,37},{6,38},{7,39},{8,40},{9,... | collective-permute-start | bytes 61448 | tf_op jit(solution)/shard_map/ppermute | solution.py:384
  12.5 7.3 %collective-permute-start.2 = (f32[40,128]{1,0:T(8,128)}, f32[40,128]{1,0:T(8,128)S(1)}, u32[]{:S(2)}, u32[]{:S(2)}) collective-permute-start(f32[40,128]{1,0:T(8,128)} %get-tuple-element.12.refs_1_.refs_0_), channel_id=1, source_target_pairs={{0,16},{1,17},{2,18},{3,19},{4,20},{5,21},{6,22},{7,23},{8,24},{9,... | collective-permute-start | bytes 61448 | tf_op jit(solution)/shard_map/ppermute | solution.py:384
  14.4 1.2 %copy-start = (bf16[16,128,256]{2,1,0:T(8,128)(2,1)S(1)}, bf16[16,128,256]{2,1,0:T(8,128)(2,1)}, u32[]{:S(2)}) copy-start(bf16[16,128,256]{2,1,0:T(8,128)(2,1)} %get-tuple-element.13.refs_0_.refs_1_.refs_4_) | copy-start | bytes 3145732
  15.6 0.7 copy-start.3
  16.3 7.0 %copy-start.4 = (s32[256]{0:T(256)S(1)}, s32[256]{0:T(256)}, u32[]{:S(2)}) copy-start(s32[256]{0:T(256)} %get-tuple-element.14.refs_0_) | copy-start | bytes 3076
  19.8 10.9 %collective-permute-start.3 = (f32[112,128]{1,0:T(8,128)S(1)}, f32[112,128]{1,0:T(8,128)S(1)}, u32[]{:S(2)}, u32[]{:S(2)}) collective-permute-start(f32[112,128]{1,0:T(8,128)S(1)} %shard_map.115.refs_5_.refs_0_), channel_id=1, source_target_pairs={{0,12},{1,13},{2,14},{3,15},{4,0},{5,1},{6,2},{7,3},{8,4},{9,5},{1... | collective-permute-start | bytes 172040 | tf_op jit(solution)/shard_map/ppermute | solution.py:384
  19.9 10.8 %collective-permute-start.4 = (f32[112,128]{1,0:T(8,128)S(1)}, f32[112,128]{1,0:T(8,128)S(1)}, u32[]{:S(2)}, u32[]{:S(2)}) collective-permute-start(f32[112,128]{1,0:T(8,128)S(1)} %shard_map.115.refs_5_.refs_0_), channel_id=1, source_target_pairs={{0,8},{1,9},{2,10},{3,11},{4,12},{5,13},{6,14},{7,15},{8,0},{9,1},... | collective-permute-start | bytes 172040 | tf_op jit(solution)/shard_map/ppermute | solution.py:384
  23.0 7.7 %collective-permute-start.5 = (f32[112,128]{1,0:T(8,128)S(1)}, f32[112,128]{1,0:T(8,128)S(1)}, u32[]{:S(2)}, u32[]{:S(2)}) collective-permute-start(f32[112,128]{1,0:T(8,128)S(1)} %shard_map.115.refs_5_.refs_0_), channel_id=1, source_target_pairs={{0,4},{1,5},{2,6},{3,7},{4,8},{5,9},{6,10},{7,11},{8,12},{9,13},{1... | collective-permute-start | bytes 172040 | tf_op jit(solution)/shard_map/ppermute | solution.py:384
  30.8 14.9 %collective-permute-start.10 = (f32[400,128]{1,0:T(8,128)S(1)}, f32[400,128]{1,0:T(8,128)S(1)}, u32[]{:S(2)}, u32[]{:S(2)}) collective-permute-start(f32[400,128]{1,0:T(8,128)S(1)} %shard_map.117.refs_6_.refs_0_), channel_id=1, source_target_pairs={{0,3},{1,0},{2,1},{3,2},{4,7},{5,4},{6,5},{7,6},{8,11},{9,8},{10,9... | collective-permute-start | bytes 614408 | tf_op jit(solution)/shard_map/ppermute | solution.py:384
  34.7 11.0 %collective-permute-start.8 = (f32[400,128]{1,0:T(8,128)S(1)}, f32[400,128]{1,0:T(8,128)S(1)}, u32[]{:S(2)}, u32[]{:S(2)}) collective-permute-start(f32[400,128]{1,0:T(8,128)S(1)} %shard_map.117.refs_6_.refs_0_), channel_id=1, source_target_pairs={{0,2},{1,3},{2,0},{3,1},{4,6},{5,7},{6,4},{7,5},{8,10},{9,11},{10,... | collective-permute-start | bytes 614408 | tf_op jit(solution)/shard_map/ppermute | solution.py:384
  34.9 10.8 %collective-permute-start.9 = (f32[400,128]{1,0:T(8,128)S(1)}, f32[400,128]{1,0:T(8,128)S(1)}, u32[]{:S(2)}, u32[]{:S(2)}) collective-permute-start(f32[400,128]{1,0:T(8,128)S(1)} %shard_map.117.refs_6_.refs_0_), channel_id=1, source_target_pairs={{0,1},{1,2},{2,3},{3,0},{4,5},{5,6},{6,7},{7,4},{8,9},{9,10},{10,1... | collective-permute-start | bytes 614408 | tf_op jit(solution)/shard_map/ppermute | solution.py:384
  45.8 23.9 %copy-start.1 = (bf16[16,128,256]{2,1,0:T(8,128)(2,1)S(1)}, bf16[16,128,256]{2,1,0:T(8,128)(2,1)}, u32[]{:S(2)}) copy-start(bf16[16,128,256]{2,1,0:T(8,128)(2,1)} %get-tuple-element.21.product) | copy-start | bytes 3145732
  45.8 23.9 %copy-start.2 = (f32[1,64,64]{2,1,0:T(8,128)S(1)}, f32[1,64,64]{2,1,0:T(8,128)}, u32[]{:S(2)}) copy-start(f32[1,64,64]{2,1,0:T(8,128)} %param.15) | copy-start | bytes 49156
  45.8 23.9 %copy-start.5 = (f32[1,3,64]{2,0,1:T(1,128)S(1)}, f32[1,3,64]{2,0,1:T(1,128)}, u32[]{:S(2)}) copy-start(f32[1,3,64]{2,0,1:T(1,128)} %param.14) | copy-start | bytes 2308
  45.8 23.9 %copy-start.6 = (f32[2,3,64]{2,0,1:T(2,128)S(1)}, f32[2,3,64]{2,0,1:T(2,128)}, u32[]{:S(2)}) copy-start(f32[2,3,64]{2,0,1:T(2,128)} %param.16) | copy-start | bytes 4612
  45.8 23.9 %copy-start.7 = (s32[1,16]{1,0:T(1,128)S(1)}, s32[1,16]{1,0:T(1,128)}, u32[]{:S(2)}) copy-start(s32[1,16]{1,0:T(1,128)} %far_list_in.1) | copy-start | bytes 196
  45.8 23.8 %collective-permute-start.11 = (f32[1552,128]{1,0:T(8,128)S(1)}, f32[1552,128]{1,0:T(8,128)S(1)}, u32[]{:S(2)}, u32[]{:S(2)}) collective-permute-start(f32[1552,128]{1,0:T(8,128)S(1)} %shard_map.119.refs_6_.mine), channel_id=1, source_target_pairs={{0,64},{64,0},{1,65},{65,1},{2,66},{66,2},{3,67},{67,3},{4,68},{68... | collective-permute-start | bytes 2383880 | tf_op jit(solution)/shard_map/ppermute | solution.py:429

commit v5 on v4

--- a/solution.py
+++ b/solution.py
@@ -59,39 +59,36 @@
     return (t + LOG2E) * e, x * e
 
 
-def write_rows(rows, points, source):
+def write_parts(rows, points):
     leaves = points[0].shape[0]
     spread = rows.shape[0] // 2
-
-    def put(row, value):
+    scaled = [p * ALPHA for p in points]
+    square = scaled[0] * scaled[0] + scaled[1] * scaled[1] + scaled[2] * scaled[2]
+    coords = [split3(value) for value in scaled]
+    parts = [coords[c][part] for part in range(3) for c in range(3)]
+    parts += [*split3(square + X0), *split3(square), jnp.ones_like(square)]
+    for row, value in enumerate(parts):
         for h in range(2):
-            rows[pl.ds(h * spread + row, leaves, stride=32), :] = value[:, 128 * h : 128 * h + 128]
-
-    scaled = [p * (-2.0 * ALPHA if source else ALPHA) for p in points]
-    square = scaled[0] * scaled[0] + scaled[1] * scaled[1] + scaled[2] * scaled[2]
-    square = square * 0.25 if source else square + X0
-    picks = (0, 1, 0, 1, 2, 0, 2, 1) if source else (0, 0, 1, 1, 0, 2, 1, 2)
-    for c, value in enumerate(scaled):
-        parts = split3(value)
-        for r, pick in enumerate(picks):
-            put(8 * c + r, parts[pick])
-    one = jnp.ones_like(square)
-    norms = split3(square)
-    for r in range(3):
-        put(24 + r, one if source else norms[r])
-        put(27 + r, norms[r] if source else one)
-        if r:
-            put(29 + r, jnp.zeros_like(square))
-
-
-def leaf_rows(rows, l):
+            rows[pl.ds(h * spread + row, leaves, stride=16), :] = value[:, 128 * h : 128 * h + 128]
+
+
+def leaf_parts(rows, l):
     spread = rows.shape[0] // 2
-    return [rows[pl.ds(h * spread + 32 * l, 32), :] for h in range(2)]
-
-
-def write_source(wa, at, rows, l):
-    for h, part in enumerate(leaf_rows(rows, l)):
-        wa[at, 128 * h : 128 * h + 128, :] = jnp.transpose(part).astype(BF)
+    return jnp.concatenate([rows[pl.ds(h * spread + 16 * l, 16), :] for h in range(2)], axis=1).astype(BF)
+
+
+def choice():
+    row = lax.broadcasted_iota(jnp.int32, (64, 16), 0)
+    column = lax.broadcasted_iota(jnp.int32, (64, 16), 1)
+    source, r = row < 32, row & 31
+    e = r & 7
+    first = jnp.where((e == 1) | (e == 3) | (e == 7), 1, jnp.where((e == 4) | (e == 6), 2, 0))
+    second = jnp.where((e == 2) | (e == 3) | (e == 6), 1, jnp.where((e == 5) | (e == 7), 2, 0))
+    coordinate = jnp.where(source, first, second) * 3 + (r >> 3)
+    early, late = jnp.where(source, 15, r - 15), jnp.where(source, r - 15, 15)
+    wanted = jnp.where(r < 24, coordinate, jnp.where(r < 27, early, jnp.where(r < 30, late, -1)))
+    scale = jnp.where(source & (r < 24), -2.0, 1.0)
+    return jnp.where(column == wanted, scale, 0.0).astype(BF)
 
 
 def dot_t(a, b):
@@ -144,11 +141,10 @@
             edges[i, 16 * c : 16 * c + reach, :] = coords[c][first : first + reach]
             edges[i, 16 * c + reach : 16 * c + 16, :] = jnp.zeros((16 - reach, 256), F32)
         store(edges.at[i], (up, down)[i].at[pl.ds(moved, 48)])
-    for source in (True, False):
-        write_rows(rows, coords, source)
-        at = 0 if source else 32
-        for l in range(leaves):
-            packed[l, at : at + 32, :] = jnp.concatenate(leaf_rows(rows, l), axis=1).astype(BF)
+    write_parts(rows, coords)
+    chosen = choice()
+    for l in range(leaves):
+        packed[l, 0:64, :] = dot(chosen, leaf_parts(rows, l)).astype(BF)
     loads[1].wait()
     store(charges.at[pl.ds(32 * (leaves - reach), moved)], up.at[pl.ds(0, moved)])
     store(charges.at[pl.ds(0, moved)], down.at[pl.ds(0, moved)])
@@ -276,10 +272,11 @@
     leaves, half = packed.shape[0], before.shape[0] // 35
     total = leaves + 2 * half
     unpack(packed, wa, c2, c8, half)
+    chosen = choice()[:32]
     for ref, offset in ((before, 0), (after, half + leaves)):
-        write_rows(rows, [ref[32 * half + 16 * c : 32 * half + 16 * c + half, :] for c in range(3)], True)
+        write_parts(rows, [ref[32 * half + 16 * c : 32 * half + 16 * c + half, :] for c in range(3)])
         for l in range(half):
-            write_source(wa, offset + l, rows, l)
+            wa[offset + l] = jnp.transpose(dot(chosen, leaf_parts(rows, l))).astype(BF)
             high, low = split2(ref[32 * l : 32 * l + 32, :])
             c2[offset + l, 0:32, :], c2[offset + l, 32:64, :] = high, low
             c8[offset + l] = small_charges(high)
@@ -389,7 +386,7 @@
     skeleton = jnp.transpose(dev_skeleton, (1, 0, 2))
     total = leaves + 2 * REACH
     strip = ((REACH * 32 + 48, 256), F32)
-    rows = pltpu.VMEM((leaves * 64, 128), F32)
+    rows = pltpu.VMEM((leaves * 32, 128), F32)
     held = (points, charges.reshape(leaves * 32, 256), neighbours, counts, basis, leaf_transfer, dev_transfer[0], skeleton)
     wide = ((leaves, 128, 256), BF)
     pairs = ((256,), jnp.int32)
@@ -413,19 +410,19 @@
         lambda *refs: own_kernel(CUTS[0], *refs),
         [partial], [VMEM, anywhere], [pltpu.VMEM(*source) for source in sources] + slots, (packed, mine), 24,
     )
-    mine = gathered(mine, 16, near0, (3, 2, 1))
+    mine = gathered(mine, 16, near0, (2, 3, 1))
     near1, *held = call(
         lambda *refs: first_kernel(CUTS[0], CUTS[1], *refs),
         [partial] + [((total + 1, *shape[1:]), kind) for shape, kind in sources],
         [anywhere] + [VMEM] * 4 + [anywhere], [rows] + listing + slots,
         (order, packed, before, after, near0, mine), 24,
     )
-    mine = gathered(mine, 4, near1, (3, 2, 1))
+    mine = gathered(mine, 4, near1, (2, 3, 1))
     (near2,) = call(
         lambda *refs: next_kernel(CUTS[1], CUTS[2], *refs),
         [partial], [anywhere] + [VMEM] * 5 + [anywhere], listing + slots, (order, *held, packed, near1, mine), 24,
     )
-    mine = gathered(mine, 1, near2, (2, 1, 3))
+    mine = gathered(mine, 1, near2, (3, 1, 2))
     theirs = lax.ppermute(mine, "group", [(0, 1), (1, 0)])
     (near3,) = call(
         lambda *refs: next_kernel(CUTS[2], leaves * width // DEPTH, *refs),

time: 73.3 us -> 70.6 us (0.963)
  the two profiles are of different devices: /device:TPU:91 before, /device:TPU:73 now
where the time goes in v5:
time: 70.6 us; the launch traced here: 69.8 us
  Pallas kernels  44.7 us (63%)
  starting transfers between devices  22.2 us (31%)
  local copies, waits for them, and re-layouts  1.98 us (3%)
  between operations  0.89 us (1%)
    pallas_call x9, Pallas kernels, call(): pl.pallas_call(kernel, out_shape=tuple((jax.ShapeDtypeStruct(shape, kind)...  44.7 us
    ppermute x9, starting transfers between devices, gathered(): lax.ppermute(block, 'dev', dev_shift(div, k))  9.77 us
    ppermute x1, starting transfers between devices, local(): theirs = lax.ppermute(mine, 'group', [(0, 1), (1, 0)])  5.04 us
    ppermute x1, starting transfers between devices, local(): after = lax.ppermute(down, AXES, [(j, i) for i, j in forward])  4.27 us
    ppermute x1, starting transfers between devices, local(): before = lax.ppermute(up, AXES, forward)  3.12 us
    unnamed x16, local copies, waits for them, and re-layouts  1.98 us
  transfers between devices with their start and end apart: 12, of which 0 were waited for; matrix products, arithmetic and copies ran while one was open for 0% of the time, Pallas kernels for 51%

profile of v5, /device:TPU:73, one launch (start us, length us, event | category | flops | bytes accessed | tf_op | source)
XLA Modules:
  0.0 69.8 jit_solution(7820082395679581109)
XLA Ops:
  0.6 5.0 %shard_map.113 = (f32[496,256]{1,0:T(8,128)}, f32[496,256]{1,0:T(8,128)}, bf16[16,128,256]{2,1,0:T(8,128)(2,1)}, bf16[16,128,256]{2,1,0:T(8,128)(2,1)}, s32[256]{0:T(256)}, /*index=5*/f32[40,128]{1,0:T(8,128)}) custom-call(f32[3,16,256]{2,1,0:T(8,128)} %bitcast.11, f32[512,256]{1,0:T(8,128)} %bitcast.10, s32[16,12]{1,0:T(8,128)} %refs_2_.1, s32[16]{0:T(128)} %refs_3_.1, ...), custom_call_target="tpu_custom_call" | custom-call | flops 1000 | bytes 1000 | tf_op jit(solution)/shard_map/pallas_call | solution.py:369
  5.7 3.1 %collective-permute-start.6 = (f32[496,256]{1,0:T(8,128)}, f32[496,256]{1,0:T(8,128)S(1)}, u32[]{:S(2)}, u32[]{:S(2)}) collective-permute-start(f32[496,256]{1,0:T(8,128)} %get-tuple-element.15), channel_id=1, source_target_pairs={{0,1},{1,2},{2,3},{3,4},{4,5},{5,6},{6,7},{7,8},{8,9},{9,10},{10,1... | collective-permute-start | bytes 1523720 | tf_op jit(solution)/shard_map/ppermute | solution.py:402
  8.8 4.3 %collective-permute-start.7 = (f32[496,256]{1,0:T(8,128)}, f32[496,256]{1,0:T(8,128)S(1)}, u32[]{:S(2)}, u32[]{:S(2)}) collective-permute-start(f32[496,256]{1,0:T(8,128)} %get-tuple-element.16), channel_id=1, source_target_pairs={{1,0},{2,1},{3,2},{4,3},{5,4},{6,5},{7,6},{8,7},{9,8},{10,9},{11,1... | collective-permute-start | bytes 1523720 | tf_op jit(solution)/shard_map/ppermute | solution.py:403
  13.1 2.1 %collective-permute-start = (f32[40,128]{1,0:T(8,128)}, f32[40,128]{1,0:T(8,128)S(1)}, u32[]{:S(2)}, u32[]{:S(2)}) collective-permute-start(f32[40,128]{1,0:T(8,128)} %get-tuple-element.12.refs_1_.refs_0_), channel_id=1, source_target_pairs={{0,32},{1,33},{2,34},{3,35},{4,36},{5,37},{6,38},{7,39},{8,40},{9,... | collective-permute-start | bytes 61448 | tf_op jit(solution)/shard_map/ppermute | solution.py:381
  15.2 1.1 %collective-permute-start.1 = (f32[40,128]{1,0:T(8,128)}, f32[40,128]{1,0:T(8,128)S(1)}, u32[]{:S(2)}, u32[]{:S(2)}) collective-permute-start(f32[40,128]{1,0:T(8,128)} %get-tuple-element.12.refs_1_.refs_0_), channel_id=1, source_target_pairs={{0,48},{1,49},{2,50},{3,51},{4,52},{5,53},{6,54},{7,55},{8,56},{9,... | collective-permute-start | bytes 61448 | tf_op jit(solution)/shard_map/ppermute | solution.py:381
  16.2 0.4 collective-permute-start.2
  16.6 1.2 %copy-done = bf16[16,128,256]{2,1,0:T(8,128)(2,1)S(1)} copy-done((bf16[16,128,256]{2,1,0:T(8,128)(2,1)S(1)}, bf16[16,128,256]{2,1,0:T(8,128)(2,1)}, u32[]{:S(2)}) %copy-start) | copy-done | bytes 1048600
  17.9 0.7 %copy-done.3 = f32[40,128]{1,0:T(8,128)S(1)} copy-done((f32[40,128]{1,0:T(8,128)S(1)}, f32[40,128]{1,0:T(8,128)}, u32[]{:S(2)}) %copy-start.3) | copy-done | bytes 20504
  18.6 3.4 %shard_map.114.refs_4_ = f32[16,128,256]{2,1,0:T(8,128)S(1)} custom-call(bf16[16,128,256]{2,1,0:T(8,128)(2,1)S(1)} %copy-done, f32[40,128]{1,0:T(8,128)S(1)} %copy-done.3), custom_call_target="tpu_custom_call" | custom-call | flops 1000 | bytes 1000 | tf_op jit(solution)/shard_map/pallas_call | solution.py:369
  22.0 0.0 collective-permute-done.refs_1_
  22.0 0.0 collective-permute-done.1.refs_2_
  22.0 0.0 collective-permute-done.2.refs_3_
  22.1 2.7 %collective-permute-start.3 = (f32[112,128]{1,0:T(8,128)S(1)}, f32[112,128]{1,0:T(8,128)S(1)}, u32[]{:S(2)}, u32[]{:S(2)}) collective-permute-start(f32[112,128]{1,0:T(8,128)S(1)} %shard_map.115.refs_5_.refs_0_), channel_id=1, source_target_pairs={{0,8},{1,9},{2,10},{3,11},{4,12},{5,13},{6,14},{7,15},{8,0},{9,1},... | collective-permute-start | bytes 172040 | tf_op jit(solution)/shard_map/ppermute | solution.py:381
  24.8 0.9 %collective-permute-start.4 = (f32[112,128]{1,0:T(8,128)S(1)}, f32[112,128]{1,0:T(8,128)S(1)}, u32[]{:S(2)}, u32[]{:S(2)}) collective-permute-start(f32[112,128]{1,0:T(8,128)S(1)} %shard_map.115.refs_5_.refs_0_), channel_id=1, source_target_pairs={{0,12},{1,13},{2,14},{3,15},{4,0},{5,1},{6,2},{7,3},{8,4},{9,5},{1... | collective-permute-start | bytes 172040 | tf_op jit(solution)/shard_map/ppermute | solution.py:381
  25.7 0.6 collective-permute-start.5
  26.3 7.0 %shard_map.116 = (f32[16,128,256]{2,1,0:T(8,128)S(1)}, bf16[45,256,32]{2,1,0:T(8,128)(2,1)S(1)}, bf16[45,64,256]{2,1,0:T(8,128)(2,1)S(1)}, f8e5m2[45,32,256]{2,1,0:T(32,128)(4,1)S(1)}) custom-call(s32[256]{0:T(256)S(1)} %copy-done.4, bf16[16,128,256]{2,1,0:T(8,128)(2,1)S(1)} %copy-done, f32[496,256]{1,0:T(8,128)S(1)} %collective-permute-done.6.refs_2_, ...), custom_call_target="tpu_custom_call" | custom-call | flops 1000 | bytes 1000 | tf_op jit(solution)/shard_map/pallas_call | solution.py:369
  33.3 0.0 collective-permute-done.4.refs_2_
  33.3 0.0 collective-permute-done.5.refs_3_
  33.3 0.1 collective-permute-start.10
  33.4 1.4 %collective-permute-start.8 = (f32[400,128]{1,0:T(8,128)S(1)}, f32[400,128]{1,0:T(8,128)S(1)}, u32[]{:S(2)}, u32[]{:S(2)}) collective-permute-start(f32[400,128]{1,0:T(8,128)S(1)} %shard_map.117.refs_6_.refs_0_), channel_id=1, source_target_pairs={{0,3},{1,0},{2,1},{3,2},{4,7},{5,4},{6,5},{7,6},{8,11},{9,8},{10,9... | collective-permute-start | bytes 614408 | tf_op jit(solution)/shard_map/ppermute | solution.py:381
  34.9 0.5 collective-permute-start.9
  35.4 8.8 %shard_map.118.refs_4_.refs_5_ = f32[16,128,256]{2,1,0:T(8,128)S(1)} custom-call(s32[256]{0:T(256)S(1)} %copy-done.4, bf16[45,256,32]{2,1,0:T(8,128)(2,1)S(1)} %get-tuple-element.18.refs_1_, bf16[45,64,256]{2,1,0:T(8,128)(2,1)S(1)} %get-tuple-element.19.refs_2_, f8e5m2[45,32,256]{2,1,0:T(32,128)(4,1)S(1)} %get-tuple-element.20.refs_3_, ...), custom_call_target="tpu_custom_call" | custom-call | flops 1000 | bytes 1000 | tf_op jit(solution)/shard_map/pallas_call | solution.py:369
  44.1 0.0 collective-permute-done.10.refs_3_
  44.1 0.0 collective-permute-done.8.refs_1_
  44.2 0.1 shard_map.119.refs_6_.mine
  44.2 0.0 copy-start.2
  44.3 0.0 copy-start.5
  44.3 0.0 copy-start.6
  44.3 0.0 copy-start.7
  44.3 5.0 %collective-permute-start.11 = (f32[1552,128]{1,0:T(8,128)S(1)}, f32[1552,128]{1,0:T(8,128)S(1)}, u32[]{:S(2)}, u32[]{:S(2)}) collective-permute-start(f32[1552,128]{1,0:T(8,128)S(1)} %shard_map.119.refs_6_.mine), channel_id=1, source_target_pairs={{0,64},{64,0},{1,65},{65,1},{2,66},{66,2},{3,67},{67,3},{4,68},{68... | collective-permute-start | bytes 2383880 | tf_op jit(solution)/shard_map/ppermute | solution.py:426
  49.3 16.6 %shard_map.120.near = f32[16,128,256]{2,1,0:T(8,128)S(1)} custom-call(s32[256]{0:T(256)S(1)} %copy-done.4, bf16[45,256,32]{2,1,0:T(8,128)(2,1)S(1)} %get-tuple-element.18.refs_1_, bf16[45,64,256]{2,1,0:T(8,128)(2,1)S(1)} %get-tuple-element.19.refs_2_, f8e5m2[45,32,256]{2,1,0:T(32,128)(4,1)S(1)} %get-tuple-element.20.refs_3_, ...), custom_call_target="tpu_custom_call" | custom-call | flops 1000 | bytes 1000 | tf_op jit(solution)/shard_map/pallas_call | solution.py:369
  66.0 3.9 %shard_map.121 = (f32[16,32,256]{2,1,0:T(8,128)}, f32[16,32,256]{2,1,0:T(8,128)}) custom-call(s32[1,16]{1,0:T(1,128)S(1)} %copy-done.7, f32[1552,128]{1,0:T(8,128)S(1)} %shard_map.119.refs_6_.mine, f32[1552,128]{1,0:T(8,128)S(1)} %collective-permute-done.11.theirs, f32[3,1,64]{2,1,0:T(1,128)S(1)} %bitcast.8, f32[3,2,64]{2,1,0:T(2,128)S(1)} %bitcast.9, ...), custom_call_target="tpu_custom_call" | custom-call | flops 1000 | bytes 1000 | tf_op jit(solution)/shard_map/pallas_call | solution.py:369
  (17 shorter events, 0.1 us)
Async XLA Ops:
  5.7 20.6 %collective-permute-start.6 = (f32[496,256]{1,0:T(8,128)}, f32[496,256]{1,0:T(8,128)S(1)}, u32[]{:S(2)}, u32[]{:S(2)}) collective-permute-start(f32[496,256]{1,0:T(8,128)} %get-tuple-element.15), channel_id=1, source_target_pairs={{0,1},{1,2},{2,3},{3,4},{4,5},{5,6},{6,7},{7,8},{8,9},{9,10},{10,1... | collective-permute-start | bytes 1523720 | tf_op jit(solution)/shard_map/ppermute | solution.py:402
  8.8 17.5 %collective-permute-start.7 = (f32[496,256]{1,0:T(8,128)}, f32[496,256]{1,0:T(8,128)S(1)}, u32[]{:S(2)}, u32[]{:S(2)}) collective-permute-start(f32[496,256]{1,0:T(8,128)} %get-tuple-element.16), channel_id=1, source_target_pairs={{1,0},{2,1},{3,2},{4,3},{5,4},{6,5},{7,6},{8,7},{9,8},{10,9},{11,1... | collective-permute-start | bytes 1523720 | tf_op jit(solution)/shard_map/ppermute | solution.py:403
  13.1 9.0 %collective-permute-start = (f32[40,128]{1,0:T(8,128)}, f32[40,128]{1,0:T(8,128)S(1)}, u32[]{:S(2)}, u32[]{:S(2)}) collective-permute-start(f32[40,128]{1,0:T(8,128)} %get-tuple-element.12.refs_1_.refs_0_), channel_id=1, source_target_pairs={{0,32},{1,33},{2,34},{3,35},{4,36},{5,37},{6,38},{7,39},{8,40},{9,... | collective-permute-start | bytes 61448 | tf_op jit(solution)/shard_map/ppermute | solution.py:381
  15.2 6.9 %collective-permute-start.1 = (f32[40,128]{1,0:T(8,128)}, f32[40,128]{1,0:T(8,128)S(1)}, u32[]{:S(2)}, u32[]{:S(2)}) collective-permute-start(f32[40,128]{1,0:T(8,128)} %get-tuple-element.12.refs_1_.refs_0_), channel_id=1, source_target_pairs={{0,48},{1,49},{2,50},{3,51},{4,52},{5,53},{6,54},{7,55},{8,56},{9,... | collective-permute-start | bytes 61448 | tf_op jit(solution)/shard_map/ppermute | solution.py:381
  16.2 5.8 %collective-permute-start.2 = (f32[40,128]{1,0:T(8,128)}, f32[40,128]{1,0:T(8,128)S(1)}, u32[]{:S(2)}, u32[]{:S(2)}) collective-permute-start(f32[40,128]{1,0:T(8,128)} %get-tuple-element.12.refs_1_.refs_0_), channel_id=1, source_target_pairs={{0,16},{1,17},{2,18},{3,19},{4,20},{5,21},{6,22},{7,23},{8,24},{9,... | collective-permute-start | bytes 61448 | tf_op jit(solution)/shard_map/ppermute | solution.py:381
  16.6 1.2 %copy-start = (bf16[16,128,256]{2,1,0:T(8,128)(2,1)S(1)}, bf16[16,128,256]{2,1,0:T(8,128)(2,1)}, u32[]{:S(2)}) copy-start(bf16[16,128,256]{2,1,0:T(8,128)(2,1)} %get-tuple-element.13.refs_0_.refs_1_.refs_4_) | copy-start | bytes 3145732
  17.9 0.7 %copy-start.3 = (f32[40,128]{1,0:T(8,128)S(1)}, f32[40,128]{1,0:T(8,128)}, u32[]{:S(2)}) copy-start(f32[40,128]{1,0:T(8,128)} %get-tuple-element.12.refs_1_.refs_0_) | copy-start | bytes 61444
  18.6 7.7 %copy-start.4 = (s32[256]{0:T(256)S(1)}, s32[256]{0:T(256)}, u32[]{:S(2)}) copy-start(s32[256]{0:T(256)} %get-tuple-element.14.refs_0_) | copy-start | bytes 3076
  22.1 11.2 %collective-permute-start.3 = (f32[112,128]{1,0:T(8,128)S(1)}, f32[112,128]{1,0:T(8,128)S(1)}, u32[]{:S(2)}, u32[]{:S(2)}) collective-permute-start(f32[112,128]{1,0:T(8,128)S(1)} %shard_map.115.refs_5_.refs_0_), channel_id=1, source_target_pairs={{0,8},{1,9},{2,10},{3,11},{4,12},{5,13},{6,14},{7,15},{8,0},{9,1},... | collective-permute-start | bytes 172040 | tf_op jit(solution)/shard_map/ppermute | solution.py:381
  24.8 8.5 %collective-permute-start.4 = (f32[112,128]{1,0:T(8,128)S(1)}, f32[112,128]{1,0:T(8,128)S(1)}, u32[]{:S(2)}, u32[]{:S(2)}) collective-permute-start(f32[112,128]{1,0:T(8,128)S(1)} %shard_map.115.refs_5_.refs_0_), channel_id=1, source_target_pairs={{0,12},{1,13},{2,14},{3,15},{4,0},{5,1},{6,2},{7,3},{8,4},{9,5},{1... | collective-permute-start | bytes 172040 | tf_op jit(solution)/shard_map/ppermute | solution.py:381
  25.7 7.6 %collective-permute-start.5 = (f32[112,128]{1,0:T(8,128)S(1)}, f32[112,128]{1,0:T(8,128)S(1)}, u32[]{:S(2)}, u32[]{:S(2)}) collective-permute-start(f32[112,128]{1,0:T(8,128)S(1)} %shard_map.115.refs_5_.refs_0_), channel_id=1, source_target_pairs={{0,4},{1,5},{2,6},{3,7},{4,8},{5,9},{6,10},{7,11},{8,12},{9,13},{1... | collective-permute-start | bytes 172040 | tf_op jit(solution)/shard_map/ppermute | solution.py:381
  33.3 10.8 %collective-permute-start.10 = (f32[400,128]{1,0:T(8,128)S(1)}, f32[400,128]{1,0:T(8,128)S(1)}, u32[]{:S(2)}, u32[]{:S(2)}) collective-permute-start(f32[400,128]{1,0:T(8,128)S(1)} %shard_map.117.refs_6_.refs_0_), channel_id=1, source_target_pairs={{0,2},{1,3},{2,0},{3,1},{4,6},{5,7},{6,4},{7,5},{8,10},{9,11},{10,... | collective-permute-start | bytes 614408 | tf_op jit(solution)/shard_map/ppermute | solution.py:381
  33.4 10.7 %collective-permute-start.8 = (f32[400,128]{1,0:T(8,128)S(1)}, f32[400,128]{1,0:T(8,128)S(1)}, u32[]{:S(2)}, u32[]{:S(2)}) collective-permute-start(f32[400,128]{1,0:T(8,128)S(1)} %shard_map.117.refs_6_.refs_0_), channel_id=1, source_target_pairs={{0,3},{1,0},{2,1},{3,2},{4,7},{5,4},{6,5},{7,6},{8,11},{9,8},{10,9... | collective-permute-start | bytes 614408 | tf_op jit(solution)/shard_map/ppermute | solution.py:381
  34.9 9.3 %collective-permute-start.9 = (f32[400,128]{1,0:T(8,128)S(1)}, f32[400,128]{1,0:T(8,128)S(1)}, u32[]{:S(2)}, u32[]{:S(2)}) collective-permute-start(f32[400,128]{1,0:T(8,128)S(1)} %shard_map.117.refs_6_.refs_0_), channel_id=1, source_target_pairs={{0,1},{1,2},{2,3},{3,0},{4,5},{5,6},{6,7},{7,4},{8,9},{9,10},{10,1... | collective-permute-start | bytes 614408 | tf_op jit(solution)/shard_map/ppermute | solution.py:381
  44.2 21.7 %copy-start.1 = (bf16[16,128,256]{2,1,0:T(8,128)(2,1)S(1)}, bf16[16,128,256]{2,1,0:T(8,128)(2,1)}, u32[]{:S(2)}) copy-start(bf16[16,128,256]{2,1,0:T(8,128)(2,1)} %get-tuple-element.21.product) | copy-start | bytes 3145732
  44.2 21.7 %copy-start.2 = (f32[1,64,64]{2,1,0:T(8,128)S(1)}, f32[1,64,64]{2,1,0:T(8,128)}, u32[]{:S(2)}) copy-start(f32[1,64,64]{2,1,0:T(8,128)} %param.15) | copy-start | bytes 49156
  44.3 21.7 %copy-start.5 = (f32[1,3,64]{2,0,1:T(1,128)S(1)}, f32[1,3,64]{2,0,1:T(1,128)}, u32[]{:S(2)}) copy-start(f32[1,3,64]{2,0,1:T(1,128)} %param.14) | copy-start | bytes 2308
  44.3 21.7 %copy-start.6 = (f32[2,3,64]{2,0,1:T(2,128)S(1)}, f32[2,3,64]{2,0,1:T(2,128)}, u32[]{:S(2)}) copy-start(f32[2,3,64]{2,0,1:T(2,128)} %param.16) | copy-start | bytes 4612
  44.3 21.7 %copy-start.7 = (s32[1,16]{1,0:T(1,128)S(1)}, s32[1,16]{1,0:T(1,128)}, u32[]{:S(2)}) copy-start(s32[1,16]{1,0:T(1,128)} %far_list_in.1) | copy-start | bytes 196
  44.3 21.6 %collective-permute-start.11 = (f32[1552,128]{1,0:T(8,128)S(1)}, f32[1552,128]{1,0:T(8,128)S(1)}, u32[]{:S(2)}, u32[]{:S(2)}) collective-permute-start(f32[1552,128]{1,0:T(8,128)S(1)} %shard_map.119.refs_6_.mine), channel_id=1, source_target_pairs={{0,64},{64,0},{1,65},{65,1},{2,66},{66,2},{3,67},{67,3},{4,68},{68... | collective-permute-start | bytes 2383880 | tf_op jit(solution)/shard_map/ppermute | solution.py:426

commit v6 on v5

--- a/solution.py
+++ b/solution.py
@@ -217,10 +217,11 @@
 
     def step(i, b):
         xs[(b + 1) % DEPTH][...] = distances(jnp.minimum(i + 1, DEPTH * hi - 1))
-        for k, term in enumerate(matern_terms(xs[b][...], LIFT)):
-            high = term.astype(BF)
-            highs[b][k] = high
-            lows[b][k] = (term - high.astype(F32)).astype(F8)
+        for r in range(0, 256, 32):
+            for k, term in enumerate(matern_terms(xs[b][r : r + 32, :], LIFT)):
+                high = term.astype(BF)
+                highs[b][k, r : r + 32, :] = high
+                lows[b][k, r : r + 32, :] = (term - high.astype(F32)).astype(F8)
         gather_up(jnp.maximum(i - 1, DEPTH * lo), (b - 1) % DEPTH)
 
     def body(j, carry):

time: 70.6 us -> 71.6 us (1.014)
  the two profiles are of different devices: /device:TPU:73 before, /device:TPU:1 now
where the time goes in v6:
time: 71.6 us; the launch traced here: 71.8 us
  Pallas kernels  44.7 us (62%)
  starting transfers between devices  22.3 us (31%)
  local copies, waits for them, and re-layouts  1.98 us (3%)
  waiting for transfers between devices  1.92 us (3%)
  between operations  0.89 us (1%)
    pallas_call x9, Pallas kernels, call(): pl.pallas_call(kernel, out_shape=tuple((jax.ShapeDtypeStruct(shape, kind)...  44.7 us
    ppermute x1, starting transfers between devices, local(): after = lax.ppermute(down, AXES, [(j, i) for i, j in forward])  9.67 us
    ppermute x9, starting transfers between devices, gathered(): lax.ppermute(block, 'dev', dev_shift(div, k))  7.48 us
    ppermute x1, starting transfers between devices, local(): before = lax.ppermute(up, AXES, forward)  3.95 us
    unnamed x16, local copies, waits for them, and re-layouts  1.98 us
    ppermute x9, waiting for transfers between devices, gathered(): lax.ppermute(block, 'dev', dev_shift(div, k))  1.91 us
  transfers between devices with their start and end apart: 12, of which 1 were waited for; matrix products, arithmetic and copies ran while one was open for 0% of the time, Pallas kernels for 50%

profile of v6, /device:TPU:1, one launch (start us, length us, event | category | flops | bytes accessed | tf_op | source)
XLA Modules:
  0.0 71.8 jit_solution(7820082395679581109)
XLA Ops:
  0.6 5.0 %shard_map.113 = (f32[496,256]{1,0:T(8,128)}, f32[496,256]{1,0:T(8,128)}, bf16[16,128,256]{2,1,0:T(8,128)(2,1)}, bf16[16,128,256]{2,1,0:T(8,128)(2,1)}, s32[256]{0:T(256)}, /*index=5*/f32[40,128]{1,0:T(8,128)}) custom-call(f32[3,16,256]{2,1,0:T(8,128)} %bitcast.11, f32[512,256]{1,0:T(8,128)} %bitcast.10, s32[16,12]{1,0:T(8,128)} %refs_2_.1, s32[16]{0:T(128)} %refs_3_.1, ...), custom_call_target="tpu_custom_call" | custom-call | flops 1000 | bytes 1000 | tf_op jit(solution)/shard_map/pallas_call | solution.py:370
  5.7 3.9 %collective-permute-start.6 = (f32[496,256]{1,0:T(8,128)}, f32[496,256]{1,0:T(8,128)S(1)}, u32[]{:S(2)}, u32[]{:S(2)}) collective-permute-start(f32[496,256]{1,0:T(8,128)} %get-tuple-element.15), channel_id=1, source_target_pairs={{0,1},{1,2},{2,3},{3,4},{4,5},{5,6},{6,7},{7,8},{8,9},{9,10},{10,1... | collective-permute-start | bytes 1523720 | tf_op jit(solution)/shard_map/ppermute | solution.py:403
  9.6 9.7 %collective-permute-start.7 = (f32[496,256]{1,0:T(8,128)}, f32[496,256]{1,0:T(8,128)S(1)}, u32[]{:S(2)}, u32[]{:S(2)}) collective-permute-start(f32[496,256]{1,0:T(8,128)} %get-tuple-element.16), channel_id=1, source_target_pairs={{1,0},{2,1},{3,2},{4,3},{5,4},{6,5},{7,6},{8,7},{9,8},{10,9},{11,1... | collective-permute-start | bytes 1523720 | tf_op jit(solution)/shard_map/ppermute | solution.py:404
  19.3 0.1 collective-permute-start
  19.4 0.6 collective-permute-start.1
  19.9 1.0 %collective-permute-start.2 = (f32[40,128]{1,0:T(8,128)}, f32[40,128]{1,0:T(8,128)S(1)}, u32[]{:S(2)}, u32[]{:S(2)}) collective-permute-start(f32[40,128]{1,0:T(8,128)} %get-tuple-element.12.refs_1_.refs_0_), channel_id=1, source_target_pairs={{0,16},{1,17},{2,18},{3,19},{4,20},{5,21},{6,22},{7,23},{8,24},{9,... | collective-permute-start | bytes 61448 | tf_op jit(solution)/shard_map/ppermute | solution.py:382
  20.9 1.2 %copy-done = bf16[16,128,256]{2,1,0:T(8,128)(2,1)S(1)} copy-done((bf16[16,128,256]{2,1,0:T(8,128)(2,1)S(1)}, bf16[16,128,256]{2,1,0:T(8,128)(2,1)}, u32[]{:S(2)}) %copy-start) | copy-done | bytes 1048600
  22.1 0.7 %copy-done.3 = f32[40,128]{1,0:T(8,128)S(1)} copy-done((f32[40,128]{1,0:T(8,128)S(1)}, f32[40,128]{1,0:T(8,128)}, u32[]{:S(2)}) %copy-start.3) | copy-done | bytes 20504
  22.9 3.4 %shard_map.114.refs_4_ = f32[16,128,256]{2,1,0:T(8,128)S(1)} custom-call(bf16[16,128,256]{2,1,0:T(8,128)(2,1)S(1)} %copy-done, f32[40,128]{1,0:T(8,128)S(1)} %copy-done.3), custom_call_target="tpu_custom_call" | custom-call | flops 1000 | bytes 1000 | tf_op jit(solution)/shard_map/pallas_call | solution.py:370
  26.3 0.0 collective-permute-done.refs_1_
  26.3 0.0 collective-permute-done.1.refs_2_
  26.4 1.1 %collective-permute-start.3 = (f32[112,128]{1,0:T(8,128)S(1)}, f32[112,128]{1,0:T(8,128)S(1)}, u32[]{:S(2)}, u32[]{:S(2)}) collective-permute-start(f32[112,128]{1,0:T(8,128)S(1)} %shard_map.115.refs_5_.refs_0_), channel_id=1, source_target_pairs={{0,8},{1,9},{2,10},{3,11},{4,12},{5,13},{6,14},{7,15},{8,0},{9,1},... | collective-permute-start | bytes 172040 | tf_op jit(solution)/shard_map/ppermute | solution.py:382
  27.5 2.6 %collective-permute-start.4 = (f32[112,128]{1,0:T(8,128)S(1)}, f32[112,128]{1,0:T(8,128)S(1)}, u32[]{:S(2)}, u32[]{:S(2)}) collective-permute-start(f32[112,128]{1,0:T(8,128)S(1)} %shard_map.115.refs_5_.refs_0_), channel_id=1, source_target_pairs={{0,12},{1,13},{2,14},{3,15},{4,0},{5,1},{6,2},{7,3},{8,4},{9,5},{1... | collective-permute-start | bytes 172040 | tf_op jit(solution)/shard_map/ppermute | solution.py:382
  30.1 0.5 collective-permute-start.5
  30.6 0.0 collective-permute-done.6.refs_2_
  30.6 0.0 collective-permute-done.7.refs_3_
  30.6 7.0 %shard_map.116 = (f32[16,128,256]{2,1,0:T(8,128)S(1)}, bf16[45,256,32]{2,1,0:T(8,128)(2,1)S(1)}, bf16[45,64,256]{2,1,0:T(8,128)(2,1)S(1)}, f8e5m2[45,32,256]{2,1,0:T(32,128)(4,1)S(1)}) custom-call(s32[256]{0:T(256)S(1)} %copy-done.4, bf16[16,128,256]{2,1,0:T(8,128)(2,1)S(1)} %copy-done, f32[496,256]{1,0:T(8,128)S(1)} %collective-permute-done.6.refs_2_, ...), custom_call_target="tpu_custom_call" | custom-call | flops 1000 | bytes 1000 | tf_op jit(solution)/shard_map/pallas_call | solution.py:370
  37.6 0.0 collective-permute-done.4.refs_2_
  37.6 0.0 collective-permute-done.5.refs_3_
  37.7 0.1 collective-permute-start.10
  37.8 0.1 collective-permute-start.8
  37.9 1.5 %collective-permute-start.9 = (f32[400,128]{1,0:T(8,128)S(1)}, f32[400,128]{1,0:T(8,128)S(1)}, u32[]{:S(2)}, u32[]{:S(2)}) collective-permute-start(f32[400,128]{1,0:T(8,128)S(1)} %shard_map.117.refs_6_.refs_0_), channel_id=1, source_target_pairs={{0,1},{1,2},{2,3},{3,0},{4,5},{5,6},{6,7},{7,4},{8,9},{9,10},{10,1... | collective-permute-start | bytes 614408 | tf_op jit(solution)/shard_map/ppermute | solution.py:382
  39.3 8.8 %shard_map.118.refs_4_.refs_5_ = f32[16,128,256]{2,1,0:T(8,128)S(1)} custom-call(s32[256]{0:T(256)S(1)} %copy-done.4, bf16[45,256,32]{2,1,0:T(8,128)(2,1)S(1)} %get-tuple-element.18.refs_1_, bf16[45,64,256]{2,1,0:T(8,128)(2,1)S(1)} %get-tuple-element.19.refs_2_, f8e5m2[45,32,256]{2,1,0:T(32,128)(4,1)S(1)} %get-tuple-element.20.refs_3_, ...), custom_call_target="tpu_custom_call" | custom-call | flops 1000 | bytes 1000 | tf_op jit(solution)/shard_map/pallas_call | solution.py:370
  48.1 1.9 %collective-permute-done.9.refs_2_ = f32[400,128]{1,0:T(8,128)S(1)} collective-permute-done((f32[400,128]{1,0:T(8,128)S(1)}, f32[400,128]{1,0:T(8,128)S(1)}, u32[]{:S(2)}, u32[]{:S(2)}) %collective-permute-start.9) | collective-permute-done | bytes 204832 | tf_op jit(solution)/shard_map/ppermute | solution.py:382
  50.0 0.1 shard_map.119.refs_6_.mine
  50.1 0.0 copy-start.2
  50.1 0.0 copy-start.5
  50.1 0.0 copy-start.6
  50.1 0.0 copy-start.7
  50.1 1.2 %collective-permute-start.11 = (f32[1552,128]{1,0:T(8,128)S(1)}, f32[1552,128]{1,0:T(8,128)S(1)}, u32[]{:S(2)}, u32[]{:S(2)}) collective-permute-start(f32[1552,128]{1,0:T(8,128)S(1)} %shard_map.119.refs_6_.mine), channel_id=1, source_target_pairs={{0,64},{64,0},{1,65},{65,1},{2,66},{66,2},{3,67},{67,3},{4,68},{68... | collective-permute-start | bytes 2383880 | tf_op jit(solution)/shard_map/ppermute | solution.py:427
  51.3 16.6 %shard_map.120.near = f32[16,128,256]{2,1,0:T(8,128)S(1)} custom-call(s32[256]{0:T(256)S(1)} %copy-done.4, bf16[45,256,32]{2,1,0:T(8,128)(2,1)S(1)} %get-tuple-element.18.refs_1_, bf16[45,64,256]{2,1,0:T(8,128)(2,1)S(1)} %get-tuple-element.19.refs_2_, f8e5m2[45,32,256]{2,1,0:T(32,128)(4,1)S(1)} %get-tuple-element.20.refs_3_, ...), custom_call_target="tpu_custom_call" | custom-call | flops 1000 | bytes 1000 | tf_op jit(solution)/shard_map/pallas_call | solution.py:370
  68.0 3.9 %shard_map.121 = (f32[16,32,256]{2,1,0:T(8,128)}, f32[16,32,256]{2,1,0:T(8,128)}) custom-call(s32[1,16]{1,0:T(1,128)S(1)} %copy-done.7, f32[1552,128]{1,0:T(8,128)S(1)} %shard_map.119.refs_6_.mine, f32[1552,128]{1,0:T(8,128)S(1)} %collective-permute-done.11.theirs, f32[3,1,64]{2,1,0:T(1,128)S(1)} %bitcast.8, f32[3,2,64]{2,1,0:T(2,128)S(1)} %bitcast.9, ...), custom_call_target="tpu_custom_call" | custom-call | flops 1000 | bytes 1000 | tf_op jit(solution)/shard_map/pallas_call | solution.py:370
  (17 shorter events, 0.1 us)
Async XLA Ops:
  5.7 25.0 %collective-permute-start.6 = (f32[496,256]{1,0:T(8,128)}, f32[496,256]{1,0:T(8,128)S(1)}, u32[]{:S(2)}, u32[]{:S(2)}) collective-permute-start(f32[496,256]{1,0:T(8,128)} %get-tuple-element.15), channel_id=1, source_target_pairs={{0,1},{1,2},{2,3},{3,4},{4,5},{5,6},{6,7},{7,8},{8,9},{9,10},{10,1... | collective-permute-start | bytes 1523720 | tf_op jit(solution)/shard_map/ppermute | solution.py:403
  9.6 21.0 %collective-permute-start.7 = (f32[496,256]{1,0:T(8,128)}, f32[496,256]{1,0:T(8,128)S(1)}, u32[]{:S(2)}, u32[]{:S(2)}) collective-permute-start(f32[496,256]{1,0:T(8,128)} %get-tuple-element.16), channel_id=1, source_target_pairs={{1,0},{2,1},{3,2},{4,3},{5,4},{6,5},{7,6},{8,7},{9,8},{10,9},{11,1... | collective-permute-start | bytes 1523720 | tf_op jit(solution)/shard_map/ppermute | solution.py:404
  19.3 7.0 %collective-permute-start = (f32[40,128]{1,0:T(8,128)}, f32[40,128]{1,0:T(8,128)S(1)}, u32[]{:S(2)}, u32[]{:S(2)}) collective-permute-start(f32[40,128]{1,0:T(8,128)} %get-tuple-element.12.refs_1_.refs_0_), channel_id=1, source_target_pairs={{0,32},{1,33},{2,34},{3,35},{4,36},{5,37},{6,38},{7,39},{8,40},{9,... | collective-permute-start | bytes 61448 | tf_op jit(solution)/shard_map/ppermute | solution.py:382
  19.4 6.9 %collective-permute-start.1 = (f32[40,128]{1,0:T(8,128)}, f32[40,128]{1,0:T(8,128)S(1)}, u32[]{:S(2)}, u32[]{:S(2)}) collective-permute-start(f32[40,128]{1,0:T(8,128)} %get-tuple-element.12.refs_1_.refs_0_), channel_id=1, source_target_pairs={{0,48},{1,49},{2,50},{3,51},{4,52},{5,53},{6,54},{7,55},{8,56},{9,... | collective-permute-start | bytes 61448 | tf_op jit(solution)/shard_map/ppermute | solution.py:382
  19.9 6.4 %collective-permute-start.2 = (f32[40,128]{1,0:T(8,128)}, f32[40,128]{1,0:T(8,128)S(1)}, u32[]{:S(2)}, u32[]{:S(2)}) collective-permute-start(f32[40,128]{1,0:T(8,128)} %get-tuple-element.12.refs_1_.refs_0_), channel_id=1, source_target_pairs={{0,16},{1,17},{2,18},{3,19},{4,20},{5,21},{6,22},{7,23},{8,24},{9,... | collective-permute-start | bytes 61448 | tf_op jit(solution)/shard_map/ppermute | solution.py:382
  20.9 1.2 %copy-start = (bf16[16,128,256]{2,1,0:T(8,128)(2,1)S(1)}, bf16[16,128,256]{2,1,0:T(8,128)(2,1)}, u32[]{:S(2)}) copy-start(bf16[16,128,256]{2,1,0:T(8,128)(2,1)} %get-tuple-element.13.refs_0_.refs_1_.refs_4_) | copy-start | bytes 3145732
  22.1 0.7 %copy-start.3 = (f32[40,128]{1,0:T(8,128)S(1)}, f32[40,128]{1,0:T(8,128)}, u32[]{:S(2)}) copy-start(f32[40,128]{1,0:T(8,128)} %get-tuple-element.12.refs_1_.refs_0_) | copy-start | bytes 61444
  22.9 7.8 %copy-start.4 = (s32[256]{0:T(256)S(1)}, s32[256]{0:T(256)}, u32[]{:S(2)}) copy-start(s32[256]{0:T(256)} %get-tuple-element.14.refs_0_) | copy-start | bytes 3076
  26.4 11.3 %collective-permute-start.3 = (f32[112,128]{1,0:T(8,128)S(1)}, f32[112,128]{1,0:T(8,128)S(1)}, u32[]{:S(2)}, u32[]{:S(2)}) collective-permute-start(f32[112,128]{1,0:T(8,128)S(1)} %shard_map.115.refs_5_.refs_0_), channel_id=1, source_target_pairs={{0,8},{1,9},{2,10},{3,11},{4,12},{5,13},{6,14},{7,15},{8,0},{9,1},... | collective-permute-start | bytes 172040 | tf_op jit(solution)/shard_map/ppermute | solution.py:382
  27.5 10.2 %collective-permute-start.4 = (f32[112,128]{1,0:T(8,128)S(1)}, f32[112,128]{1,0:T(8,128)S(1)}, u32[]{:S(2)}, u32[]{:S(2)}) collective-permute-start(f32[112,128]{1,0:T(8,128)S(1)} %shard_map.115.refs_5_.refs_0_), channel_id=1, source_target_pairs={{0,12},{1,13},{2,14},{3,15},{4,0},{5,1},{6,2},{7,3},{8,4},{9,5},{1... | collective-permute-start | bytes 172040 | tf_op jit(solution)/shard_map/ppermute | solution.py:382
  30.1 7.5 %collective-permute-start.5 = (f32[112,128]{1,0:T(8,128)S(1)}, f32[112,128]{1,0:T(8,128)S(1)}, u32[]{:S(2)}, u32[]{:S(2)}) collective-permute-start(f32[112,128]{1,0:T(8,128)S(1)} %shard_map.115.refs_5_.refs_0_), channel_id=1, source_target_pairs={{0,4},{1,5},{2,6},{3,7},{4,8},{5,9},{6,10},{7,11},{8,12},{9,13},{1... | collective-permute-start | bytes 172040 | tf_op jit(solution)/shard_map/ppermute | solution.py:382
  37.7 10.4 %collective-permute-start.10 = (f32[400,128]{1,0:T(8,128)S(1)}, f32[400,128]{1,0:T(8,128)S(1)}, u32[]{:S(2)}, u32[]{:S(2)}) collective-permute-start(f32[400,128]{1,0:T(8,128)S(1)} %shard_map.117.refs_6_.refs_0_), channel_id=1, source_target_pairs={{0,2},{1,3},{2,0},{3,1},{4,6},{5,7},{6,4},{7,5},{8,10},{9,11},{10,... | collective-permute-start | bytes 614408 | tf_op jit(solution)/shard_map/ppermute | solution.py:382
  37.8 10.3 %collective-permute-start.8 = (f32[400,128]{1,0:T(8,128)S(1)}, f32[400,128]{1,0:T(8,128)S(1)}, u32[]{:S(2)}, u32[]{:S(2)}) collective-permute-start(f32[400,128]{1,0:T(8,128)S(1)} %shard_map.117.refs_6_.refs_0_), channel_id=1, source_target_pairs={{0,3},{1,0},{2,1},{3,2},{4,7},{5,4},{6,5},{7,6},{8,11},{9,8},{10,9... | collective-permute-start | bytes 614408 | tf_op jit(solution)/shard_map/ppermute | solution.py:382
  37.9 12.1 %collective-permute-start.9 = (f32[400,128]{1,0:T(8,128)S(1)}, f32[400,128]{1,0:T(8,128)S(1)}, u32[]{:S(2)}, u32[]{:S(2)}) collective-permute-start(f32[400,128]{1,0:T(8,128)S(1)} %shard_map.117.refs_6_.refs_0_), channel_id=1, source_target_pairs={{0,1},{1,2},{2,3},{3,0},{4,5},{5,6},{6,7},{7,4},{8,9},{9,10},{10,1... | collective-permute-start | bytes 614408 | tf_op jit(solution)/shard_map/ppermute | solution.py:382
  50.1 17.9 %copy-start.1 = (bf16[16,128,256]{2,1,0:T(8,128)(2,1)S(1)}, bf16[16,128,256]{2,1,0:T(8,128)(2,1)}, u32[]{:S(2)}) copy-start(bf16[16,128,256]{2,1,0:T(8,128)(2,1)} %get-tuple-element.21.product) | copy-start | bytes 3145732
  50.1 17.9 %copy-start.2 = (f32[1,64,64]{2,1,0:T(8,128)S(1)}, f32[1,64,64]{2,1,0:T(8,128)}, u32[]{:S(2)}) copy-start(f32[1,64,64]{2,1,0:T(8,128)} %param.15) | copy-start | bytes 49156
  50.1 17.9 %copy-start.5 = (f32[1,3,64]{2,0,1:T(1,128)S(1)}, f32[1,3,64]{2,0,1:T(1,128)}, u32[]{:S(2)}) copy-start(f32[1,3,64]{2,0,1:T(1,128)} %param.14) | copy-start | bytes 2308
  50.1 17.9 %copy-start.6 = (f32[2,3,64]{2,0,1:T(2,128)S(1)}, f32[2,3,64]{2,0,1:T(2,128)}, u32[]{:S(2)}) copy-start(f32[2,3,64]{2,0,1:T(2,128)} %param.16) | copy-start | bytes 4612
  50.1 17.9 %copy-start.7 = (s32[1,16]{1,0:T(1,128)S(1)}, s32[1,16]{1,0:T(1,128)}, u32[]{:S(2)}) copy-start(s32[1,16]{1,0:T(1,128)} %far_list_in.1) | copy-start | bytes 196
  50.1 17.8 %collective-permute-start.11 = (f32[1552,128]{1,0:T(8,128)S(1)}, f32[1552,128]{1,0:T(8,128)S(1)}, u32[]{:S(2)}, u32[]{:S(2)}) collective-permute-start(f32[1552,128]{1,0:T(8,128)S(1)} %shard_map.119.refs_6_.mine), channel_id=1, source_target_pairs={{0,64},{64,0},{1,65},{65,1},{2,66},{66,2},{3,67},{67,3},{4,68},{68... | collective-permute-start | bytes 2383880 | tf_op jit(solution)/shard_map/ppermute | solution.py:427
